TPU v7x, 32 devices: a whole 2x2x4 slice. The times are simulated.
32 devices in a mesh: lat: 4 (over z), lon: 8 (over y, x, core).
Axes of the slice: x: 2, y: 2, z: 4, core: 2. Of those that a mesh axis runs over, the one named last changes fastest.
Arguments:
- tokens: float32 [4, 8, 512, 1024], P('lat', 'lon')
- norm_gain: float32 [1024], replicated, may hold values from 0.5 to 6, as said below
- qkv_weight: bfloat16 [1024, 3072], replicated, may hold values from -0.1875 to 0.1875
- out_weight: bfloat16 [1024, 1024], replicated, may hold values from -0.1875 to 0.1875
- band_counts: int32 [4], P('lat'), may hold values from 256 to 512, as said below
- halo_rows: int32 [4, 2, 128], replicated, may hold values from 0 to 511, as said below
- window_mask: int32 [4, 8, 4, 5], P('lat', 'lon'), may hold values from 0 to 1, as said below
Outputs:
- updated: float32 [4, 8, 512, 1024], P('lat', 'lon')
Inputs may be any that keep to these rules, and one draw needn't show every extreme that they name: `band_counts`: counts lie between 256 and 512; some band has exactly 512 and some band exactly 256. `halo_rows`: every entry names a live slot of the neighbour band it refers to (the band itself where that neighbour does not exist). `window_mask`: entries are 0 or 1; the middle entry (offset 0) is always 1. `norm_gain`: gains are positive.
All inputs are finite; a program needn't handle non-finite values.
Results may differ from a plain program's by a relative error of at most 0.002.
The roundings to bfloat16 on the way count: a program that leaves them out, or rounds other values in their place, can miss the bound.
Values may be sent and summed in bfloat16 or wider, within the bound.
No kernel may reach another device: no remote copies, remote signals or barrier semaphores. Data moves between devices by JAX's collectives and lax.ppermute only.
A program may use at most 192 MiB of HBM per device.

v0:
```python
import functools
import math

import jax
import jax.numpy as jnp
from jax import lax
from jax.experimental import pallas as pl
from jax.experimental.pallas import tpu as pltpu
from jax.sharding import PartitionSpec as P

HEADS = 16
LANES = 128
GROUP = 256
PARTS = 2
NEG = -1e30
FLOOR = -1e25
LOG2E = math.log2(math.e)
VMEM_LIMIT = 48 * 1024 * 1024

epsilon = 1e-05


def contract_last(a, b):
    return lax.dot_general(a, b, (((1,), (1,)), ((), ())), preferred_element_type=jnp.float32)


def matmul(a, b):
    return jnp.dot(a, b, preferred_element_type=jnp.float32)


def norm_kernel(bands, tokens_ref, gain_ref, halo_rows_ref, *outs):
    normed_refs, (north_ref, south_ref) = outs[:-2], outs[-2:]
    values = tokens_ref[...]
    average = jnp.mean(values, axis=-1, keepdims=True)
    centered = values - average
    variance = jnp.mean(centered * centered, axis=-1, keepdims=True)
    normed = (centered * lax.rsqrt(variance + epsilon) * gain_ref[...]).astype(jnp.bfloat16)
    rows = values.shape[0]
    part = rows // len(normed_refs)
    for i, ref in enumerate(normed_refs):
        ref[...] = normed[i * part : (i + 1) * part]
    band = lax.axis_index("lat")
    lists = ((jnp.maximum(band - 1, 0), 1, north_ref), (jnp.minimum(band + 1, bands - 1), 0, south_ref))
    for owner, side, out in lists:
        wanted = halo_rows_ref[pl.ds(owner, 1), side, :]
        slots = lax.broadcasted_iota(jnp.int32, (rows, wanted.shape[1]), 0)
        picks = (slots == wanted).astype(jnp.float32).astype(jnp.bfloat16)
        picked = lax.dot_general(
            picks, normed, (((0,), (0,)), ((), ())), preferred_element_type=jnp.float32
        )
        out[...] = picked.astype(jnp.bfloat16)


def norm_call(tokens, gain, halo_rows):
    rows, width = tokens.shape
    bands, _, halo = halo_rows.shape
    whole = pl.BlockSpec(memory_space=pltpu.VMEM)
    part = jax.ShapeDtypeStruct((rows // PARTS, width), jnp.bfloat16)
    edge = jax.ShapeDtypeStruct((halo, width), jnp.bfloat16)
    return pl.pallas_call(
        functools.partial(norm_kernel, bands),
        out_shape=[part] * PARTS + [edge] * 2,
        in_specs=[whole] * 3,
        out_specs=[whole] * (PARTS + 2),
        compiler_params=pltpu.CompilerParams(vmem_limit_bytes=VMEM_LIMIT),
        cost_estimate=pl.CostEstimate(flops=10 * rows * width, bytes_accessed=6 * rows * width, transcendentals=0),
        name="layer_norm",
    )(tokens, gain.reshape(1, width), halo_rows)


def pair_attention(query, tiles, head_size):
    rows = query.shape[0]
    low = lax.broadcasted_iota(jnp.int32, (rows, LANES), 1) < head_size
    ones = jnp.ones((tiles[0][1].shape[0], LANES), jnp.bfloat16)
    outs = []
    for head in range(2):
        own = jnp.where(low if head == 0 else ~low, query, jnp.zeros_like(query))
        scored = []
        peak = None
        for key, value, key_bias, row_bias in tiles:
            scores = contract_last(own, key) * (LOG2E * head_size**-0.5)
            chunks = []
            for c in range(key.shape[0] // LANES):
                chunk = scores[:, c * LANES : (c + 1) * LANES]
                if key_bias[c] is not None:
                    chunk = chunk + key_bias[c]
                chunks.append(chunk)
            tile_peak = functools.reduce(jnp.maximum, chunks)
            tile_peak = tile_peak + row_bias
            peak = tile_peak if peak is None else jnp.maximum(peak, tile_peak)
            scored.append(chunks)
        top = jnp.maximum(jnp.max(peak, axis=-1, keepdims=True), FLOOR)
        weights, values = [], []
        for chunks, (key, value, key_bias, row_bias) in zip(scored, tiles):
            shift = top - row_bias
            weights += [jnp.exp2(chunk - shift).astype(jnp.bfloat16) for chunk in chunks]
            values.append(jnp.concatenate([value, jnp.ones((value.shape[0], LANES), jnp.bfloat16)], axis=1))
        result = matmul(jnp.concatenate(weights, axis=1), jnp.concatenate(values, axis=0))
        outs.append((result[:, :LANES], result[:, LANES:], top))
    (acc0, sum0, top0), (acc1, sum1, top1) = outs
    return jnp.where(low, acc0, acc1), jnp.where(low, sum0, sum1), jnp.where(low, top0, top1)


def stage_kernel(spec, *refs):
    first, last, sectors, halos, head_size = spec
    refs = list(refs)

    def take(count):
        taken = refs[:count]
        del refs[:count]
        return taken

    counts_ref, mask_ref = take(2)
    sector_refs = [take(PARTS) for _ in sectors]
    halo_refs = take(2) if halos else []
    wq_ref = take(1)[0] if first else None
    wk_ref, wv_ref = take(2)
    query_in = take(1)[0] if not first else None
    state_in = take(3) if not first else None
    if last:
        tokens_ref, wo_ref, out_ref, res_ref = take(4)
    else:
        if first:
            query_out = take(1)[0]
        state_out = take(3)

    blocks, reach = mask_ref.shape[0], mask_ref.shape[1] // 2
    lon, lat = lax.axis_index("lon"), lax.axis_index("lat")
    bands = lax.axis_size("lat")
    core, odd = lon % 2, (lon // 2) % 2
    offsets = {"own": 0, "partner": 1 - 2 * core, "same": 2 - 4 * odd, "across": 4 * odd - 2, "near": 2 * core - 1}
    count = counts_ref[0]

    wk, wv = wk_ref[...], wv_ref[...]
    if first:
        query = jnp.concatenate([matmul(ref[...], wq_ref[...]).astype(jnp.bfloat16) for ref in sector_refs[0]], axis=0)
        query_out[...] = query
    else:
        query = query_in[...]
    rows = query.shape[0]
    width = query.shape[1]
    block_rows = rows // blocks
    part_rows = rows // PARTS

    tiles = []
    for name, parts in zip(sectors, sector_refs):
        column = reach + offsets[name]
        row_bias = jnp.concatenate(
            [
                jnp.full((block_rows, LANES), jnp.where(mask_ref[b, column] > 0, 0.0, NEG), jnp.float32)
                for b in range(blocks)
            ],
            axis=0,
        )
        for i, ref in enumerate(parts):
            key = matmul(ref[...], wk).astype(jnp.bfloat16)
            value = matmul(ref[...], wv).astype(jnp.bfloat16)
            bias = []
            for c in range(part_rows // LANES):
                start = i * part_rows + c * LANES
                if start + LANES <= rows // 2:
                    bias.append(None)
                else:
                    slot = start + lax.broadcasted_iota(jnp.int32, (1, LANES), 1)
                    bias.append(jnp.where(slot < count, 0.0, NEG))
            tiles.append((key, value, bias, row_bias))
    for ref, seen in zip(halo_refs, (lat > 0, lat < bands - 1)):
        key = matmul(ref[...], wk).astype(jnp.bfloat16)
        value = matmul(ref[...], wv).astype(jnp.bfloat16)
        row_bias = jnp.full((rows, LANES), jnp.where(seen, 0.0, NEG), jnp.float32)
        tiles.append((key, value, [None] * (key.shape[0] // LANES), row_bias))

    attended = []
    for pair in range(width // LANES):
        lanes = slice(pair * LANES, (pair + 1) * LANES)
        pair_tiles = [(key[:, lanes], value[:, lanes], kb, rb) for key, value, kb, rb in tiles]
        acc, total, top = pair_attention(query[:, lanes], pair_tiles, head_size)
        if not first:
            old_acc, old_total, old_top = [ref[:, lanes] for ref in state_in]
            new_top = jnp.maximum(old_top, top)
            old_scale, scale = jnp.exp2(old_top - new_top), jnp.exp2(top - new_top)
            acc = old_acc * old_scale + acc * scale
            total = old_total * old_scale + total * scale
            top = new_top
        if last:
            attended.append((acc / total).astype(jnp.bfloat16))
        else:
            for ref, value in zip(state_out, (acc, total, top)):
                ref[:, lanes] = value
    if last:
        step = pl.program_id(0)

        @pl.when(step == 0)
        def _():
            res_ref[...] = jnp.zeros_like(res_ref)

        columns = pl.ds(pl.multiple_of(step * width, width), width)
        res_ref[:, columns] += tokens_ref[...]
        res_ref[...] += matmul(jnp.concatenate(attended, axis=1), wo_ref[...])

        @pl.when(step == pl.num_programs(0) - 1)
        def _():
            slot = lax.broadcasted_iota(jnp.int32, res_ref.shape, 0)
            out_ref[...] = jnp.where(slot < count, res_ref[...], 0.0)


def stage_call(counts, mask, sectors, sector_parts, halos, qkv_weight, query=None, state=None, tokens=None, out_weight=None):
    first, last = query is None, tokens is not None
    model, width = qkv_weight.shape[0], qkv_weight.shape[1] // 3
    head_size = width // HEADS
    rows = sum(p.shape[0] for p in sector_parts[0])
    steps = width // GROUP
    smem = pl.BlockSpec(memory_space=pltpu.SMEM)

    def fixed(shape):
        return pl.BlockSpec(shape, lambda g: (0, 0), pipeline_mode=pl.Buffered(1))

    def weight(third):
        return pl.BlockSpec((model, GROUP), lambda g: (0, third * steps + g))

    columns = pl.BlockSpec((rows, GROUP), lambda g: (0, g))
    args, specs = [counts, mask], [smem, smem]
    for parts in sector_parts:
        args += parts
        specs += [fixed(p.shape) for p in parts]
    for halo in halos:
        args.append(halo)
        specs.append(fixed(halo.shape))
    for third in range(0 if first else 1, 3):
        args.append(qkv_weight)
        specs.append(weight(third))
    if not first:
        args += [query, *state]
        specs += [columns] * 4
    scratch = []
    state_shape = jax.ShapeDtypeStruct((rows, width), jnp.float32)
    if last:
        args += [tokens, out_weight]
        specs += [columns, pl.BlockSpec((GROUP, out_weight.shape[1]), lambda g: (g, 0))]
        out_shape = [state_shape]
        out_specs = [pl.BlockSpec((rows, width), lambda g: (0, 0), pipeline_mode=pl.Buffered(1))]
        scratch = [pltpu.VMEM((rows, width), jnp.float32)]
    else:
        out_shape = [state_shape] * 3
        out_specs = [columns] * 3
        if first:
            out_shape = [jax.ShapeDtypeStruct((rows, width), jnp.bfloat16)] + out_shape
            out_specs = [columns] + out_specs
    keys = sum(p.shape[0] for parts in sector_parts for p in parts) + sum(h.shape[0] for h in halos)
    flops = 2 * keys * model * 2 * width + 16 * rows * keys * width
    flops += 2 * rows * model * width * (int(first) + int(last))
    moved = sum(a.size * a.dtype.itemsize for a in args[2:] if a is not qkv_weight) + 3 * model * width * 2
    outs = pl.pallas_call(
        functools.partial(stage_kernel, (first, last, sectors, bool(halos), head_size)),
        out_shape=out_shape,
        grid=(steps,),
        in_specs=specs,
        out_specs=out_specs,
        scratch_shapes=scratch,
        compiler_params=pltpu.CompilerParams(vmem_limit_bytes=VMEM_LIMIT),
        cost_estimate=pl.CostEstimate(flops=flops, bytes_accessed=moved, transcendentals=rows * keys * HEADS),
        name="attend_" + "_".join(sectors),
    )(*args)
    if last:
        return outs[0]
    if first:
        return outs[0], outs[1:]
    return outs


def permuted(values, axis, target):
    size = lax.axis_size(axis)
    pairs = [(i, target(i)) for i in range(size) if 0 <= target(i) < size]
    return [lax.ppermute(v, axis, pairs) for v in values]


def on_device(tokens, norm_gain, qkv_weight, out_weight, band_counts, halo_rows, window_mask):
    mask = window_mask[0, 0]
    ring = lax.axis_size("lon")
    assert mask.shape[1] == 5 and ring % 4 == 0 and ring >= 8
    local = tokens[0, 0]
    outs = norm_call(local, norm_gain, halo_rows)
    own, north_rows, south_rows = outs[:PARTS], outs[PARTS], outs[PARTS + 1]

    partner = permuted(own, "lon", lambda i: i ^ 1)
    same = permuted(own, "lon", lambda i: i ^ 2)
    from_south = permuted([north_rows], "lat", lambda b: b - 1)[0]
    from_north = permuted([south_rows], "lat", lambda b: b + 1)[0]

    across = permuted(same, "lon", lambda i: (i + (4 if (i // 2) % 2 == 0 else -4)) % ring)
    lon = lax.axis_index("lon")
    gives_same = lon % 2 == (lon // 2) % 2
    near = permuted([jnp.where(gives_same, s, a) for s, a in zip(same, across)], "lon", lambda i: i ^ 1)

    query, state = stage_call(band_counts, mask, ["own"], [own], [], qkv_weight)
    state = stage_call(band_counts, mask, ["partner"], [partner], [from_north, from_south], qkv_weight, query, state)
    state = stage_call(band_counts, mask, ["same"], [same], [], qkv_weight, query, state)
    result = stage_call(
        band_counts, mask, ["across", "near"], [across, near], [], qkv_weight, query, state, local, out_weight
    )
    return result[None, None]


def solution(mesh):
    in_specs = (
        P("lat", "lon", None, None),
        P(),
        P(),
        P(),
        P("lat"),
        P(),
        P("lat", "lon", None, None),
    )
    out_specs = P("lat", "lon", None, None)
    return jax.shard_map(
        on_device, mesh=mesh, in_specs=in_specs, out_specs=out_specs, check_vma=False
    )
```

profile of v0, /device:TPU:0, one launch (start us, length us, event | category | flops | bytes accessed | tf_op | source)
XLA Modules:
  0.0 98.1 jit_solution(8739596936284670734)
XLA Ops:
  0.0 0.0 copy-start.3
  0.0 0.0 copy-start
  0.0 1.6 %copy-done = f32[1,1,512,1024]{3,2,1,0:T(8,128)S(1)} copy-done((f32[1,1,512,1024]{3,2,1,0:T(8,128)S(1)}, f32[1,1,512,1024]{3,2,1,0:T(8,128)}, u32[]{:S(2)}) %copy-start) | copy-done | bytes 2097176
  1.6 0.0 copy-start.1
  1.6 0.7 copy-done.1
  2.3 0.0 copy-start.2
  2.3 0.7 copy-done.2
  3.0 1.6 %layer_norm.1 = (bf16[256,1024]{1,0:T(8,128)(2,1)S(1)}, bf16[256,1024]{1,0:T(8,128)(2,1)S(1)}, bf16[128,1024]{1,0:T(8,128)(2,1)}, bf16[128,1024]{1,0:T(8,128)(2,1)S(1)}) custom-call(f32[512,1024]{1,0:T(8,128)S(1)} %bitcast.5, f32[1,1024]{1,0:T(1,128)S(1)} %bitcast.6, s32[4,2,128]{2,1,0:T(2,128)S(1)} %copy-done.2), custom_call_target="tpu_custom_call" | custom-call | flops 5242880 | bytes 3145728 | tf_op jit(solution)/shard_map/layer_norm/pallas_call | solution.py:60
  4.6 4.9 %collective-permute-start.8 = (bf16[128,1024]{1,0:T(8,128)(2,1)S(1)}, bf16[128,1024]{1,0:T(8,128)(2,1)S(1)}, u32[]{:S(2)}, u32[]{:S(2)}) collective-permute-start(bf16[128,1024]{1,0:T(8,128)(2,1)S(1)} %get-tuple-element.22), channel_id=1, source_target_pairs={{0,8},{8,16},{16,24},{1,9},{9,17},{17,25},{2,10},{10,18},{18,26},{... | collective-permute-start | bytes 786440 | tf_op jit(solution)/shard_map/ppermute | solution.py:274
  9.5 0.1 collective-permute-start.6
  9.6 1.6 %collective-permute-start = (bf16[256,1024]{1,0:T(8,128)(2,1)S(1)}, bf16[256,1024]{1,0:T(8,128)(2,1)S(1)}, u32[]{:S(2)}, u32[]{:S(2)}) collective-permute-start(bf16[256,1024]{1,0:T(8,128)(2,1)S(1)} %get-tuple-element.19.refs_2_), channel_id=1, source_target_pairs={{0,2},{1,3},{2,0},{3,1},{4,6},{5,7},{6,4},{7,5},{8,10},{9,11},{10,... | collective-permute-start | bytes 1572872 | tf_op jit(solution)/shard_map/ppermute | solution.py:274
  11.1 0.2 collective-permute-start.7
  11.3 0.5 collective-permute-start.2
  12.5 2.5 %collective-permute-done.8.refs_4_ = bf16[128,1024]{1,0:T(8,128)(2,1)S(1)} collective-permute-done((bf16[128,1024]{1,0:T(8,128)(2,1)S(1)}, bf16[128,1024]{1,0:T(8,128)(2,1)S(1)}, u32[]{:S(2)}, u32[]{:S(2)}) %collective-permute-start.8) | collective-permute-done | bytes 262176 | tf_op jit(solution)/shard_map/ppermute | solution.py:274
  15.0 1.3 %collective-permute-start.9 = (bf16[128,1024]{1,0:T(8,128)(2,1)}, bf16[128,1024]{1,0:T(8,128)(2,1)}, u32[]{:S(2)}, u32[]{:S(2)}) collective-permute-start(bf16[128,1024]{1,0:T(8,128)(2,1)} %get-tuple-element.23), channel_id=1, source_target_pairs={{8,0},{16,8},{24,16},{9,1},{17,9},{25,17},{10,2},{18,10},{26,18},{... | collective-permute-start | bytes 786440 | tf_op jit(solution)/shard_map/ppermute | solution.py:274
  16.3 0.0 copy-done.3
  16.3 12.9 %attend_own.1 = (bf16[512,1024]{1,0:T(8,128)(2,1)S(1)}, f32[512,1024]{1,0:T(8,128)S(1)}, f32[512,1024]{1,0:T(8,128)}, f32[512,1024]{1,0:T(8,128)}) custom-call(s32[1]{0:T(128)S(6)} %copy.8.refs_0_, s32[4,5]{1,0:T(4,128)S(1)} %bitcast.7, bf16[256,1024]{1,0:T(8,128)(2,1)S(1)} %get-tuple-element.19.refs_2_, bf16[256,1024]{1,0:T(8,128)(2,1)S(1)} %get-tuple-element.20.refs_3_, ...), custom_call_target="tpu_custom_call" | custom-call | flops 7516192768 | bytes 7340032 | tf_op jit(solution)/shard_map/attend_own/pallas_call | solution.py:253
  29.3 0.0 copy-start.5
  29.3 1.1 %copy-done.5 = bf16[512,1024]{1,0:T(8,128)(2,1)} copy-done((bf16[512,1024]{1,0:T(8,128)(2,1)}, bf16[512,1024]{1,0:T(8,128)(2,1)S(1)}, u32[]{:S(2)}) %copy-start.5) | copy-done | bytes 1048600
  30.3 0.0 copy-start.8
  30.3 1.4 %copy-done.8 = f32[512,1024]{1,0:T(8,128)} copy-done((f32[512,1024]{1,0:T(8,128)}, f32[512,1024]{1,0:T(8,128)S(1)}, u32[]{:S(2)}) %copy-start.8) | copy-done | bytes 2097176
  31.7 3.5 %collective-permute-done.2.refs_3_ = bf16[256,1024]{1,0:T(8,128)(2,1)S(1)} collective-permute-done((bf16[256,1024]{1,0:T(8,128)(2,1)S(1)}, bf16[256,1024]{1,0:T(8,128)(2,1)S(1)}, u32[]{:S(2)}, u32[]{:S(2)}) %collective-permute-start.2) | collective-permute-done | bytes 524320 | tf_op jit(solution)/shard_map/ppermute | solution.py:274
  35.2 1.5 %collective-permute-start.3 = (bf16[256,1024]{1,0:T(8,128)(2,1)S(1)}, bf16[256,1024]{1,0:T(8,128)(2,1)S(1)}, u32[]{:S(2)}, u32[]{:S(2)}) collective-permute-start(bf16[256,1024]{1,0:T(8,128)(2,1)S(1)} %collective-permute-done.2.refs_3_), channel_id=1, source_target_pairs={{0,4},{1,5},{2,6},{3,7},{4,0},{5,1},{6,2},{7,3},{8,12},{9,13},{10,... | collective-permute-start | bytes 1572872 | tf_op jit(solution)/shard_map/ppermute | solution.py:274
  36.7 0.0 collective-permute-done.refs_2_
  36.7 0.5 collective-permute-start.1
  37.2 0.0 collective-permute-done.9.refs_5_
  37.2 0.0 collective-permute-done.6.refs_2_
  37.2 0.0 collective-permute-done.7.refs_3_
  37.2 0.0 copy-start.6
  37.2 1.2 %copy-done.6 = bf16[512,1024]{1,0:T(8,128)(2,1)S(1)} copy-done((bf16[512,1024]{1,0:T(8,128)(2,1)S(1)}, bf16[512,1024]{1,0:T(8,128)(2,1)}, u32[]{:S(2)}) %copy-start.6) | copy-done | bytes 1048600
  38.4 18.1 %attend_partner.1 = (f32[512,1024]{1,0:T(8,128)S(1)}, f32[512,1024]{1,0:T(8,128)}, f32[512,1024]{1,0:T(8,128)}) custom-call(s32[1]{0:T(128)S(6)} %copy.8.refs_0_, s32[4,5]{1,0:T(4,128)S(1)} %bitcast.8, bf16[256,1024]{1,0:T(8,128)(2,1)S(1)} %collective-permute-done.6.refs_2_, bf16[256,1024]{1,0:T(8,128)(2,1)S(1)} %collective-permute-done.7.refs_3_, ...), custom_call_target="tpu_custom_call" | custom-call | flops 9663676416 | bytes 15204352 | tf_op jit(solution)/shard_map/attend_partner/pallas_call | solution.py:253
  56.5 0.0 copy-start.4
  56.5 1.3 %copy-done.4 = f32[512,1024]{1,0:T(8,128)} copy-done((f32[512,1024]{1,0:T(8,128)}, f32[512,1024]{1,0:T(8,128)S(1)}, u32[]{:S(2)}) %copy-start.4) | copy-done | bytes 2097176
  57.8 0.0 copy-start.7
  57.8 0.0 collective-permute-done.3.refs_3_
  57.8 0.1 broadcast_select_fusion
  57.9 0.1 collective-permute-start.5
  58.0 1.9 %collective-permute-done.1.refs_2_ = bf16[256,1024]{1,0:T(8,128)(2,1)S(1)} collective-permute-done((bf16[256,1024]{1,0:T(8,128)(2,1)S(1)}, bf16[256,1024]{1,0:T(8,128)(2,1)S(1)}, u32[]{:S(2)}, u32[]{:S(2)}) %collective-permute-start.1) | collective-permute-done | bytes 524320 | tf_op jit(solution)/shard_map/ppermute | solution.py:274
  59.9 0.1 broadcast_select_fusion.1
  60.0 0.1 collective-permute-start.4
  60.0 0.0 copy-done.7
  60.1 13.0 %attend_same.1 = (f32[512,1024]{1,0:T(8,128)S(1)}, f32[512,1024]{1,0:T(8,128)}, f32[512,1024]{1,0:T(8,128)}) custom-call(s32[1]{0:T(128)S(6)} %copy.8.refs_0_, s32[4,5]{1,0:T(4,128)S(1)} %bitcast.9, bf16[256,1024]{1,0:T(8,128)(2,1)S(1)} %collective-permute-done.refs_2_, bf16[256,1024]{1,0:T(8,128)(2,1)S(1)} %collective-permute-done.2.refs_3_, ...), custom_call_target="tpu_custom_call" | custom-call | flops 6442450944 | bytes 14680064 | tf_op jit(solution)/shard_map/attend_same/pallas_call | solution.py:253
  73.0 0.0 collective-permute-done.5.refs_5_
  73.0 0.0 collective-permute-done.4.refs_4_
  73.0 25.1 %attend_across_near.1 = f32[512,1024]{1,0:T(8,128)} custom-call(s32[1]{0:T(128)S(6)} %copy.8.refs_0_, s32[4,5]{1,0:T(4,128)S(1)} %bitcast.10, bf16[256,1024]{1,0:T(8,128)(2,1)S(1)} %collective-permute-done.1.refs_2_, bf16[256,1024]{1,0:T(8,128)(2,1)S(1)} %collective-permute-done.3.refs_3_, bf16[256,1024]{1,0:T(8,128)(2,1)S(1)} %collective-permute-done.4.refs_4_, ...), custom_call_target="tpu_custom_call" | custom-call | flops 13958643712 | bytes 19922944 | tf_op jit(solution)/shard_map/attend_across_near/pallas_call | solution.py:253
Async XLA Ops:
  0.0 16.3 %copy-start.3 = (s32[1,1,4,5]{3,2,1,0:T(4,128)S(1)}, s32[1,1,4,5]{3,2,1,0:T(4,128)}, u32[]{:S(2)}) copy-start(s32[1,1,4,5]{3,2,1,0:T(4,128)} %param.13) | copy-start | bytes 244
  0.0 1.6 %copy-start = (f32[1,1,512,1024]{3,2,1,0:T(8,128)S(1)}, f32[1,1,512,1024]{3,2,1,0:T(8,128)}, u32[]{:S(2)}) copy-start(f32[1,1,512,1024]{3,2,1,0:T(8,128)} %param.7) | copy-start | bytes 6291460
  1.6 0.7 copy-start.1
  2.3 0.7 copy-start.2
  4.6 10.5 %collective-permute-start.8 = (bf16[128,1024]{1,0:T(8,128)(2,1)S(1)}, bf16[128,1024]{1,0:T(8,128)(2,1)S(1)}, u32[]{:S(2)}, u32[]{:S(2)}) collective-permute-start(bf16[128,1024]{1,0:T(8,128)(2,1)S(1)} %get-tuple-element.22), channel_id=1, source_target_pairs={{0,8},{8,16},{16,24},{1,9},{9,17},{17,25},{2,10},{10,18},{18,26},{... | collective-permute-start | bytes 786440 | tf_op jit(solution)/shard_map/ppermute | solution.py:274
  9.5 27.7 %collective-permute-start.6 = (bf16[256,1024]{1,0:T(8,128)(2,1)S(1)}, bf16[256,1024]{1,0:T(8,128)(2,1)S(1)}, u32[]{:S(2)}, u32[]{:S(2)}) collective-permute-start(bf16[256,1024]{1,0:T(8,128)(2,1)S(1)} %get-tuple-element.19.refs_2_), channel_id=1, source_target_pairs={{0,1},{1,0},{2,3},{3,2},{4,5},{5,4},{6,7},{7,6},{8,9},{9,8},{10,11... | collective-permute-start | bytes 1572872 | tf_op jit(solution)/shard_map/ppermute | solution.py:274
  9.6 27.1 %collective-permute-start = (bf16[256,1024]{1,0:T(8,128)(2,1)S(1)}, bf16[256,1024]{1,0:T(8,128)(2,1)S(1)}, u32[]{:S(2)}, u32[]{:S(2)}) collective-permute-start(bf16[256,1024]{1,0:T(8,128)(2,1)S(1)} %get-tuple-element.19.refs_2_), channel_id=1, source_target_pairs={{0,2},{1,3},{2,0},{3,1},{4,6},{5,7},{6,4},{7,5},{8,10},{9,11},{10,... | collective-permute-start | bytes 1572872 | tf_op jit(solution)/shard_map/ppermute | solution.py:274
  11.1 26.1 %collective-permute-start.7 = (bf16[256,1024]{1,0:T(8,128)(2,1)S(1)}, bf16[256,1024]{1,0:T(8,128)(2,1)S(1)}, u32[]{:S(2)}, u32[]{:S(2)}) collective-permute-start(bf16[256,1024]{1,0:T(8,128)(2,1)S(1)} %get-tuple-element.20.refs_3_), channel_id=1, source_target_pairs={{0,1},{1,0},{2,3},{3,2},{4,5},{5,4},{6,7},{7,6},{8,9},{9,8},{10,11... | collective-permute-start | bytes 1572872 | tf_op jit(solution)/shard_map/ppermute | solution.py:274
  11.3 23.9 %collective-permute-start.2 = (bf16[256,1024]{1,0:T(8,128)(2,1)S(1)}, bf16[256,1024]{1,0:T(8,128)(2,1)S(1)}, u32[]{:S(2)}, u32[]{:S(2)}) collective-permute-start(bf16[256,1024]{1,0:T(8,128)(2,1)S(1)} %get-tuple-element.20.refs_3_), channel_id=1, source_target_pairs={{0,2},{1,3},{2,0},{3,1},{4,6},{5,7},{6,4},{7,5},{8,10},{9,11},{10,... | collective-permute-start | bytes 1572872 | tf_op jit(solution)/shard_map/ppermute | solution.py:274
  15.0 22.2 %collective-permute-start.9 = (bf16[128,1024]{1,0:T(8,128)(2,1)}, bf16[128,1024]{1,0:T(8,128)(2,1)}, u32[]{:S(2)}, u32[]{:S(2)}) collective-permute-start(bf16[128,1024]{1,0:T(8,128)(2,1)} %get-tuple-element.23), channel_id=1, source_target_pairs={{8,0},{16,8},{24,16},{9,1},{17,9},{25,17},{10,2},{18,10},{26,18},{... | collective-permute-start | bytes 786440 | tf_op jit(solution)/shard_map/ppermute | solution.py:274
  29.3 1.1 %copy-start.5 = (bf16[512,1024]{1,0:T(8,128)(2,1)}, bf16[512,1024]{1,0:T(8,128)(2,1)S(1)}, u32[]{:S(2)}) copy-start(bf16[512,1024]{1,0:T(8,128)(2,1)S(1)} %get-tuple-element.21.refs_8_.refs_6_) | copy-start | bytes 3145732
  30.3 1.4 %copy-start.8 = (f32[512,1024]{1,0:T(8,128)}, f32[512,1024]{1,0:T(8,128)S(1)}, u32[]{:S(2)}) copy-start(f32[512,1024]{1,0:T(8,128)S(1)} %get-tuple-element.24.refs_9_) | copy-start | bytes 6291460
  35.2 22.7 %collective-permute-start.3 = (bf16[256,1024]{1,0:T(8,128)(2,1)S(1)}, bf16[256,1024]{1,0:T(8,128)(2,1)S(1)}, u32[]{:S(2)}, u32[]{:S(2)}) collective-permute-start(bf16[256,1024]{1,0:T(8,128)(2,1)S(1)} %collective-permute-done.2.refs_3_), channel_id=1, source_target_pairs={{0,4},{1,5},{2,6},{3,7},{4,0},{5,1},{6,2},{7,3},{8,12},{9,13},{10,... | collective-permute-start | bytes 1572872 | tf_op jit(solution)/shard_map/ppermute | solution.py:274
  36.7 23.2 %collective-permute-start.1 = (bf16[256,1024]{1,0:T(8,128)(2,1)S(1)}, bf16[256,1024]{1,0:T(8,128)(2,1)S(1)}, u32[]{:S(2)}, u32[]{:S(2)}) collective-permute-start(bf16[256,1024]{1,0:T(8,128)(2,1)S(1)} %collective-permute-done.refs_2_), channel_id=1, source_target_pairs={{0,4},{1,5},{2,6},{3,7},{4,0},{5,1},{6,2},{7,3},{8,12},{9,13},{10,... | collective-permute-start | bytes 1572872 | tf_op jit(solution)/shard_map/ppermute | solution.py:274
  37.2 1.2 %copy-start.6 = (bf16[512,1024]{1,0:T(8,128)(2,1)S(1)}, bf16[512,1024]{1,0:T(8,128)(2,1)}, u32[]{:S(2)}) copy-start(bf16[512,1024]{1,0:T(8,128)(2,1)} %copy-done.5) | copy-start | bytes 3145732
  56.5 1.3 %copy-start.4 = (f32[512,1024]{1,0:T(8,128)}, f32[512,1024]{1,0:T(8,128)S(1)}, u32[]{:S(2)}) copy-start(f32[512,1024]{1,0:T(8,128)S(1)} %get-tuple-element.27.refs_7_) | copy-start | bytes 6291460
  57.8 2.2 %copy-start.7 = (bf16[512,1024]{1,0:T(8,128)(2,1)S(1)}, bf16[512,1024]{1,0:T(8,128)(2,1)}, u32[]{:S(2)}) copy-start(bf16[512,1024]{1,0:T(8,128)(2,1)} %copy-done.5) | copy-start | bytes 3145732
  57.9 15.1 %collective-permute-start.5 = (bf16[256,1024]{1,0:T(8,128)(2,1)S(1)}, bf16[256,1024]{1,0:T(8,128)(2,1)S(1)}, u32[]{:S(2)}, u32[]{:S(2)}) collective-permute-start(bf16[256,1024]{1,0:T(8,128)(2,1)S(1)} %broadcast_select_fusion), channel_id=1, source_target_pairs={{0,1},{1,0},{2,3},{3,2},{4,5},{5,4},{6,7},{7,6},{8,9},{9,8},{10,11... | collective-permute-start | bytes 1572872 | tf_op jit(solution)/shard_map/ppermute | solution.py:274
  60.0 13.1 %collective-permute-start.4 = (bf16[256,1024]{1,0:T(8,128)(2,1)S(1)}, bf16[256,1024]{1,0:T(8,128)(2,1)S(1)}, u32[]{:S(2)}, u32[]{:S(2)}) collective-permute-start(bf16[256,1024]{1,0:T(8,128)(2,1)S(1)} %broadcast_select_fusion.1), channel_id=1, source_target_pairs={{0,1},{1,0},{2,3},{3,2},{4,5},{5,4},{6,7},{7,6},{8,9},{9,8},{10,11... | collective-permute-start | bytes 1572872 | tf_op jit(solution)/shard_map/ppermute | solution.py:274
where the time goes:
time: 98.4 us; the launch traced here: 98.1 us
  Pallas kernels  70.6 us (72%)
  starting transfers between devices  10.7 us (11%)
  waiting for transfers between devices  7.96 us (8%)
  local copies, waits for them, and re-layouts  7.94 us (8%)
    pallas_call x4, Pallas kernels, stage_call(): pl.pallas_call(functools.partial(stage_kernel, (first, last, sectors, boo...  69 us
    ppermute x10, starting transfers between devices, permuted(): return [lax.ppermute(v, axis, pairs) for v in values]  10.7 us
    ppermute x10, waiting for transfers between devices, permuted(): return [lax.ppermute(v, axis, pairs) for v in values]  7.96 us
    unnamed x18, local copies, waits for them, and re-layouts  7.94 us
  transfers between devices with their start and end apart: 10, of which 3 were waited for; matrix products, arithmetic and copies ran while one was open for 0% of the time, Pallas kernels for 45%

commit v1 on v0

v1 whole, which is shorter than its diff:
```python
import functools
import math

import jax
import jax.numpy as jnp
from jax import lax
from jax.experimental import pallas as pl
from jax.experimental.pallas import tpu as pltpu
from jax.sharding import PartitionSpec as P

HEADS = 16
LANES = 128
GROUP = 256
PARTS = 2
NEG = -1e30
FLOOR = -1e25
LOG2E = math.log2(math.e)
SUM_MIN, SUM_MAX = 2.0**-60, 2.0**100
VMEM_LIMIT = 32 * 1024 * 1024

epsilon = 1e-05


def contract_last(a, b):
    return lax.dot_general(a, b, (((1,), (1,)), ((), ())), preferred_element_type=jnp.float32)


def matmul(a, b):
    return jnp.dot(a, b, preferred_element_type=jnp.float32)


def norm_kernel(bands, tokens_ref, gain_ref, halo_rows_ref, *refs):
    part_refs, (north_ref, south_ref), picked_ref = refs[:PARTS], refs[PARTS : PARTS + 2], refs[PARTS + 2]
    step, steps = pl.program_id(0), pl.num_programs(0)
    values = tokens_ref[...]
    average = jnp.mean(values, axis=-1, keepdims=True)
    centered = values - average
    variance = jnp.mean(centered * centered, axis=-1, keepdims=True)
    normed = (centered * lax.rsqrt(variance + epsilon) * gain_ref[...]).astype(jnp.bfloat16)
    each = steps // PARTS
    for i, ref in enumerate(part_refs):

        @pl.when(step // each == i)
        def _(ref=ref):
            ref[...] = normed

    @pl.when(step == 0)
    def _():
        picked_ref[...] = jnp.zeros_like(picked_ref)

    band = lax.axis_index("lat")
    lists = ((jnp.maximum(band - 1, 0), 1, north_ref), (jnp.minimum(band + 1, bands - 1), 0, south_ref))
    rows = values.shape[0]
    for which, (owner, side, out) in enumerate(lists):
        wanted = halo_rows_ref[pl.ds(owner, 1), side, :]
        slots = step * rows + lax.broadcasted_iota(jnp.int32, (rows, wanted.shape[1]), 0)
        picks = (slots == wanted).astype(jnp.float32).astype(jnp.bfloat16)
        picked = lax.dot_general(
            picks, normed, (((0,), (0,)), ((), ())), preferred_element_type=jnp.float32
        )
        picked_ref[which] += picked

        @pl.when(step == steps - 1)
        def _(which=which, out=out):
            out[...] = picked_ref[which].astype(jnp.bfloat16)


def norm_call(tokens, gain, halo_rows):
    rows, width = tokens.shape
    bands, _, halo = halo_rows.shape
    each = 2
    steps = PARTS * each
    block = rows // steps
    part = jax.ShapeDtypeStruct((rows // PARTS, width), jnp.bfloat16)
    edge = jax.ShapeDtypeStruct((halo, width), jnp.bfloat16)

    def part_spec(i):
        return pl.BlockSpec((block, width), lambda g: (jnp.clip(g - i * each, 0, each - 1), 0))

    return pl.pallas_call(
        functools.partial(norm_kernel, bands),
        out_shape=[part] * PARTS + [edge] * 2,
        grid=(steps,),
        in_specs=[
            pl.BlockSpec((block, width), lambda g: (g, 0)),
            pl.BlockSpec((1, width), lambda g: (0, 0)),
            pl.BlockSpec(halo_rows.shape, lambda g: (0, 0, 0)),
        ],
        out_specs=[part_spec(i) for i in range(PARTS)] + [pl.BlockSpec((halo, width), lambda g: (0, 0))] * 2,
        scratch_shapes=[pltpu.VMEM((2, halo, width), jnp.float32)],
        compiler_params=pltpu.CompilerParams(vmem_limit_bytes=VMEM_LIMIT),
        cost_estimate=pl.CostEstimate(flops=10 * rows * width, bytes_accessed=6 * rows * width, transcendentals=0),
        name="layer_norm",
    )(tokens, gain.reshape(1, width), halo_rows)


def sector_columns(lon, reach):
    core, odd = lon % 2, (lon // 2) % 2
    return {
        "own": reach,
        "partner": reach + 1 - 2 * core,
        "same": reach + 2 - 4 * odd,
        "across": reach + 4 * odd - 2,
        "near": reach + 2 * core - 1,
    }


def block_bias(mask_ref, column, rows, dtype):
    blocks = mask_ref.shape[0]
    values = [jnp.where(mask_ref[b, column] > 0, 0.0, NEG) for b in range(blocks)]
    return jnp.concatenate([jnp.full((rows // blocks, LANES), v, jnp.float32) for v in values], axis=0).astype(dtype)


def safe_group(query, weights, sources, counts_ref, mask_ref, scratch, head_size):
    rows_ref, key_ref, value_ref, top_ref, sum_ref, acc_ref, flag_ref, limit_ref, sem = scratch
    rows = query.shape[0]
    wk, wv = weights
    tile = sources[0][0].shape[0]
    tiles = len(sources)
    blocks = mask_ref.shape[0]
    for t, (ref, column, seen, start) in enumerate(sources):
        size = ref.shape[0]
        copy = pltpu.make_async_copy(ref, rows_ref.at[pl.ds(0, size)], sem)
        copy.start()
        copy.wait()
        key_ref[pl.ds(t * tile, size)] = matmul(rows_ref[pl.ds(0, size)], wk[...]).astype(jnp.bfloat16)
        value_ref[pl.ds(t * tile, size)] = matmul(rows_ref[pl.ds(0, size)], wv[...]).astype(jnp.bfloat16)
        if size < tile:
            rest = pl.ds(t * tile + size, tile - size)
            key_ref[rest] = jnp.zeros((tile - size, key_ref.shape[1]), jnp.bfloat16)
            value_ref[rest] = jnp.zeros((tile - size, key_ref.shape[1]), jnp.bfloat16)
        for b in range(blocks):
            flag_ref[t, b] = mask_ref[b, column] if column is not None else 1
        if column is None:
            limit_ref[t] = jnp.where(seen, size, 0)
        else:
            limit_ref[t] = counts_ref[0] - start
    low = lax.broadcasted_iota(jnp.int32, (rows, LANES), 1) < head_size
    outs = []
    for pair in range(query.shape[1] // LANES):
        lanes = slice(pair * LANES, (pair + 1) * LANES)
        halves = []
        for head in range(2):
            own = jnp.where(low if head == 0 else ~low, query[:, lanes], jnp.zeros((), jnp.bfloat16))
            top_ref[...] = jnp.full_like(top_ref, FLOOR)
            sum_ref[...] = jnp.zeros_like(sum_ref)
            acc_ref[...] = jnp.zeros_like(acc_ref)

            def body(t, carry, own=own, lanes=lanes):
                at = pl.ds(pl.multiple_of(t * tile, tile), tile)
                scores = contract_last(own, key_ref[at, lanes]) * (LOG2E * head_size**-0.5)
                slot = lax.broadcasted_iota(jnp.int32, (1, tile), 1)
                scores = scores + jnp.where(slot < limit_ref[t], 0.0, NEG)
                row_bias = jnp.concatenate(
                    [
                        jnp.full((rows // blocks, 1), jnp.where(flag_ref[t, b] > 0, 0.0, NEG), jnp.float32)
                        for b in range(blocks)
                    ],
                    axis=0,
                )
                scores = scores + row_bias
                old = top_ref[...]
                new = jnp.maximum(old, jnp.max(scores, axis=-1, keepdims=True))
                scale = jnp.exp2(old - new)
                weight = jnp.exp2(scores - new[:, :1])
                sum_ref[...] = sum_ref[...] * scale + jnp.sum(weight, axis=-1, keepdims=True)
                acc_ref[...] = acc_ref[...] * scale + matmul(weight.astype(jnp.bfloat16), value_ref[at, lanes])
                top_ref[...] = new
                return carry

            lax.fori_loop(0, tiles, body, 0)
            halves.append(acc_ref[...] / sum_ref[...])
        outs.append(jnp.where(low, *halves).astype(jnp.bfloat16))
    return jnp.concatenate(outs, axis=1)


def stage_kernel(spec, *refs):
    first, last, sectors, halos, head_size = spec
    refs = list(refs)

    def take(count):
        taken = refs[:count]
        del refs[:count]
        return taken

    counts_ref, mask_ref = take(2)
    sector_refs = [take(PARTS) for _ in sectors]
    halo_refs = take(2) if halos else []
    wq_ref = take(1)[0] if first else None
    wk_ref, wv_ref = take(2)
    if not first:
        query_in, acc_in, sum_in = take(3)
    if last:
        tokens_ref, wo_ref = take(2)
        all_refs = take(5 * PARTS + 2)
        out_ref, res_ref, att_ref = take(3)
    else:
        if first:
            query_out = take(1)[0]
        acc_out, sum_out = take(2)

    reach = mask_ref.shape[1] // 2
    lon, lat = lax.axis_index("lon"), lax.axis_index("lat")
    bands = lax.axis_size("lat")
    columns = sector_columns(lon, reach)
    count = counts_ref[0]

    wk, wv = wk_ref[...], wv_ref[...]
    if first:
        query = jnp.concatenate([matmul(ref[...], wq_ref[...]).astype(jnp.bfloat16) for ref in sector_refs[0]], axis=0)
        query_out[...] = query
    else:
        query = query_in[...]
    rows, width = query.shape
    scaled = query.astype(jnp.float32) * (LOG2E * head_size**-0.5)
    query_hi = scaled.astype(jnp.bfloat16)
    query_lo = (scaled - query_hi.astype(jnp.float32)).astype(jnp.bfloat16)

    tiles = []
    zero = jnp.zeros((), jnp.bfloat16)
    one = jnp.ones((), jnp.bfloat16)
    for name, parts in zip(sectors, sector_refs):
        row_bias = block_bias(mask_ref, columns[name], rows, jnp.bfloat16)
        for i, ref in enumerate(parts):
            key = matmul(ref[...], wk).astype(jnp.bfloat16)
            value = matmul(ref[...], wv)
            start = i * ref.shape[0]
            live = start + lax.broadcasted_iota(jnp.int32, value.shape, 0) < count
            value = jnp.where(live, value, 0.0).astype(jnp.bfloat16)
            ones = jnp.where(live[:, :LANES], 1.0, 0.0)
            tiles.append((key, value, ones, row_bias))
    for ref, seen in zip(halo_refs, (lat > 0, lat < bands - 1)):
        key = matmul(ref[...], wk).astype(jnp.bfloat16)
        there = jnp.where(seen, 1.0, 0.0)
        value = (matmul(ref[...], wv) * there).astype(jnp.bfloat16)
        ones = jnp.full((ref.shape[0], LANES), there, jnp.float32)
        tiles.append((key, value, ones, None))

    low = lax.broadcasted_iota(jnp.int32, (rows, LANES), 1) < head_size
    total = None
    accs = []
    for pair in range(width // LANES):
        lanes = slice(pair * LANES, (pair + 1) * LANES)
        halves = []
        for head in range(2):
            half = low if head == 0 else ~low
            hi = query_hi[:, lanes]
            lo = jnp.where(half, query_lo[:, lanes], zero)
            weights, values = [], []
            for key, value, ones, row_bias in tiles:
                size = key.shape[0]
                key_half = (lax.broadcasted_iota(jnp.int32, (size, LANES), 1) < head_size) == (head == 0)
                left = jnp.where(half, hi, zero if row_bias is None else row_bias)
                left = jnp.concatenate([left, lo], axis=1)
                right = jnp.concatenate([jnp.where(key_half, key[:, lanes], one), key[:, lanes]], axis=1)
                weights.append(jnp.exp2(contract_last(left, right)).astype(jnp.bfloat16))
                here = lax.broadcasted_iota(jnp.int32, (size, LANES), 1) == 2 * pair + head
                summing = jnp.where(here, ones, 0.0).astype(jnp.bfloat16)
                values.append(jnp.concatenate([value[:, lanes], summing], axis=1))
            result = matmul(jnp.concatenate(weights, axis=1), jnp.concatenate(values, axis=0))
            halves.append(result[:, :LANES])
            total = result[:, LANES:] if total is None else total + result[:, LANES:]
        accs.append(jnp.where(low, *halves))
    acc = jnp.concatenate(accs, axis=1)
    if not first:
        acc = acc + acc_in[...]
        total = total + sum_in[...]
    if not last:
        acc_out[...] = acc
        sum_out[...] = total
        return

    inverse = 1.0 / total
    used = lax.broadcasted_iota(jnp.int32, total.shape, 1) < width // head_size
    fine = ((total > SUM_MIN) & (total < SUM_MAX)) | ~used
    attended = []
    for pair in range(width // LANES):
        lanes = slice(pair * LANES, (pair + 1) * LANES)
        scale = jnp.where(low, inverse[:, 2 * pair : 2 * pair + 1], inverse[:, 2 * pair + 1 : 2 * pair + 2])
        attended.append((acc[:, lanes] * scale).astype(jnp.bfloat16))
    att_ref[...] = jnp.concatenate(attended, axis=1)

    @pl.when(jnp.min(fine.astype(jnp.float32)) < 0.5)
    def _():
        sources = []
        for s, name in enumerate(("own", "partner", "same", "across", "near")):
            for i, ref in enumerate(all_refs[s * PARTS : (s + 1) * PARTS]):
                sources.append((ref, columns[name], None, i * ref.shape[0]))
        for ref, seen in zip(all_refs[5 * PARTS :], (lat > 0, lat < bands - 1)):
            sources.append((ref, None, seen, 0))
        att_ref[...] = safe_group(query, (wk_ref, wv_ref), sources, counts_ref, mask_ref, refs, head_size)

    step = pl.program_id(0)

    @pl.when(step == 0)
    def _():
        res_ref[...] = jnp.zeros_like(res_ref)

    at = pl.ds(pl.multiple_of(step * width, width), width)
    res_ref[:, at] += tokens_ref[...]
    res_ref[...] += matmul(att_ref[...], wo_ref[...])

    @pl.when(step == pl.num_programs(0) - 1)
    def _():
        slot = lax.broadcasted_iota(jnp.int32, res_ref.shape, 0)
        out_ref[...] = jnp.where(slot < count, res_ref[...], 0.0)


def stage_call(counts, mask, sectors, sector_parts, halos, qkv_weight, query=None, state=None, final=None):
    first, last = query is None, final is not None
    model, width = qkv_weight.shape[0], qkv_weight.shape[1] // 3
    head_size = width // HEADS
    rows = sum(p.shape[0] for p in sector_parts[0])
    steps = width // GROUP
    smem = pl.BlockSpec(memory_space=pltpu.SMEM)

    def fixed(shape):
        return pl.BlockSpec(shape, lambda g: (0, 0), pipeline_mode=pl.Buffered(1))

    def weight(third):
        return pl.BlockSpec((model, GROUP), lambda g: (0, third * steps + g))

    columns = pl.BlockSpec((rows, GROUP), lambda g: (0, g))
    sums = pl.BlockSpec((rows, LANES), lambda g: (0, g))
    args, specs = [counts, mask], [smem, smem]
    for parts in sector_parts:
        args += parts
        specs += [fixed(p.shape) for p in parts]
    for halo in halos:
        args.append(halo)
        specs.append(fixed(halo.shape))
    for third in range(0 if first else 1, 3):
        args.append(qkv_weight)
        specs.append(weight(third))
    if not first:
        args += [query, *state]
        specs += [columns, columns, sums]
    scratch = []
    wide = jax.ShapeDtypeStruct((rows, width), jnp.float32)
    moved = sum(a.size * a.dtype.itemsize for a in args[2:] if a is not qkv_weight) + 3 * model * width * 2
    if last:
        tokens, out_weight, sources = final
        args += [tokens, out_weight, *sources]
        specs += [columns, pl.BlockSpec((GROUP, out_weight.shape[1]), lambda g: (g, 0))]
        specs += [pl.BlockSpec(memory_space=pl.ANY)] * len(sources)
        out_shape = [wide]
        out_specs = [fixed((rows, width))]
        part = rows // PARTS
        scratch = [
            pltpu.VMEM((rows, width), jnp.float32),
            pltpu.VMEM((rows, GROUP), jnp.bfloat16),
            pltpu.VMEM((part, model), jnp.bfloat16),
            pltpu.VMEM((part * len(sources), GROUP), jnp.bfloat16),
            pltpu.VMEM((part * len(sources), GROUP), jnp.bfloat16),
            pltpu.VMEM((rows, LANES), jnp.float32),
            pltpu.VMEM((rows, LANES), jnp.float32),
            pltpu.VMEM((rows, LANES), jnp.float32),
            pltpu.SMEM((len(sources), mask.shape[0]), jnp.int32),
            pltpu.SMEM((len(sources),), jnp.int32),
            pltpu.SemaphoreType.DMA,
        ]
    else:
        out_shape = [wide, jax.ShapeDtypeStruct((rows, LANES * steps), jnp.float32)]
        out_specs = [columns, sums]
        if first:
            out_shape = [jax.ShapeDtypeStruct((rows, width), jnp.bfloat16)] + out_shape
            out_specs = [columns] + out_specs
    keys = sum(p.shape[0] for parts in sector_parts for p in parts) + sum(h.shape[0] for h in halos)
    flops = 2 * keys * model * 2 * width + 16 * rows * keys * width
    flops += 2 * rows * model * width * (int(first) + int(last))
    outs = pl.pallas_call(
        functools.partial(stage_kernel, (first, last, sectors, bool(halos), head_size)),
        out_shape=out_shape,
        grid=(steps,),
        in_specs=specs,
        out_specs=out_specs,
        scratch_shapes=scratch,
        compiler_params=pltpu.CompilerParams(vmem_limit_bytes=VMEM_LIMIT),
        cost_estimate=pl.CostEstimate(flops=flops, bytes_accessed=moved, transcendentals=rows * keys * HEADS),
        name="attend_" + "_".join(sectors),
    )(*args)
    if last:
        return outs[0]
    if first:
        return outs[0], outs[1:]
    return outs


def permuted(values, axis, target):
    size = lax.axis_size(axis)
    pairs = [(i, target(i)) for i in range(size) if 0 <= target(i) < size]
    return [lax.ppermute(v, axis, pairs) for v in values]


def on_device(tokens, norm_gain, qkv_weight, out_weight, band_counts, halo_rows, window_mask):
    mask = window_mask[0, 0]
    ring = lax.axis_size("lon")
    assert mask.shape[1] == 5 and ring % 4 == 0 and ring >= 8
    local = tokens[0, 0]
    outs = norm_call(local, norm_gain, halo_rows)
    own, north_rows, south_rows = outs[:PARTS], outs[PARTS], outs[PARTS + 1]

    partner = permuted(own, "lon", lambda i: i ^ 1)
    same = permuted(own, "lon", lambda i: i ^ 2)
    from_south = permuted([north_rows], "lat", lambda b: b - 1)[0]
    from_north = permuted([south_rows], "lat", lambda b: b + 1)[0]

    across = permuted(same, "lon", lambda i: (i + (4 if (i // 2) % 2 == 0 else -4)) % ring)
    lon = lax.axis_index("lon")
    gives_same = lon % 2 == (lon // 2) % 2
    near = permuted([jnp.where(gives_same, s, a) for s, a in zip(same, across)], "lon", lambda i: i ^ 1)

    halos = [from_north, from_south]
    query, state = stage_call(band_counts, mask, ["own"], [own], [], qkv_weight)
    state = stage_call(band_counts, mask, ["partner"], [partner], halos, qkv_weight, query, state)
    state = stage_call(band_counts, mask, ["same"], [same], [], qkv_weight, query, state)
    final = (local, out_weight, [*own, *partner, *same, *across, *near, *halos])
    result = stage_call(band_counts, mask, ["across", "near"], [across, near], [], qkv_weight, query, state, final)
    return result[None, None]


def solution(mesh):
    in_specs = (
        P("lat", "lon", None, None),
        P(),
        P(),
        P(),
        P("lat"),
        P(),
        P("lat", "lon", None, None),
    )
    out_specs = P("lat", "lon", None, None)
    return jax.shard_map(
        on_device, mesh=mesh, in_specs=in_specs, out_specs=out_specs, check_vma=False
    )
```

time: 98.4 us -> 256 us (2.60)
  Pallas kernels: 70.6 us -> 216 us
  local copies, waits for them, and re-layouts: 7.94 us -> 20.5 us
    pallas_call x4, Pallas kernels: 69 us -> 212 us  [stage_call(): pl.pallas_call(functools.partial(stage_kernel, (first, last, sectors, boo...]
    unnamed x18 -> x40, local copies, waits for them, and re-layouts: 7.94 us -> 20.5 us
  transfers between devices with their start and end apart: 10 -> 10, of which waited for: 3 -> 3; matrix products, arithmetic and copies ran while one was open for 0% -> 0% of each run, Pallas kernels for 45% -> 13%
where the time goes in v1:
time: 256 us; the launch traced here: 255 us
  Pallas kernels  216 us (84%)
  local copies, waits for them, and re-layouts  20.5 us (8%)
  starting transfers between devices  10.7 us (4%)
  waiting for transfers between devices  6.18 us (2%)
    pallas_call x4, Pallas kernels, stage_call(): pl.pallas_call(functools.partial(stage_kernel, (first, last, sectors, boo...  212 us
    unnamed x40, local copies, waits for them, and re-layouts  20.5 us
    ppermute x10, starting transfers between devices, permuted(): return [lax.ppermute(v, axis, pairs) for v in values]  10.7 us
    ppermute x10, waiting for transfers between devices, permuted(): return [lax.ppermute(v, axis, pairs) for v in values]  6.18 us
  transfers between devices with their start and end apart: 10, of which 3 were waited for; matrix products, arithmetic and copies ran while one was open for 0% of the time, Pallas kernels for 13%

profile of v1, /device:TPU:0, one launch (start us, length us, event | category | flops | bytes accessed | tf_op | source)
XLA Modules:
  0.0 254.9 jit_solution(2022150599924434886)
XLA Ops:
  0.0 0.0 copy-start.7
  0.0 0.0 copy-start
  0.0 1.6 copy-done
  1.6 0.0 copy-start.2
  1.6 0.7 copy-done.2
  2.3 0.0 copy-start.3
  2.3 0.7 copy-done.3
  3.0 4.0 %layer_norm.1 = (bf16[256,1024]{1,0:T(8,128)(2,1)S(1)}, bf16[256,1024]{1,0:T(8,128)(2,1)S(1)}, bf16[128,1024]{1,0:T(8,128)(2,1)}, bf16[128,1024]{1,0:T(8,128)(2,1)S(1)}) custom-call(f32[512,1024]{1,0:T(8,128)S(1)} %bitcast.4, f32[1,1024]{1,0:T(1,128)S(1)} %bitcast.6, s32[4,2,128]{2,1,0:T(2,128)S(1)} %copy-done.3), custom_call_target="tpu_custom_call" | custom-call | flops 5242880 | bytes 3145728 | tf_op jit(solution)/shard_map/layer_norm/pallas_call | solution.py:80
  7.0 4.9 %collective-permute-start.8 = (bf16[128,1024]{1,0:T(8,128)(2,1)S(1)}, bf16[128,1024]{1,0:T(8,128)(2,1)S(1)}, u32[]{:S(2)}, u32[]{:S(2)}) collective-permute-start(bf16[128,1024]{1,0:T(8,128)(2,1)S(1)} %get-tuple-element.19), channel_id=1, source_target_pairs={{0,8},{8,16},{16,24},{1,9},{9,17},{17,25},{2,10},{10,18},{18,26},{... | collective-permute-start | bytes 786440 | tf_op jit(solution)/shard_map/ppermute | solution.py:392
  12.0 0.1 collective-permute-start.6
  12.0 1.6 collective-permute-start
  13.6 0.2 collective-permute-start.7
  13.8 0.5 collective-permute-start.2
  15.0 2.5 collective-permute-done.8.refs_4_.refs_23_
  17.5 1.3 collective-permute-start.9
  18.8 0.0 copy-done.7
  18.8 0.0 copy-start.4
  18.8 2.8 %copy-done.4 = bf16[1024,3072]{1,0:T(8,128)(2,1)S(1)} copy-done((bf16[1024,3072]{1,0:T(8,128)(2,1)S(1)}, bf16[1024,3072]{1,0:T(8,128)(2,1)}, u32[]{:S(2)}) %copy-start.4) | copy-done | bytes 6291480
  21.6 10.5 %attend_own.1 = (bf16[512,1024]{1,0:T(8,128)(2,1)S(1)}, f32[512,1024]{1,0:T(8,128)S(1)}, f32[512,512]{1,0:T(8,128)S(1)}) custom-call(s32[1]{0:T(128)S(6)} %copy.8.refs_0_, s32[4,5]{1,0:T(4,128)S(1)} %bitcast.9, bf16[256,1024]{1,0:T(8,128)(2,1)S(1)} %get-tuple-element.16.refs_2_.refs_13_, bf16[256,1024]{1,0:T(8,128)(2,1)S(1)} %get-tuple-element.17.refs_3_.refs_14_, ...), custom_call_target="tpu_custom_call" | custom-call | flops 7516192768 | bytes 7340032 | tf_op jit(solution)/shard_map/attend_own/pallas_call | solution.py:371
  32.0 0.0 copy-start.12
  32.1 1.3 copy-done.12
  33.4 0.0 copy-start.14
  33.4 1.0 copy-done.14
  34.4 0.0 copy-start.16
  34.4 1.0 copy-done.16
  35.3 2.3 collective-permute-done.2.refs_3_.refs_18_
  37.6 1.5 collective-permute-start.3
  39.1 0.0 collective-permute-done.refs_2_.refs_17_
  39.1 0.5 collective-permute-start.1
  39.6 0.0 collective-permute-done.9.refs_5_.refs_24_
  39.7 0.0 collective-permute-done.6.refs_2_.refs_15_
  39.7 0.0 collective-permute-done.7.refs_3_.refs_16_
  39.7 0.0 copy-start.5
  39.7 2.8 %copy-done.5 = bf16[1024,3072]{1,0:T(8,128)(2,1)S(1)} copy-done((bf16[1024,3072]{1,0:T(8,128)(2,1)S(1)}, bf16[1024,3072]{1,0:T(8,128)(2,1)}, u32[]{:S(2)}) %copy-start.5) | copy-done | bytes 6291480
  42.4 0.0 copy-start.13
  42.5 1.6 copy-done.13
  44.0 0.0 copy-start.15
  44.0 1.2 copy-done.15
  45.3 0.0 copy-start.17
  45.3 1.2 copy-done.17
  46.5 14.3 %attend_partner.1 = (f32[512,1024]{1,0:T(8,128)S(1)}, f32[512,512]{1,0:T(8,128)S(1)}) custom-call(s32[1]{0:T(128)S(6)} %copy.8.refs_0_, s32[4,5]{1,0:T(4,128)S(1)} %bitcast.10, bf16[256,1024]{1,0:T(8,128)(2,1)S(1)} %collective-permute-done.6.refs_2_.refs_15_, bf16[256,1024]{1,0:T(8,128)(2,1)S(1)} %collective-permute-done.7.refs_3_.refs_16_, ...), custom_call_target="tpu_custom_call" | custom-call | flops 9663676416 | bytes 12058624 | tf_op jit(solution)/shard_map/attend_partner/pallas_call | solution.py:371
  60.8 0.0 copy-start.10
  60.9 0.0 collective-permute-done.3.refs_3_.refs_20_
  60.9 0.1 broadcast_select_fusion
  60.9 0.1 collective-permute-start.5
  61.0 1.3 collective-permute-done.1.refs_2_.refs_19_
  62.3 0.1 broadcast_select_fusion.1
  62.4 0.1 collective-permute-start.4
  62.5 0.0 copy-done.10
  62.5 0.0 copy-start.11
  62.5 1.7 copy-done.11
  64.3 0.0 copy-start.1
  64.3 9.4 %attend_same.1 = (f32[512,1024]{1,0:T(8,128)S(1)}, f32[512,512]{1,0:T(8,128)S(1)}) custom-call(s32[1]{0:T(128)S(6)} %copy.8.refs_0_, s32[4,5]{1,0:T(4,128)S(1)} %bitcast.11, bf16[256,1024]{1,0:T(8,128)(2,1)S(1)} %collective-permute-done.refs_2_.refs_17_, bf16[256,1024]{1,0:T(8,128)(2,1)S(1)} %collective-permute-done.2.refs_3_.refs_18_, ...), custom_call_target="tpu_custom_call" | custom-call | flops 6442450944 | bytes 11534336 | tf_op jit(solution)/shard_map/attend_same/pallas_call | solution.py:371
  73.7 0.0 copy-start.8
  73.7 1.3 copy-done.8
  75.0 0.0 collective-permute-done.5.refs_5_.refs_22_
  75.0 0.0 collective-permute-done.4.refs_4_.refs_21_
  75.0 0.0 slice-done
  75.0 0.0 copy-done.1
  75.0 0.0 slice-done.1
  75.0 0.0 copy-done.6
  75.0 0.0 copy-start.9
  75.0 1.6 copy-done.9
  76.6 178.2 %attend_across_near.1 = f32[512,1024]{1,0:T(8,128)} custom-call(s32[1]{0:T(128)S(6)} %copy.8.refs_0_, s32[4,5]{1,0:T(4,128)S(1)} %bitcast.12, bf16[256,1024]{1,0:T(8,128)(2,1)S(1)} %collective-permute-done.1.refs_2_.refs_19_, bf16[256,1024]{1,0:T(8,128)(2,1)S(1)} %collective-permute-done.3.refs_3_.refs_20_, ...), custom_call_target="tpu_custom_call" | custom-call | flops 13958643712 | bytes 12582912 | tf_op jit(solution)/shard_map/attend_across_near/pallas_call | solution.py:371
  (4 shorter events, 0.0 us)
Async XLA Ops:
  0.0 18.8 %copy-start.7 = (s32[1,1,4,5]{3,2,1,0:T(4,128)S(1)}, s32[1,1,4,5]{3,2,1,0:T(4,128)}, u32[]{:S(2)}) copy-start(s32[1,1,4,5]{3,2,1,0:T(4,128)} %param.13) | copy-start | bytes 244
  0.0 1.6 copy-start
  1.6 0.7 copy-start.2
  2.3 0.7 copy-start.3
  7.0 10.5 %collective-permute-start.8 = (bf16[128,1024]{1,0:T(8,128)(2,1)S(1)}, bf16[128,1024]{1,0:T(8,128)(2,1)S(1)}, u32[]{:S(2)}, u32[]{:S(2)}) collective-permute-start(bf16[128,1024]{1,0:T(8,128)(2,1)S(1)} %get-tuple-element.19), channel_id=1, source_target_pairs={{0,8},{8,16},{16,24},{1,9},{9,17},{17,25},{2,10},{10,18},{18,26},{... | collective-permute-start | bytes 786440 | tf_op jit(solution)/shard_map/ppermute | solution.py:392
  12.0 27.7 %collective-permute-start.6 = (bf16[256,1024]{1,0:T(8,128)(2,1)S(1)}, bf16[256,1024]{1,0:T(8,128)(2,1)S(1)}, u32[]{:S(2)}, u32[]{:S(2)}) collective-permute-start(bf16[256,1024]{1,0:T(8,128)(2,1)S(1)} %get-tuple-element.16.refs_2_.refs_13_), channel_id=1, source_target_pairs={{0,1},{1,0},{2,3},{3,2},{4,5},{5,4},{6,7},{7,6},{8,9},{9,8},{10,11... | collective-permute-start | bytes 1572872 | tf_op jit(solution)/shard_map/ppermute | solution.py:392
  12.0 27.1 %collective-permute-start = (bf16[256,1024]{1,0:T(8,128)(2,1)S(1)}, bf16[256,1024]{1,0:T(8,128)(2,1)S(1)}, u32[]{:S(2)}, u32[]{:S(2)}) collective-permute-start(bf16[256,1024]{1,0:T(8,128)(2,1)S(1)} %get-tuple-element.16.refs_2_.refs_13_), channel_id=1, source_target_pairs={{0,2},{1,3},{2,0},{3,1},{4,6},{5,7},{6,4},{7,5},{8,10},{9,11},{10,... | collective-permute-start | bytes 1572872 | tf_op jit(solution)/shard_map/ppermute | solution.py:392
  13.6 26.1 %collective-permute-start.7 = (bf16[256,1024]{1,0:T(8,128)(2,1)S(1)}, bf16[256,1024]{1,0:T(8,128)(2,1)S(1)}, u32[]{:S(2)}, u32[]{:S(2)}) collective-permute-start(bf16[256,1024]{1,0:T(8,128)(2,1)S(1)} %get-tuple-element.17.refs_3_.refs_14_), channel_id=1, source_target_pairs={{0,1},{1,0},{2,3},{3,2},{4,5},{5,4},{6,7},{7,6},{8,9},{9,8},{10,11... | collective-permute-start | bytes 1572872 | tf_op jit(solution)/shard_map/ppermute | solution.py:392
  13.8 23.9 %collective-permute-start.2 = (bf16[256,1024]{1,0:T(8,128)(2,1)S(1)}, bf16[256,1024]{1,0:T(8,128)(2,1)S(1)}, u32[]{:S(2)}, u32[]{:S(2)}) collective-permute-start(bf16[256,1024]{1,0:T(8,128)(2,1)S(1)} %get-tuple-element.17.refs_3_.refs_14_), channel_id=1, source_target_pairs={{0,2},{1,3},{2,0},{3,1},{4,6},{5,7},{6,4},{7,5},{8,10},{9,11},{10,... | collective-permute-start | bytes 1572872 | tf_op jit(solution)/shard_map/ppermute | solution.py:392
  17.5 22.2 %collective-permute-start.9 = (bf16[128,1024]{1,0:T(8,128)(2,1)}, bf16[128,1024]{1,0:T(8,128)(2,1)}, u32[]{:S(2)}, u32[]{:S(2)}) collective-permute-start(bf16[128,1024]{1,0:T(8,128)(2,1)} %get-tuple-element.20), channel_id=1, source_target_pairs={{8,0},{16,8},{24,16},{9,1},{17,9},{25,17},{10,2},{18,10},{26,18},{... | collective-permute-start | bytes 786440 | tf_op jit(solution)/shard_map/ppermute | solution.py:392
  18.8 2.8 %copy-start.4 = (bf16[1024,3072]{1,0:T(8,128)(2,1)S(1)}, bf16[1024,3072]{1,0:T(8,128)(2,1)}, u32[]{:S(2)}) copy-start(bf16[1024,3072]{1,0:T(8,128)(2,1)} %refs_7_.3) | copy-start | bytes 18874372
  32.0 1.3 copy-start.12
  33.4 1.0 copy-start.14
  34.4 1.0 copy-start.16
  37.6 23.2 %collective-permute-start.3 = (bf16[256,1024]{1,0:T(8,128)(2,1)S(1)}, bf16[256,1024]{1,0:T(8,128)(2,1)S(1)}, u32[]{:S(2)}, u32[]{:S(2)}) collective-permute-start(bf16[256,1024]{1,0:T(8,128)(2,1)S(1)} %collective-permute-done.2.refs_3_.refs_18_), channel_id=1, source_target_pairs={{0,4},{1,5},{2,6},{3,7},{4,0},{5,1},{6,2},{7,3},{8,12},{9,13},{10,... | collective-permute-start | bytes 1572872 | tf_op jit(solution)/shard_map/ppermute | solution.py:392
  39.1 23.2 %collective-permute-start.1 = (bf16[256,1024]{1,0:T(8,128)(2,1)S(1)}, bf16[256,1024]{1,0:T(8,128)(2,1)S(1)}, u32[]{:S(2)}, u32[]{:S(2)}) collective-permute-start(bf16[256,1024]{1,0:T(8,128)(2,1)S(1)} %collective-permute-done.refs_2_.refs_17_), channel_id=1, source_target_pairs={{0,4},{1,5},{2,6},{3,7},{4,0},{5,1},{6,2},{7,3},{8,12},{9,13},{10,... | collective-permute-start | bytes 1572872 | tf_op jit(solution)/shard_map/ppermute | solution.py:392
  39.7 2.8 %copy-start.5 = (bf16[1024,3072]{1,0:T(8,128)(2,1)S(1)}, bf16[1024,3072]{1,0:T(8,128)(2,1)}, u32[]{:S(2)}) copy-start(bf16[1024,3072]{1,0:T(8,128)(2,1)} %refs_7_.3) | copy-start | bytes 18874372
  42.4 1.6 copy-start.13
  44.0 1.2 copy-start.15
  45.3 1.2 copy-start.17
  60.8 1.7 copy-start.10
  60.9 14.0 %collective-permute-start.5 = (bf16[256,1024]{1,0:T(8,128)(2,1)S(1)}, bf16[256,1024]{1,0:T(8,128)(2,1)S(1)}, u32[]{:S(2)}, u32[]{:S(2)}) collective-permute-start(bf16[256,1024]{1,0:T(8,128)(2,1)S(1)} %broadcast_select_fusion), channel_id=1, source_target_pairs={{0,1},{1,0},{2,3},{3,2},{4,5},{5,4},{6,7},{7,6},{8,9},{9,8},{10,11... | collective-permute-start | bytes 1572872 | tf_op jit(solution)/shard_map/ppermute | solution.py:392
  62.3 12.6 %slice-start = ((s8[6291456]{0:T(1024)(128)(4,1)}), s8[4194304]{0:T(1024)(128)(4,1)S(1)}, s32[]{:S(2)}) async-start(s8[6291456]{0:T(1024)(128)(4,1)} %bitcast.7), calls=%async_computation | async-start | bytes 8388608
  62.4 12.6 %collective-permute-start.4 = (bf16[256,1024]{1,0:T(8,128)(2,1)S(1)}, bf16[256,1024]{1,0:T(8,128)(2,1)S(1)}, u32[]{:S(2)}, u32[]{:S(2)}) collective-permute-start(bf16[256,1024]{1,0:T(8,128)(2,1)S(1)} %broadcast_select_fusion.1), channel_id=1, source_target_pairs={{0,1},{1,0},{2,3},{3,2},{4,5},{5,4},{6,7},{7,6},{8,9},{9,8},{10,11... | collective-permute-start | bytes 1572872 | tf_op jit(solution)/shard_map/ppermute | solution.py:392
  62.5 1.7 copy-start.11
  64.3 10.7 %copy-start.1 = (f32[1,1,512,1024]{3,2,1,0:T(8,128)S(1)}, f32[1,1,512,1024]{3,2,1,0:T(8,128)}, u32[]{:S(2)}) copy-start(f32[1,1,512,1024]{3,2,1,0:T(8,128)} %param.7) | copy-start | bytes 6291460
  64.3 10.7 %slice-start.1 = ((s8[6291456]{0:T(1024)(128)(4,1)}), s8[2097152]{0:T(1024)(128)(4,1)S(1)}, s32[]{:S(2)}) async-start(s8[6291456]{0:T(1024)(128)(4,1)} %bitcast.7), calls=%async_computation.1 | async-start | bytes 4194304
  64.3 10.8 %copy-start.6 = (bf16[1024,1024]{1,0:T(8,128)(2,1)S(1)}, bf16[1024,1024]{1,0:T(8,128)(2,1)}, u32[]{:S(2)}) copy-start(bf16[1024,1024]{1,0:T(8,128)(2,1)} %refs_12_.1) | copy-start | bytes 6291460
  73.7 1.3 copy-start.8
  75.0 1.6 copy-start.9

commit v2 on v1

--- a/solution.py
+++ b/solution.py
@@ -16,7 +16,8 @@
 FLOOR = -1e25
 LOG2E = math.log2(math.e)
 SUM_MIN, SUM_MAX = 2.0**-60, 2.0**100
-VMEM_LIMIT = 32 * 1024 * 1024
+VMEM_LIMIT = 60 * 1024 * 1024
+CHUNKS = 4
 
 epsilon = 1e-05
 
@@ -29,65 +30,78 @@
     return jnp.dot(a, b, preferred_element_type=jnp.float32)
 
 
-def norm_kernel(bands, tokens_ref, gain_ref, halo_rows_ref, *refs):
-    part_refs, (north_ref, south_ref), picked_ref = refs[:PARTS], refs[PARTS : PARTS + 2], refs[PARTS + 2]
-    step, steps = pl.program_id(0), pl.num_programs(0)
-    values = tokens_ref[...]
-    average = jnp.mean(values, axis=-1, keepdims=True)
-    centered = values - average
-    variance = jnp.mean(centered * centered, axis=-1, keepdims=True)
-    normed = (centered * lax.rsqrt(variance + epsilon) * gain_ref[...]).astype(jnp.bfloat16)
-    each = steps // PARTS
-    for i, ref in enumerate(part_refs):
-
-        @pl.when(step // each == i)
-        def _(ref=ref):
-            ref[...] = normed
-
-    @pl.when(step == 0)
-    def _():
-        picked_ref[...] = jnp.zeros_like(picked_ref)
-
+def norm_kernel(bands, tokens_hbm, gain_hbm, halo_rows_hbm, *refs):
+    outs = refs[: PARTS + 3]
+    tokens_ref, gain_ref, halo_rows_ref, normed_ref, edge_ref, in_sem, out_sem = refs[PARTS + 3 :]
+    rows = tokens_ref.shape[0]
+    block = rows // CHUNKS
+
+    def chunk(i):
+        at = pl.ds(i * block, block)
+        return pltpu.make_async_copy(tokens_hbm.at[at], tokens_ref.at[at], in_sem.at[i])
+
+    small = [
+        pltpu.make_async_copy(gain_hbm, gain_ref, in_sem.at[CHUNKS]),
+        pltpu.make_async_copy(halo_rows_hbm, halo_rows_ref, in_sem.at[CHUNKS + 1]),
+    ]
+    for copy in [chunk(0)] + small + [chunk(i) for i in range(1, CHUNKS)]:
+        copy.start()
+    small[0].wait()
+    gain = gain_ref[...]
+    sent = []
+    part = rows // PARTS
+    for i in range(CHUNKS):
+        chunk(i).wait()
+        at = pl.ds(i * block, block)
+        values = tokens_ref[at]
+        average = jnp.mean(values, axis=-1, keepdims=True)
+        centered = values - average
+        variance = jnp.mean(centered * centered, axis=-1, keepdims=True)
+        normed_ref[at] = (centered * lax.rsqrt(variance + epsilon) * gain).astype(jnp.bfloat16)
+        if (i + 1) * PARTS % CHUNKS == 0:
+            p = (i + 1) * PARTS // CHUNKS - 1
+            sent.append(pltpu.make_async_copy(normed_ref.at[pl.ds(p * part, part)], outs[p], out_sem.at[p]))
+            sent[-1].start()
+    sent.append(pltpu.make_async_copy(normed_ref, outs[PARTS], out_sem.at[PARTS]))
+    sent[-1].start()
+    small[1].wait()
     band = lax.axis_index("lat")
-    lists = ((jnp.maximum(band - 1, 0), 1, north_ref), (jnp.minimum(band + 1, bands - 1), 0, south_ref))
-    rows = values.shape[0]
-    for which, (owner, side, out) in enumerate(lists):
+    lists = ((jnp.maximum(band - 1, 0), 1), (jnp.minimum(band + 1, bands - 1), 0))
+    for which, (owner, side) in enumerate(lists):
         wanted = halo_rows_ref[pl.ds(owner, 1), side, :]
-        slots = step * rows + lax.broadcasted_iota(jnp.int32, (rows, wanted.shape[1]), 0)
+        slots = lax.broadcasted_iota(jnp.int32, (rows, wanted.shape[1]), 0)
         picks = (slots == wanted).astype(jnp.float32).astype(jnp.bfloat16)
         picked = lax.dot_general(
-            picks, normed, (((0,), (0,)), ((), ())), preferred_element_type=jnp.float32
+            picks, normed_ref[...], (((0,), (0,)), ((), ())), preferred_element_type=jnp.float32
         )
-        picked_ref[which] += picked
-
-        @pl.when(step == steps - 1)
-        def _(which=which, out=out):
-            out[...] = picked_ref[which].astype(jnp.bfloat16)
+        edge_ref[which] = picked.astype(jnp.bfloat16)
+        place = PARTS + 1 + which
+        sent.append(pltpu.make_async_copy(edge_ref.at[which], outs[place], out_sem.at[place]))
+        sent[-1].start()
+    for copy in sent:
+        copy.wait()
 
 
 def norm_call(tokens, gain, halo_rows):
     rows, width = tokens.shape
     bands, _, halo = halo_rows.shape
-    each = 2
-    steps = PARTS * each
-    block = rows // steps
     part = jax.ShapeDtypeStruct((rows // PARTS, width), jnp.bfloat16)
+    whole = jax.ShapeDtypeStruct((rows, width), jnp.bfloat16)
     edge = jax.ShapeDtypeStruct((halo, width), jnp.bfloat16)
-
-    def part_spec(i):
-        return pl.BlockSpec((block, width), lambda g: (jnp.clip(g - i * each, 0, each - 1), 0))
-
     return pl.pallas_call(
         functools.partial(norm_kernel, bands),
-        out_shape=[part] * PARTS + [edge] * 2,
-        grid=(steps,),
-        in_specs=[
-            pl.BlockSpec((block, width), lambda g: (g, 0)),
-            pl.BlockSpec((1, width), lambda g: (0, 0)),
-            pl.BlockSpec(halo_rows.shape, lambda g: (0, 0, 0)),
+        out_shape=[part] * PARTS + [whole] + [edge] * 2,
+        in_specs=[pl.BlockSpec(memory_space=pl.ANY)] * 3,
+        out_specs=[pl.BlockSpec(memory_space=pltpu.HBM)] * (PARTS + 3),
+        scratch_shapes=[
+            pltpu.VMEM((rows, width), jnp.float32),
+            pltpu.VMEM((1, width), jnp.float32),
+            pltpu.VMEM(halo_rows.shape, jnp.int32),
+            pltpu.VMEM((rows, width), jnp.bfloat16),
+            pltpu.VMEM((2, halo, width), jnp.bfloat16),
+            pltpu.SemaphoreType.DMA((CHUNKS + 2,)),
+            pltpu.SemaphoreType.DMA((PARTS + 3,)),
         ],
-        out_specs=[part_spec(i) for i in range(PARTS)] + [pl.BlockSpec((halo, width), lambda g: (0, 0))] * 2,
-        scratch_shapes=[pltpu.VMEM((2, halo, width), jnp.float32)],
         compiler_params=pltpu.CompilerParams(vmem_limit_bytes=VMEM_LIMIT),
         cost_estimate=pl.CostEstimate(flops=10 * rows * width, bytes_accessed=6 * rows * width, transcendentals=0),
         name="layer_norm",
@@ -175,7 +189,7 @@
 
 
 def stage_kernel(spec, *refs):
-    first, last, sectors, halos, head_size = spec
+    first, last, sectors, part_counts, halos, head_size, row_block = spec
     refs = list(refs)
 
     def take(count):
@@ -184,7 +198,7 @@
         return taken
 
     counts_ref, mask_ref = take(2)
-    sector_refs = [take(PARTS) for _ in sectors]
+    sector_refs = [take(n) for n in part_counts]
     halo_refs = take(2) if halos else []
     wq_ref = take(1)[0] if first else None
     wk_ref, wv_ref = take(2)
@@ -192,8 +206,8 @@
         query_in, acc_in, sum_in = take(3)
     if last:
         tokens_ref, wo_ref = take(2)
-        all_refs = take(5 * PARTS + 2)
-        out_ref, res_ref, att_ref = take(3)
+        all_refs = take(1 + 4 * PARTS + 2)
+        out_ref, res_ref, att_ref, acc_ref, sum_ref = take(5)
     else:
         if first:
             query_out = take(1)[0]
@@ -227,18 +241,16 @@
             start = i * ref.shape[0]
             live = start + lax.broadcasted_iota(jnp.int32, value.shape, 0) < count
             value = jnp.where(live, value, 0.0).astype(jnp.bfloat16)
-            ones = jnp.where(live[:, :LANES], 1.0, 0.0)
+            ones = jnp.where(live[:, :LANES], 1.0, 0.0).astype(jnp.bfloat16)
             tiles.append((key, value, ones, row_bias))
     for ref, seen in zip(halo_refs, (lat > 0, lat < bands - 1)):
         key = matmul(ref[...], wk).astype(jnp.bfloat16)
         there = jnp.where(seen, 1.0, 0.0)
         value = (matmul(ref[...], wv) * there).astype(jnp.bfloat16)
-        ones = jnp.full((ref.shape[0], LANES), there, jnp.float32)
+        ones = jnp.full((ref.shape[0], LANES), there, jnp.float32).astype(jnp.bfloat16)
         tiles.append((key, value, ones, None))
 
     low = lax.broadcasted_iota(jnp.int32, (rows, LANES), 1) < head_size
-    total = None
-    accs = []
     for pair in range(width // LANES):
         lanes = slice(pair * LANES, (pair + 1) * LANES)
         halves = []
@@ -246,47 +258,51 @@
             half = low if head == 0 else ~low
             hi = query_hi[:, lanes]
             lo = jnp.where(half, query_lo[:, lanes], zero)
-            weights, values = [], []
+            lefts, rights, values = [], [], []
             for key, value, ones, row_bias in tiles:
-                size = key.shape[0]
-                key_half = (lax.broadcasted_iota(jnp.int32, (size, LANES), 1) < head_size) == (head == 0)
+                key_half = (lax.broadcasted_iota(jnp.int32, (key.shape[0], LANES), 1) < head_size) == (head == 0)
                 left = jnp.where(half, hi, zero if row_bias is None else row_bias)
-                left = jnp.concatenate([left, lo], axis=1)
-                right = jnp.concatenate([jnp.where(key_half, key[:, lanes], one), key[:, lanes]], axis=1)
-                weights.append(jnp.exp2(contract_last(left, right)).astype(jnp.bfloat16))
-                here = lax.broadcasted_iota(jnp.int32, (size, LANES), 1) == 2 * pair + head
-                summing = jnp.where(here, ones, 0.0).astype(jnp.bfloat16)
-                values.append(jnp.concatenate([value[:, lanes], summing], axis=1))
-            result = matmul(jnp.concatenate(weights, axis=1), jnp.concatenate(values, axis=0))
-            halves.append(result[:, :LANES])
-            total = result[:, LANES:] if total is None else total + result[:, LANES:]
-        accs.append(jnp.where(low, *halves))
-    acc = jnp.concatenate(accs, axis=1)
-    if not first:
-        acc = acc + acc_in[...]
-        total = total + sum_in[...]
+                lefts.append(jnp.concatenate([left, lo], axis=1))
+                rights.append(jnp.concatenate([jnp.where(key_half, key[:, lanes], one), key[:, lanes]], axis=1))
+                values.append(jnp.where(key_half, value[:, lanes], ones))
+            values = jnp.concatenate(values, axis=0)
+            results = []
+            for r in range(0, rows, row_block):
+                weights = [
+                    jnp.exp2(contract_last(left[r : r + row_block], right)).astype(jnp.bfloat16)
+                    for left, right in zip(lefts, rights)
+                ]
+                results.append(matmul(jnp.concatenate(weights, axis=1), values))
+            halves.append(jnp.concatenate(results, axis=0))
+        acc, total = jnp.where(low, *halves), jnp.where(low, halves[1], halves[0])
+        if not first:
+            acc = acc + acc_in[:, lanes]
+            total = total + sum_in[:, lanes]
+        if last:
+            acc_ref[:, lanes] = acc
+            sum_ref[:, lanes] = total
+        else:
+            acc_out[:, lanes] = acc
+            sum_out[:, lanes] = total
     if not last:
-        acc_out[...] = acc
-        sum_out[...] = total
         return
 
-    inverse = 1.0 / total
-    used = lax.broadcasted_iota(jnp.int32, total.shape, 1) < width // head_size
-    fine = ((total > SUM_MIN) & (total < SUM_MAX)) | ~used
-    attended = []
+    total = sum_ref[...]
+    fine = (total > SUM_MIN) & (total < SUM_MAX)
     for pair in range(width // LANES):
         lanes = slice(pair * LANES, (pair + 1) * LANES)
-        scale = jnp.where(low, inverse[:, 2 * pair : 2 * pair + 1], inverse[:, 2 * pair + 1 : 2 * pair + 2])
-        attended.append((acc[:, lanes] * scale).astype(jnp.bfloat16))
-    att_ref[...] = jnp.concatenate(attended, axis=1)
+        att_ref[:, lanes] = (acc_ref[:, lanes] / pltpu.roll(total[:, lanes], head_size, 1)).astype(jnp.bfloat16)
 
     @pl.when(jnp.min(fine.astype(jnp.float32)) < 0.5)
     def _():
         sources = []
-        for s, name in enumerate(("own", "partner", "same", "across", "near")):
-            for i, ref in enumerate(all_refs[s * PARTS : (s + 1) * PARTS]):
-                sources.append((ref, columns[name], None, i * ref.shape[0]))
-        for ref, seen in zip(all_refs[5 * PARTS :], (lat > 0, lat < bands - 1)):
+        part = rows // PARTS
+        for i in range(PARTS):
+            sources.append((all_refs[0].at[pl.ds(i * part, part)], columns["partner"], None, i * part))
+        for s, name in enumerate(("own", "same", "across", "near")):
+            for i, ref in enumerate(all_refs[1 + s * PARTS : 1 + (s + 1) * PARTS]):
+                sources.append((ref, columns[name], None, i * part))
+        for ref, seen in zip(all_refs[1 + 4 * PARTS :], (lat > 0, lat < bands - 1)):
             sources.append((ref, None, seen, 0))
         att_ref[...] = safe_group(query, (wk_ref, wv_ref), sources, counts_ref, mask_ref, refs, head_size)
 
@@ -306,7 +322,7 @@
         out_ref[...] = jnp.where(slot < count, res_ref[...], 0.0)
 
 
-def stage_call(counts, mask, sectors, sector_parts, halos, qkv_weight, query=None, state=None, final=None):
+def stage_call(counts, mask, sectors, sector_parts, halos, qkv_weight, query=None, state=None, final=None, row_block=512):
     first, last = query is None, final is not None
     model, width = qkv_weight.shape[0], qkv_weight.shape[1] // 3
     head_size = width // HEADS
@@ -321,7 +337,6 @@
         return pl.BlockSpec((model, GROUP), lambda g: (0, third * steps + g))
 
     columns = pl.BlockSpec((rows, GROUP), lambda g: (0, g))
-    sums = pl.BlockSpec((rows, LANES), lambda g: (0, g))
     args, specs = [counts, mask], [smem, smem]
     for parts in sector_parts:
         args += parts
@@ -334,7 +349,7 @@
         specs.append(weight(third))
     if not first:
         args += [query, *state]
-        specs += [columns, columns, sums]
+        specs += [columns] * 3
     scratch = []
     wide = jax.ShapeDtypeStruct((rows, width), jnp.float32)
     moved = sum(a.size * a.dtype.itemsize for a in args[2:] if a is not qkv_weight) + 3 * model * width * 2
@@ -346,30 +361,34 @@
         out_shape = [wide]
         out_specs = [fixed((rows, width))]
         part = rows // PARTS
+        tiles = len(sources) + PARTS - 1
         scratch = [
             pltpu.VMEM((rows, width), jnp.float32),
             pltpu.VMEM((rows, GROUP), jnp.bfloat16),
+            pltpu.VMEM((rows, GROUP), jnp.float32),
+            pltpu.VMEM((rows, GROUP), jnp.float32),
             pltpu.VMEM((part, model), jnp.bfloat16),
-            pltpu.VMEM((part * len(sources), GROUP), jnp.bfloat16),
-            pltpu.VMEM((part * len(sources), GROUP), jnp.bfloat16),
+            pltpu.VMEM((part * tiles, GROUP), jnp.bfloat16),
+            pltpu.VMEM((part * tiles, GROUP), jnp.bfloat16),
             pltpu.VMEM((rows, LANES), jnp.float32),
             pltpu.VMEM((rows, LANES), jnp.float32),
             pltpu.VMEM((rows, LANES), jnp.float32),
-            pltpu.SMEM((len(sources), mask.shape[0]), jnp.int32),
-            pltpu.SMEM((len(sources),), jnp.int32),
+            pltpu.SMEM((tiles, mask.shape[0]), jnp.int32),
+            pltpu.SMEM((tiles,), jnp.int32),
             pltpu.SemaphoreType.DMA,
         ]
     else:
-        out_shape = [wide, jax.ShapeDtypeStruct((rows, LANES * steps), jnp.float32)]
-        out_specs = [columns, sums]
+        out_shape = [wide] * 2
+        out_specs = [columns] * 2
         if first:
             out_shape = [jax.ShapeDtypeStruct((rows, width), jnp.bfloat16)] + out_shape
             out_specs = [columns] + out_specs
+    part_counts = [len(parts) for parts in sector_parts]
     keys = sum(p.shape[0] for parts in sector_parts for p in parts) + sum(h.shape[0] for h in halos)
     flops = 2 * keys * model * 2 * width + 16 * rows * keys * width
     flops += 2 * rows * model * width * (int(first) + int(last))
     outs = pl.pallas_call(
-        functools.partial(stage_kernel, (first, last, sectors, bool(halos), head_size)),
+        functools.partial(stage_kernel, (first, last, sectors, part_counts, bool(halos), head_size, row_block)),
         out_shape=out_shape,
         grid=(steps,),
         in_specs=specs,
@@ -398,23 +417,24 @@
     assert mask.shape[1] == 5 and ring % 4 == 0 and ring >= 8
     local = tokens[0, 0]
     outs = norm_call(local, norm_gain, halo_rows)
-    own, north_rows, south_rows = outs[:PARTS], outs[PARTS], outs[PARTS + 1]
-
-    partner = permuted(own, "lon", lambda i: i ^ 1)
+    own, (whole, north_rows, south_rows) = outs[:PARTS], outs[PARTS:]
+
     same = permuted(own, "lon", lambda i: i ^ 2)
+    partner = permuted([whole], "lon", lambda i: i ^ 1)
     from_south = permuted([north_rows], "lat", lambda b: b - 1)[0]
     from_north = permuted([south_rows], "lat", lambda b: b + 1)[0]
 
-    across = permuted(same, "lon", lambda i: (i + (4 if (i // 2) % 2 == 0 else -4)) % ring)
+    across = permuted(same[:1], "lon", lambda i: (i + (4 if (i // 2) % 2 == 0 else -4)) % ring)
+    across += permuted(own[1:], "lon", lambda i: (i + (-2 if (i // 2) % 2 == 0 else 2)) % ring)
     lon = lax.axis_index("lon")
     gives_same = lon % 2 == (lon // 2) % 2
     near = permuted([jnp.where(gives_same, s, a) for s, a in zip(same, across)], "lon", lambda i: i ^ 1)
 
     halos = [from_north, from_south]
     query, state = stage_call(band_counts, mask, ["own"], [own], [], qkv_weight)
-    state = stage_call(band_counts, mask, ["partner"], [partner], halos, qkv_weight, query, state)
+    state = stage_call(band_counts, mask, ["partner"], [partner], halos, qkv_weight, query, state, row_block=256)
     state = stage_call(band_counts, mask, ["same"], [same], [], qkv_weight, query, state)
-    final = (local, out_weight, [*own, *partner, *same, *across, *near, *halos])
+    final = (local, out_weight, [*partner, *own, *same, *across, *near, *halos])
     result = stage_call(band_counts, mask, ["across", "near"], [across, near], [], qkv_weight, query, state, final)
     return result[None, None]
 

time: 256 us -> 289 us (1.13)
  Pallas kernels: 216 us -> 257 us
  local copies, waits for them, and re-layouts: 20.5 us -> 1.64 us
  waiting for transfers between devices: 6.18 us -> 13.9 us
    pallas_call x4, Pallas kernels: 212 us -> 254 us  [stage_call(): pl.pallas_call(functools.partial(stage_kernel, (first, last, sectors, par...]
    unnamed x40 -> x14, local copies, waits for them, and re-layouts: 20.5 us -> 1.64 us
    ppermute x10 -> x9, waiting for transfers between devices: 6.18 us -> 13.9 us  [permuted(): return [lax.ppermute(v, axis, pairs) for v in values]]
    ppermute x10 -> x9, starting transfers between devices: 10.7 us -> 13.1 us  [permuted(): return [lax.ppermute(v, axis, pairs) for v in values]]
  transfers between devices with their start and end apart: 10 -> 9, of which waited for: 3 -> 3; matrix products, arithmetic and copies ran while one was open for 0% -> 0% of each run, Pallas kernels for 13% -> 14%
where the time goes in v2:
time: 289 us; the launch traced here: 287 us
  Pallas kernels  257 us (89%)
  waiting for transfers between devices  13.9 us (5%)
  starting transfers between devices  13.1 us (5%)
    pallas_call x4, Pallas kernels, stage_call(): pl.pallas_call(functools.partial(stage_kernel, (first, last, sectors, par...  254 us
    ppermute x9, waiting for transfers between devices, permuted(): return [lax.ppermute(v, axis, pairs) for v in values]  13.9 us
    ppermute x9, starting transfers between devices, permuted(): return [lax.ppermute(v, axis, pairs) for v in values]  13.1 us
  transfers between devices with their start and end apart: 9, of which 3 were waited for; matrix products, arithmetic and copies ran while one was open for 0% of the time, Pallas kernels for 14%

profile of v2, /device:TPU:0, one launch (start us, length us, event | category | flops | bytes accessed | tf_op | source)
XLA Modules:
  0.0 286.9 jit_solution(8604978031608366691)
XLA Ops:
  0.0 3.4 %layer_norm.1 = (bf16[256,1024]{1,0:T(8,128)(2,1)}, bf16[256,1024]{1,0:T(8,128)(2,1)}, bf16[512,1024]{1,0:T(8,128)(2,1)}, bf16[128,1024]{1,0:T(8,128)(2,1)}, bf16[128,1024]{1,0:T(8,128)(2,1)}) custom-call(f32[512,1024]{1,0:T(8,128)} %bitcast.4, f32[1,1024]{1,0:T(1,128)} %bitcast.6, s32[4,2,128]{2,1,0:T(2,128)} %halo_rows_hbm.1), custom_call_target="tpu_custom_call" | custom-call | flops 5242880 | bytes 3145728 | tf_op jit(solution)/shard_map/layer_norm/pallas_call | solution.py:91
  3.4 3.0 %collective-permute-start = (bf16[256,1024]{1,0:T(8,128)(2,1)}, bf16[256,1024]{1,0:T(8,128)(2,1)S(1)}, u32[]{:S(2)}, u32[]{:S(2)}) collective-permute-start(bf16[256,1024]{1,0:T(8,128)(2,1)} %get-tuple-element.17.refs_2_.refs_14_), channel_id=1, source_target_pairs={{0,2},{1,3},{2,0},{3,1},{4,6},{5,7},{6,4},{7,5},{8,10},{9,11},{10,... | collective-permute-start | bytes 1572872 | tf_op jit(solution)/shard_map/ppermute | solution.py:411
  6.4 0.1 collective-permute-start.4
  6.5 2.9 %collective-permute-start.2 = (bf16[256,1024]{1,0:T(8,128)(2,1)}, bf16[256,1024]{1,0:T(8,128)(2,1)S(1)}, u32[]{:S(2)}, u32[]{:S(2)}) collective-permute-start(bf16[256,1024]{1,0:T(8,128)(2,1)} %get-tuple-element.18.refs_3_.refs_15_), channel_id=1, source_target_pairs={{0,6},{1,7},{2,4},{3,5},{4,2},{5,3},{6,0},{7,1},{8,14},{9,15},{10,... | collective-permute-start | bytes 1572872 | tf_op jit(solution)/shard_map/ppermute | solution.py:411
  9.4 0.0 collective-permute-start.6
  9.4 3.5 %collective-permute-start.7 = (bf16[128,1024]{1,0:T(8,128)(2,1)}, bf16[128,1024]{1,0:T(8,128)(2,1)S(1)}, u32[]{:S(2)}, u32[]{:S(2)}) collective-permute-start(bf16[128,1024]{1,0:T(8,128)(2,1)} %get-tuple-element.21), channel_id=1, source_target_pairs={{0,8},{8,16},{16,24},{1,9},{9,17},{17,25},{2,10},{10,18},{18,26},{... | collective-permute-start | bytes 786440 | tf_op jit(solution)/shard_map/ppermute | solution.py:411
  13.5 5.8 %collective-permute-done.refs_2_.refs_16_ = bf16[256,1024]{1,0:T(8,128)(2,1)S(1)} collective-permute-done((bf16[256,1024]{1,0:T(8,128)(2,1)}, bf16[256,1024]{1,0:T(8,128)(2,1)S(1)}, u32[]{:S(2)}, u32[]{:S(2)}) %collective-permute-start) | collective-permute-done | bytes 524320 | tf_op jit(solution)/shard_map/ppermute | solution.py:411
  19.4 0.0 copy-start
  19.4 2.1 collective-permute-start.1
  21.5 11.9 %attend_own.1 = (bf16[512,1024]{1,0:T(8,128)(2,1)}, f32[512,1024]{1,0:T(8,128)}, f32[512,1024]{1,0:T(8,128)}) custom-call(s32[1]{0:T(128)S(6)} %copy.8.refs_0_, s32[4,5]{1,0:T(4,128)} %bitcast.7, bf16[256,1024]{1,0:T(8,128)(2,1)} %get-tuple-element.17.refs_2_.refs_14_, bf16[256,1024]{1,0:T(8,128)(2,1)} %get-tuple-element.18.refs_3_.refs_15_, ...), custom_call_target="tpu_custom_call" | custom-call | flops 7516192768 | bytes 7340032 | tf_op jit(solution)/shard_map/attend_own/pallas_call | solution.py:390
  33.4 0.0 collective-permute-done.4.refs_3_.refs_17_
  33.4 0.0 copy-start.1
  33.4 1.3 collective-permute-start.8
  34.7 7.7 %collective-permute-done.2.refs_3_.refs_19_ = bf16[256,1024]{1,0:T(8,128)(2,1)S(1)} collective-permute-done((bf16[256,1024]{1,0:T(8,128)(2,1)}, bf16[256,1024]{1,0:T(8,128)(2,1)S(1)}, u32[]{:S(2)}, u32[]{:S(2)}) %collective-permute-start.2) | collective-permute-done | bytes 524320 | tf_op jit(solution)/shard_map/ppermute | solution.py:411
  42.3 0.0 copy-start.2
  42.3 0.1 broadcast_select_fusion
  42.4 0.1 collective-permute-start.5
  42.5 0.4 collective-permute-done.1.refs_2_.refs_18_
  42.9 0.0 copy-done
  42.9 0.0 copy-start.3
  42.9 0.1 broadcast_select_fusion.1
  43.0 0.1 collective-permute-start.3
  43.1 0.0 collective-permute-done.7.refs_3_.refs_22_
  43.1 0.0 copy-start.6
  43.1 0.0 collective-permute-done.8.refs_4_.refs_23_
  43.1 0.0 collective-permute-done.6.refs_2_.refs_13_
  43.1 0.7 copy-done.6
  43.8 16.4 %attend_partner.1 = (f32[512,1024]{1,0:T(8,128)}, f32[512,1024]{1,0:T(8,128)}) custom-call(s32[1]{0:T(128)S(6)} %copy.8.refs_0_, s32[4,5]{1,0:T(4,128)} %bitcast.8, bf16[512,1024]{1,0:T(8,128)(2,1)} %collective-permute-done.6.refs_2_.refs_13_, bf16[128,1024]{1,0:T(8,128)(2,1)} %copy-done.6, bf16[128,1024]{1,0:T(8,128)(2,1)} %collective-permute-done.8.refs_4_.refs_23_, ...), custom_call_target="tpu_custom_call" | custom-call | flops 9663676416 | bytes 13107200 | tf_op jit(solution)/shard_map/attend_partner/pallas_call | solution.py:390
  60.2 0.0 copy-done.1
  60.2 0.0 copy-done.2
  60.2 0.0 copy-done.3
  60.2 11.3 %attend_same.1 = (f32[512,1024]{1,0:T(8,128)}, f32[512,1024]{1,0:T(8,128)}) custom-call(s32[1]{0:T(128)S(6)} %copy.8.refs_0_, s32[4,5]{1,0:T(4,128)} %bitcast.9, bf16[256,1024]{1,0:T(8,128)(2,1)} %copy-done, bf16[256,1024]{1,0:T(8,128)(2,1)} %copy-done.1, bf16[1024,3072]{1,0:T(8,128)(2,1)} %refs_7_.1, bf16[1024,3072]{1,0:T(8,128)(2,1)} %refs_7_.1, ...), custom_call_target="tpu_custom_call" | custom-call | flops 6442450944 | bytes 12582912 | tf_op jit(solution)/shard_map/attend_same/pallas_call | solution.py:390
  71.5 0.0 collective-permute-done.5.refs_5_.refs_21_
  71.5 0.0 copy-start.4
  71.5 0.0 collective-permute-done.3.refs_4_.refs_20_
  71.5 0.0 copy-start.5
  71.5 0.8 copy-done.4
  72.3 0.2 copy-done.5
  72.4 214.3 %attend_across_near.1 = f32[512,1024]{1,0:T(8,128)} custom-call(s32[1]{0:T(128)S(6)} %copy.8.refs_0_, s32[4,5]{1,0:T(4,128)} %bitcast.10, bf16[256,1024]{1,0:T(8,128)(2,1)} %copy-done.3, bf16[256,1024]{1,0:T(8,128)(2,1)} %copy-done.2, bf16[256,1024]{1,0:T(8,128)(2,1)} %copy-done.5, bf16[256,1024]{1,0:T(8,128)(2,1)} %copy-done.4, bf16[1024,3072]{1,0:T(8,128)(2,1)} %refs_7_.1, ...), custom_call_target="tpu_custom_call" | custom-call | flops 13958643712 | bytes 13631488 | tf_op jit(solution)/shard_map/attend_across_near/pallas_call | solution.py:390
Async XLA Ops:
  3.4 16.0 %collective-permute-start = (bf16[256,1024]{1,0:T(8,128)(2,1)}, bf16[256,1024]{1,0:T(8,128)(2,1)S(1)}, u32[]{:S(2)}, u32[]{:S(2)}) collective-permute-start(bf16[256,1024]{1,0:T(8,128)(2,1)} %get-tuple-element.17.refs_2_.refs_14_), channel_id=1, source_target_pairs={{0,2},{1,3},{2,0},{3,1},{4,6},{5,7},{6,4},{7,5},{8,10},{9,11},{10,... | collective-permute-start | bytes 1572872 | tf_op jit(solution)/shard_map/ppermute | solution.py:411
  6.4 26.9 %collective-permute-start.4 = (bf16[256,1024]{1,0:T(8,128)(2,1)}, bf16[256,1024]{1,0:T(8,128)(2,1)S(1)}, u32[]{:S(2)}, u32[]{:S(2)}) collective-permute-start(bf16[256,1024]{1,0:T(8,128)(2,1)} %get-tuple-element.18.refs_3_.refs_15_), channel_id=1, source_target_pairs={{0,2},{1,3},{2,0},{3,1},{4,6},{5,7},{6,4},{7,5},{8,10},{9,11},{10,... | collective-permute-start | bytes 1572872 | tf_op jit(solution)/shard_map/ppermute | solution.py:411
  6.5 35.8 %collective-permute-start.2 = (bf16[256,1024]{1,0:T(8,128)(2,1)}, bf16[256,1024]{1,0:T(8,128)(2,1)S(1)}, u32[]{:S(2)}, u32[]{:S(2)}) collective-permute-start(bf16[256,1024]{1,0:T(8,128)(2,1)} %get-tuple-element.18.refs_3_.refs_15_), channel_id=1, source_target_pairs={{0,6},{1,7},{2,4},{3,5},{4,2},{5,3},{6,0},{7,1},{8,14},{9,15},{10,... | collective-permute-start | bytes 1572872 | tf_op jit(solution)/shard_map/ppermute | solution.py:411
  9.4 33.7 %collective-permute-start.6 = (bf16[512,1024]{1,0:T(8,128)(2,1)}, bf16[512,1024]{1,0:T(8,128)(2,1)}, u32[]{:S(2)}, u32[]{:S(2)}) collective-permute-start(bf16[512,1024]{1,0:T(8,128)(2,1)} %get-tuple-element.20), channel_id=1, source_target_pairs={{0,1},{1,0},{2,3},{3,2},{4,5},{5,4},{6,7},{7,6},{8,9},{9,8},{10,11... | collective-permute-start | bytes 3145736 | tf_op jit(solution)/shard_map/ppermute | solution.py:411
  9.4 33.7 %collective-permute-start.7 = (bf16[128,1024]{1,0:T(8,128)(2,1)}, bf16[128,1024]{1,0:T(8,128)(2,1)S(1)}, u32[]{:S(2)}, u32[]{:S(2)}) collective-permute-start(bf16[128,1024]{1,0:T(8,128)(2,1)} %get-tuple-element.21), channel_id=1, source_target_pairs={{0,8},{8,16},{16,24},{1,9},{9,17},{17,25},{2,10},{10,18},{18,26},{... | collective-permute-start | bytes 786440 | tf_op jit(solution)/shard_map/ppermute | solution.py:411
  19.4 23.5 %copy-start = (bf16[256,1024]{1,0:T(8,128)(2,1)}, bf16[256,1024]{1,0:T(8,128)(2,1)S(1)}, u32[]{:S(2)}) copy-start(bf16[256,1024]{1,0:T(8,128)(2,1)S(1)} %collective-permute-done.refs_2_.refs_16_) | copy-start | bytes 1572868
  19.4 23.5 %collective-permute-start.1 = (bf16[256,1024]{1,0:T(8,128)(2,1)S(1)}, bf16[256,1024]{1,0:T(8,128)(2,1)S(1)}, u32[]{:S(2)}, u32[]{:S(2)}) collective-permute-start(bf16[256,1024]{1,0:T(8,128)(2,1)S(1)} %collective-permute-done.refs_2_.refs_16_), channel_id=1, source_target_pairs={{0,4},{1,5},{2,6},{3,7},{4,0},{5,1},{6,2},{7,3},{8,12},{9,13},{10,... | collective-permute-start | bytes 1572872 | tf_op jit(solution)/shard_map/ppermute | solution.py:411
  33.4 26.8 %copy-start.1 = (bf16[256,1024]{1,0:T(8,128)(2,1)}, bf16[256,1024]{1,0:T(8,128)(2,1)S(1)}, u32[]{:S(2)}) copy-start(bf16[256,1024]{1,0:T(8,128)(2,1)S(1)} %collective-permute-done.4.refs_3_.refs_17_) | copy-start | bytes 1572868
  33.4 9.7 %collective-permute-start.8 = (bf16[128,1024]{1,0:T(8,128)(2,1)}, bf16[128,1024]{1,0:T(8,128)(2,1)}, u32[]{:S(2)}, u32[]{:S(2)}) collective-permute-start(bf16[128,1024]{1,0:T(8,128)(2,1)} %get-tuple-element.22), channel_id=1, source_target_pairs={{8,0},{16,8},{24,16},{9,1},{17,9},{25,17},{10,2},{18,10},{26,18},{... | collective-permute-start | bytes 786440 | tf_op jit(solution)/shard_map/ppermute | solution.py:411
  42.3 17.8 %copy-start.2 = (bf16[256,1024]{1,0:T(8,128)(2,1)}, bf16[256,1024]{1,0:T(8,128)(2,1)S(1)}, u32[]{:S(2)}) copy-start(bf16[256,1024]{1,0:T(8,128)(2,1)S(1)} %collective-permute-done.2.refs_3_.refs_19_) | copy-start | bytes 1572868
  42.4 29.1 %collective-permute-start.5 = (bf16[256,1024]{1,0:T(8,128)(2,1)S(1)}, bf16[256,1024]{1,0:T(8,128)(2,1)S(1)}, u32[]{:S(2)}, u32[]{:S(2)}) collective-permute-start(bf16[256,1024]{1,0:T(8,128)(2,1)S(1)} %broadcast_select_fusion), channel_id=1, source_target_pairs={{0,1},{1,0},{2,3},{3,2},{4,5},{5,4},{6,7},{7,6},{8,9},{9,8},{10,11... | collective-permute-start | bytes 1572872 | tf_op jit(solution)/shard_map/ppermute | solution.py:411
  42.9 17.3 %copy-start.3 = (bf16[256,1024]{1,0:T(8,128)(2,1)}, bf16[256,1024]{1,0:T(8,128)(2,1)S(1)}, u32[]{:S(2)}) copy-start(bf16[256,1024]{1,0:T(8,128)(2,1)S(1)} %collective-permute-done.1.refs_2_.refs_18_) | copy-start | bytes 1572868
  43.0 28.5 %collective-permute-start.3 = (bf16[256,1024]{1,0:T(8,128)(2,1)S(1)}, bf16[256,1024]{1,0:T(8,128)(2,1)S(1)}, u32[]{:S(2)}, u32[]{:S(2)}) collective-permute-start(bf16[256,1024]{1,0:T(8,128)(2,1)S(1)} %broadcast_select_fusion.1), channel_id=1, source_target_pairs={{0,1},{1,0},{2,3},{3,2},{4,5},{5,4},{6,7},{7,6},{8,9},{9,8},{10,11... | collective-permute-start | bytes 1572872 | tf_op jit(solution)/shard_map/ppermute | solution.py:411
  43.1 0.7 copy-start.6
  71.5 0.8 copy-start.4
  71.5 1.0 copy-start.5

commit v3 on v2

--- a/solution.py
+++ b/solution.py
@@ -189,7 +189,7 @@
 
 
 def stage_kernel(spec, *refs):
-    first, last, sectors, part_counts, halos, head_size, row_block = spec
+    first, last, sectors, part_starts, halos, head_size = spec
     refs = list(refs)
 
     def take(count):
@@ -198,7 +198,7 @@
         return taken
 
     counts_ref, mask_ref = take(2)
-    sector_refs = [take(n) for n in part_counts]
+    sector_refs = [take(len(starts)) for starts in part_starts]
     halo_refs = take(2) if halos else []
     wq_ref = take(1)[0] if first else None
     wk_ref, wv_ref = take(2)
@@ -207,11 +207,14 @@
     if last:
         tokens_ref, wo_ref = take(2)
         all_refs = take(1 + 4 * PARTS + 2)
-        out_ref, res_ref, att_ref, acc_ref, sum_ref = take(5)
+        (out_ref,) = take(1)
     else:
         if first:
             query_out = take(1)[0]
         acc_out, sum_out = take(2)
+    key_ref, value_ref, ones_ref, score_ref, weight_ref = take(5)
+    if last:
+        res_ref, att_ref, acc_out, sum_out = take(4)
 
     reach = mask_ref.shape[1] // 2
     lon, lat = lax.axis_index("lon"), lax.axis_index("lat")
@@ -230,68 +233,91 @@
     query_hi = scaled.astype(jnp.bfloat16)
     query_lo = (scaled - query_hi.astype(jnp.float32)).astype(jnp.bfloat16)
 
-    tiles = []
     zero = jnp.zeros((), jnp.bfloat16)
     one = jnp.ones((), jnp.bfloat16)
-    for name, parts in zip(sectors, sector_refs):
-        row_bias = block_bias(mask_ref, columns[name], rows, jnp.bfloat16)
-        for i, ref in enumerate(parts):
-            key = matmul(ref[...], wk).astype(jnp.bfloat16)
+    biases, spans = [], []
+    at = 0
+    for name, parts, starts in zip(sectors, sector_refs, part_starts):
+        begin = at
+        for ref, start in zip(parts, starts):
+            size = ref.shape[0]
+            here = pl.ds(at, size)
+            key_ref[:, here] = matmul(ref[...], wk).astype(jnp.bfloat16).T
             value = matmul(ref[...], wv)
-            start = i * ref.shape[0]
-            live = start + lax.broadcasted_iota(jnp.int32, value.shape, 0) < count
-            value = jnp.where(live, value, 0.0).astype(jnp.bfloat16)
-            ones = jnp.where(live[:, :LANES], 1.0, 0.0).astype(jnp.bfloat16)
-            tiles.append((key, value, ones, row_bias))
-    for ref, seen in zip(halo_refs, (lat > 0, lat < bands - 1)):
-        key = matmul(ref[...], wk).astype(jnp.bfloat16)
-        there = jnp.where(seen, 1.0, 0.0)
-        value = (matmul(ref[...], wv) * there).astype(jnp.bfloat16)
-        ones = jnp.full((ref.shape[0], LANES), there, jnp.float32).astype(jnp.bfloat16)
-        tiles.append((key, value, ones, None))
+            if start + size <= rows // 2:
+                value_ref[here] = value.astype(jnp.bfloat16)
+                ones_ref[here] = jnp.ones((size, LANES), jnp.bfloat16)
+            else:
+                live = start + lax.broadcasted_iota(jnp.int32, value.shape, 0) < count
+                value_ref[here] = jnp.where(live, value, 0.0).astype(jnp.bfloat16)
+                ones_ref[here] = jnp.where(live[:, :LANES], 1.0, 0.0).astype(jnp.bfloat16)
+            at += size
+        spans.append((begin, at))
+        biases.append(block_bias(mask_ref, columns[name], rows, jnp.bfloat16))
+    if halo_refs:
+        begin = at
+        for ref, seen in zip(halo_refs, (lat > 0, lat < bands - 1)):
+            size = ref.shape[0]
+            here = pl.ds(at, size)
+            there = jnp.where(seen, 1.0, 0.0)
+            key_ref[:, here] = matmul(ref[...], wk).astype(jnp.bfloat16).T
+            value_ref[here] = (matmul(ref[...], wv) * there).astype(jnp.bfloat16)
+            ones_ref[here] = jnp.full((size, LANES), there, jnp.float32).astype(jnp.bfloat16)
+            at += size
+        spans.append((begin, at))
+        biases.append(None)
 
     low = lax.broadcasted_iota(jnp.int32, (rows, LANES), 1) < head_size
-    for pair in range(width // LANES):
-        lanes = slice(pair * LANES, (pair + 1) * LANES)
-        halves = []
-        for head in range(2):
-            half = low if head == 0 else ~low
-            hi = query_hi[:, lanes]
-            lo = jnp.where(half, query_lo[:, lanes], zero)
-            lefts, rights, values = [], [], []
-            for key, value, ones, row_bias in tiles:
-                key_half = (lax.broadcasted_iota(jnp.int32, (key.shape[0], LANES), 1) < head_size) == (head == 0)
-                left = jnp.where(half, hi, zero if row_bias is None else row_bias)
-                lefts.append(jnp.concatenate([left, lo], axis=1))
-                rights.append(jnp.concatenate([jnp.where(key_half, key[:, lanes], one), key[:, lanes]], axis=1))
-                values.append(jnp.where(key_half, value[:, lanes], ones))
-            values = jnp.concatenate(values, axis=0)
-            results = []
-            for r in range(0, rows, row_block):
-                weights = [
-                    jnp.exp2(contract_last(left[r : r + row_block], right)).astype(jnp.bfloat16)
-                    for left, right in zip(lefts, rights)
-                ]
-                results.append(matmul(jnp.concatenate(weights, axis=1), values))
-            halves.append(jnp.concatenate(results, axis=0))
-        acc, total = jnp.where(low, *halves), jnp.where(low, halves[1], halves[0])
+    low_key = lax.broadcasted_iota(jnp.int32, (LANES, at), 0) < head_size
+    low_value = lax.broadcasted_iota(jnp.int32, (at, LANES), 1) < head_size
+
+    def lanes_of(unit):
+        return slice(unit // 2 * LANES, (unit // 2 + 1) * LANES)
+
+    def score(unit):
+        lanes, odd = lanes_of(unit), unit % 2
+        half = ~low if odd else low
+        lo = jnp.where(half, query_lo[:, lanes], zero)
+        key = key_ref[lanes, :]
+        right = jnp.concatenate([jnp.where(~low_key if odd else low_key, key, one), key], axis=0)
+        for (begin, end), bias in zip(spans, biases):
+            left = jnp.where(half, query_hi[:, lanes], zero if bias is None else bias)
+            score_ref[odd, :, begin:end] = matmul(jnp.concatenate([left, lo], axis=1), right[:, begin:end])
+
+    def weigh(unit):
+        weight_ref[unit % 2] = jnp.exp2(score_ref[unit % 2]).astype(jnp.bfloat16)
+
+    halves = {}
+
+    def gather(unit):
+        lanes, odd = lanes_of(unit), unit % 2
+        values = jnp.where(~low_value if odd else low_value, value_ref[:, lanes], ones_ref[...])
+        halves[odd] = matmul(weight_ref[odd], values)
+        if not odd:
+            return
+        acc, total = jnp.where(low, halves[0], halves[1]), jnp.where(low, halves[1], halves[0])
         if not first:
             acc = acc + acc_in[:, lanes]
             total = total + sum_in[:, lanes]
-        if last:
-            acc_ref[:, lanes] = acc
-            sum_ref[:, lanes] = total
-        else:
-            acc_out[:, lanes] = acc
-            sum_out[:, lanes] = total
+        acc_out[:, lanes] = acc
+        sum_out[:, lanes] = total
+
+    units = width // head_size
+    for u in range(units + 2):
+        if u < units:
+            score(u)
+        if 0 <= u - 1 < units:
+            weigh(u - 1)
+        if 0 <= u - 2 < units:
+            gather(u - 2)
     if not last:
         return
 
-    total = sum_ref[...]
+    total = sum_out[...]
     fine = (total > SUM_MIN) & (total < SUM_MAX)
     for pair in range(width // LANES):
         lanes = slice(pair * LANES, (pair + 1) * LANES)
-        att_ref[:, lanes] = (acc_ref[:, lanes] / pltpu.roll(total[:, lanes], head_size, 1)).astype(jnp.bfloat16)
+        att_ref[:, lanes] = (acc_out[:, lanes] / pltpu.roll(total[:, lanes], head_size, 1)).astype(jnp.bfloat16)
 
     @pl.when(jnp.min(fine.astype(jnp.float32)) < 0.5)
     def _():
@@ -322,11 +348,11 @@
         out_ref[...] = jnp.where(slot < count, res_ref[...], 0.0)
 
 
-def stage_call(counts, mask, sectors, sector_parts, halos, qkv_weight, query=None, state=None, final=None, row_block=512):
+def stage_call(block_rows, counts, mask, sectors, sector_parts, halos, qkv_weight, query=None, state=None, final=None, starts=None):
     first, last = query is None, final is not None
     model, width = qkv_weight.shape[0], qkv_weight.shape[1] // 3
     head_size = width // HEADS
-    rows = sum(p.shape[0] for p in sector_parts[0])
+    rows = mask.shape[0] * block_rows
     steps = width // GROUP
     smem = pl.BlockSpec(memory_space=pltpu.SMEM)
 
@@ -350,7 +376,14 @@
     if not first:
         args += [query, *state]
         specs += [columns] * 3
-    scratch = []
+    keys = sum(p.shape[0] for parts in sector_parts for p in parts) + sum(h.shape[0] for h in halos)
+    scratch = [
+        pltpu.VMEM((GROUP, keys), jnp.bfloat16),
+        pltpu.VMEM((keys, GROUP), jnp.bfloat16),
+        pltpu.VMEM((keys, LANES), jnp.bfloat16),
+        pltpu.VMEM((2, rows, keys), jnp.float32),
+        pltpu.VMEM((2, rows, keys), jnp.bfloat16),
+    ]
     wide = jax.ShapeDtypeStruct((rows, width), jnp.float32)
     moved = sum(a.size * a.dtype.itemsize for a in args[2:] if a is not qkv_weight) + 3 * model * width * 2
     if last:
@@ -362,7 +395,7 @@
         out_specs = [fixed((rows, width))]
         part = rows // PARTS
         tiles = len(sources) + PARTS - 1
-        scratch = [
+        scratch += [
             pltpu.VMEM((rows, width), jnp.float32),
             pltpu.VMEM((rows, GROUP), jnp.bfloat16),
             pltpu.VMEM((rows, GROUP), jnp.float32),
@@ -383,12 +416,10 @@
         if first:
             out_shape = [jax.ShapeDtypeStruct((rows, width), jnp.bfloat16)] + out_shape
             out_specs = [columns] + out_specs
-    part_counts = [len(parts) for parts in sector_parts]
-    keys = sum(p.shape[0] for parts in sector_parts for p in parts) + sum(h.shape[0] for h in halos)
     flops = 2 * keys * model * 2 * width + 16 * rows * keys * width
     flops += 2 * rows * model * width * (int(first) + int(last))
     outs = pl.pallas_call(
-        functools.partial(stage_kernel, (first, last, sectors, part_counts, bool(halos), head_size, row_block)),
+        functools.partial(stage_kernel, (first, last, sectors, starts, bool(halos), head_size)),
         out_shape=out_shape,
         grid=(steps,),
         in_specs=specs,
@@ -416,26 +447,48 @@
     ring = lax.axis_size("lon")
     assert mask.shape[1] == 5 and ring % 4 == 0 and ring >= 8
     local = tokens[0, 0]
+    rows = local.shape[0]
     outs = norm_call(local, norm_gain, halo_rows)
     own, (whole, north_rows, south_rows) = outs[:PARTS], outs[PARTS:]
 
     same = permuted(own, "lon", lambda i: i ^ 2)
+    across = permuted(own[1:], "lon", lambda i: (i + (-2 if (i // 2) % 2 == 0 else 2)) % ring)
     partner = permuted([whole], "lon", lambda i: i ^ 1)
-    from_south = permuted([north_rows], "lat", lambda b: b - 1)[0]
-    from_north = permuted([south_rows], "lat", lambda b: b + 1)[0]
-
-    across = permuted(same[:1], "lon", lambda i: (i + (4 if (i // 2) % 2 == 0 else -4)) % ring)
-    across += permuted(own[1:], "lon", lambda i: (i + (-2 if (i // 2) % 2 == 0 else 2)) % ring)
+    halos = [
+        permuted([south_rows], "lat", lambda b: b + 1)[0],
+        permuted([north_rows], "lat", lambda b: b - 1)[0],
+    ]
     lon = lax.axis_index("lon")
     gives_same = lon % 2 == (lon // 2) % 2
-    near = permuted([jnp.where(gives_same, s, a) for s, a in zip(same, across)], "lon", lambda i: i ^ 1)
-
-    halos = [from_north, from_south]
-    query, state = stage_call(band_counts, mask, ["own"], [own], [], qkv_weight)
-    state = stage_call(band_counts, mask, ["partner"], [partner], halos, qkv_weight, query, state, row_block=256)
-    state = stage_call(band_counts, mask, ["same"], [same], [], qkv_weight, query, state)
+
+    def swapped(mine, others):
+        return permuted([jnp.where(gives_same, mine, others)], "lon", lambda i: i ^ 1)[0]
+
+    stage = functools.partial(stage_call, rows // mask.shape[0], band_counts, mask)
+    half = rows // PARTS
+    query, state = stage(["own"], [own], [], qkv_weight, starts=[[0, half]])
+
+    same[0], query, state = lax.optimization_barrier((same[0], query, state))
+    across = permuted(same[:1], "lon", lambda i: (i + (4 if (i // 2) % 2 == 0 else -4)) % ring) + across
+    state = stage(["partner"], [partner], halos, qkv_weight, query, state, starts=[[0]])
+
+    across[0], state = lax.optimization_barrier((across[0], state))
+    near = [swapped(same[0], across[0])]
+    state = stage(["same", "across"], [same[:1], across[:1]], [], qkv_weight, query, state, starts=[[0], [0]])
+
+    across[1], state = lax.optimization_barrier((across[1], state))
+    near.append(swapped(same[1], across[1]))
     final = (local, out_weight, [*partner, *own, *same, *across, *near, *halos])
-    result = stage_call(band_counts, mask, ["across", "near"], [across, near], [], qkv_weight, query, state, final)
+    result = stage(
+        ["same", "across", "near"],
+        [same[1:], across[1:], near],
+        [],
+        qkv_weight,
+        query,
+        state,
+        final,
+        starts=[[half], [half], [0, half]],
+    )
     return result[None, None]
 
 

time: 289 us -> 277 us (0.958)
  waiting for transfers between devices: 13.9 us -> 2.22 us
    ppermute x9, waiting for transfers between devices: 13.9 us -> 2.22 us  [permuted(): return [lax.ppermute(v, axis, pairs) for v in values]]
  transfers between devices with their start and end apart: 9 -> 9, of which waited for: 3 -> 2; matrix products, arithmetic and copies ran while one was open for 0% -> 0% of each run, Pallas kernels for 14% -> 14%
where the time goes in v3:
time: 277 us; the launch traced here: 274 us
  Pallas kernels  255 us (92%)
  starting transfers between devices  12.2 us (4%)
  local copies, waits for them, and re-layouts  2.89 us (1%)
    pallas_call x4, Pallas kernels, stage_call(): pl.pallas_call(functools.partial(stage_kernel, (first, last, sectors, sta...  252 us
    ppermute x9, starting transfers between devices, permuted(): return [lax.ppermute(v, axis, pairs) for v in values]  12.2 us
  transfers between devices with their start and end apart: 9, of which 2 were waited for; matrix products, arithmetic and copies ran while one was open for 0% of the time, Pallas kernels for 14%

profile of v3, /device:TPU:0, one launch (start us, length us, event | category | flops | bytes accessed | tf_op | source)
XLA Modules:
  0.0 273.6 jit_solution(16432207842976103565)
XLA Ops:
  0.0 3.4 %layer_norm.1 = (bf16[256,1024]{1,0:T(8,128)(2,1)}, bf16[256,1024]{1,0:T(8,128)(2,1)}, bf16[512,1024]{1,0:T(8,128)(2,1)}, bf16[128,1024]{1,0:T(8,128)(2,1)}, bf16[128,1024]{1,0:T(8,128)(2,1)}) custom-call(f32[512,1024]{1,0:T(8,128)} %bitcast.4, f32[1,1024]{1,0:T(1,128)} %bitcast.6, s32[4,2,128]{2,1,0:T(2,128)} %halo_rows_hbm.1), custom_call_target="tpu_custom_call" | custom-call | flops 5242880 | bytes 3145728 | tf_op jit(solution)/shard_map/layer_norm/pallas_call | solution.py:91
  3.4 0.5 collective-permute-start.4
  3.9 2.6 collective-permute-start.2
  6.5 3.5 %collective-permute-start.5 = (bf16[128,1024]{1,0:T(8,128)(2,1)}, bf16[128,1024]{1,0:T(8,128)(2,1)S(1)}, u32[]{:S(2)}, u32[]{:S(2)}) collective-permute-start(bf16[128,1024]{1,0:T(8,128)(2,1)} %get-tuple-element.34), channel_id=1, source_target_pairs={{0,8},{8,16},{16,24},{1,9},{9,17},{17,25},{2,10},{10,18},{18,26},{... | collective-permute-start | bytes 786440 | tf_op jit(solution)/shard_map/ppermute | solution.py:442
  10.0 1.3 collective-permute-start.6
  11.3 1.6 collective-permute-start.1
  13.5 11.7 %attend_own.1 = (bf16[512,1024]{1,0:T(8,128)(2,1)}, f32[512,1024]{1,0:T(8,128)}, f32[512,1024]{1,0:T(8,128)}) custom-call(s32[1]{0:T(128)S(6)} %copy.8.refs_0_, s32[4,5]{1,0:T(4,128)} %bitcast.7, bf16[256,1024]{1,0:T(8,128)(2,1)} %get-tuple-element.28.refs_2_.refs_14_, bf16[256,1024]{1,0:T(8,128)(2,1)} %get-tuple-element.27.refs_3_.refs_15_, ...), custom_call_target="tpu_custom_call" | custom-call | flops 7516192768 | bytes 7340032 | tf_op jit(solution)/shard_map/attend_own/pallas_call | solution.py:421
  25.2 0.0 collective-permute-done.2.refs_2_.refs_16_
  25.2 0.0 copy-start
  25.2 1.6 collective-permute-start
  26.7 0.0 collective-permute-done.5.refs_3_.refs_22_
  26.7 0.0 copy-start.8
  26.7 0.5 collective-permute-start.3
  27.3 0.0 collective-permute-done.6.refs_4_.refs_23_
  27.3 0.0 collective-permute-done.4.refs_2_.refs_13_
  27.3 0.2 copy-done.8
  27.5 0.0 copy-start.5
  27.5 1.0 copy-done.5
  28.5 15.1 %attend_partner.1 = (f32[512,1024]{1,0:T(8,128)}, f32[512,1024]{1,0:T(8,128)}) custom-call(s32[1]{0:T(128)S(6)} %copy.8.refs_0_, s32[4,5]{1,0:T(4,128)} %bitcast.8, bf16[512,1024]{1,0:T(8,128)(2,1)} %copy-done.5, bf16[128,1024]{1,0:T(8,128)(2,1)} %copy-done.8, bf16[128,1024]{1,0:T(8,128)(2,1)} %collective-permute-done.6.refs_4_.refs_23_, ...), custom_call_target="tpu_custom_call" | custom-call | flops 9663676416 | bytes 13107200 | tf_op jit(solution)/shard_map/attend_partner/pallas_call | solution.py:421
  43.6 0.0 copy-done
  43.6 0.0 collective-permute-done.3.refs_3_.refs_18_
  43.6 0.0 copy-start.4
  43.6 0.8 copy-done.4
  44.4 0.0 copy-start.1
  44.4 11.2 %attend_same_across.1 = (f32[512,1024]{1,0:T(8,128)}, f32[512,1024]{1,0:T(8,128)}) custom-call(s32[1]{0:T(128)S(6)} %copy.8.refs_0_, s32[4,5]{1,0:T(4,128)} %bitcast.9, bf16[256,1024]{1,0:T(8,128)(2,1)} %copy-done, bf16[256,1024]{1,0:T(8,128)(2,1)} %copy-done.4, bf16[1024,3072]{1,0:T(8,128)(2,1)} %refs_7_.1, bf16[1024,3072]{1,0:T(8,128)(2,1)} %refs_7_.1, ...), custom_call_target="tpu_custom_call" | custom-call | flops 6442450944 | bytes 12582912 | tf_op jit(solution)/shard_map/attend_same_across/pallas_call | solution.py:421
  55.6 0.0 collective-permute-done.1.refs_3_.refs_19_
  55.6 0.0 copy-start.2
  55.6 0.0 copy-done.1
  55.6 0.1 broadcast_select_fusion.1
  55.7 0.0 collective-permute-done.refs_2_.refs_17_
  55.7 0.0 copy-start.3
  55.7 0.1 broadcast_select_fusion
  55.8 0.6 collective-permute-start.8
  56.4 0.1 collective-permute-start.7
  56.5 1.5 collective-permute-done.8.refs_5_.refs_21_
  57.9 0.0 copy-start.6
  57.9 0.7 collective-permute-done.7.refs_4_.refs_20_
  58.7 0.0 copy-done.2
  58.7 0.0 copy-done.3
  58.7 0.1 copy-done.6
  58.7 0.0 copy-start.7
  58.7 0.8 copy-done.7
  59.5 213.9 %attend_same_across_near.1 = f32[512,1024]{1,0:T(8,128)} custom-call(s32[1]{0:T(128)S(6)} %copy.8.refs_0_, s32[4,5]{1,0:T(4,128)} %bitcast.10, bf16[256,1024]{1,0:T(8,128)(2,1)} %copy-done.3, bf16[256,1024]{1,0:T(8,128)(2,1)} %copy-done.2, bf16[256,1024]{1,0:T(8,128)(2,1)} %copy-done.7, bf16[256,1024]{1,0:T(8,128)(2,1)} %copy-done.6, ...), custom_call_target="tpu_custom_call" | custom-call | flops 13958643712 | bytes 13631488 | tf_op jit(solution)/shard_map/attend_same_across_near/pallas_call | solution.py:421
Async XLA Ops:
  3.4 23.8 %collective-permute-start.4 = (bf16[512,1024]{1,0:T(8,128)(2,1)}, bf16[512,1024]{1,0:T(8,128)(2,1)S(1)}, u32[]{:S(2)}, u32[]{:S(2)}) collective-permute-start(bf16[512,1024]{1,0:T(8,128)(2,1)} %get-tuple-element.33), channel_id=1, source_target_pairs={{0,1},{1,0},{2,3},{3,2},{4,5},{5,4},{6,7},{7,6},{8,9},{9,8},{10,11... | collective-permute-start | bytes 3145736 | tf_op jit(solution)/shard_map/ppermute | solution.py:442
  3.9 21.2 %collective-permute-start.2 = (bf16[256,1024]{1,0:T(8,128)(2,1)}, bf16[256,1024]{1,0:T(8,128)(2,1)S(1)}, u32[]{:S(2)}, u32[]{:S(2)}) collective-permute-start(bf16[256,1024]{1,0:T(8,128)(2,1)} %get-tuple-element.28.refs_2_.refs_14_), channel_id=1, source_target_pairs={{0,2},{1,3},{2,0},{3,1},{4,6},{5,7},{6,4},{7,5},{8,10},{9,11},{10,... | collective-permute-start | bytes 1572872 | tf_op jit(solution)/shard_map/ppermute | solution.py:442
  6.5 20.2 %collective-permute-start.5 = (bf16[128,1024]{1,0:T(8,128)(2,1)}, bf16[128,1024]{1,0:T(8,128)(2,1)S(1)}, u32[]{:S(2)}, u32[]{:S(2)}) collective-permute-start(bf16[128,1024]{1,0:T(8,128)(2,1)} %get-tuple-element.34), channel_id=1, source_target_pairs={{0,8},{8,16},{16,24},{1,9},{9,17},{17,25},{2,10},{10,18},{18,26},{... | collective-permute-start | bytes 786440 | tf_op jit(solution)/shard_map/ppermute | solution.py:442
  10.0 17.3 %collective-permute-start.6 = (bf16[128,1024]{1,0:T(8,128)(2,1)}, bf16[128,1024]{1,0:T(8,128)(2,1)}, u32[]{:S(2)}, u32[]{:S(2)}) collective-permute-start(bf16[128,1024]{1,0:T(8,128)(2,1)} %get-tuple-element.35), channel_id=1, source_target_pairs={{8,0},{16,8},{24,16},{9,1},{17,9},{25,17},{10,2},{18,10},{26,18},{... | collective-permute-start | bytes 786440 | tf_op jit(solution)/shard_map/ppermute | solution.py:442
  11.3 44.3 %collective-permute-start.1 = (bf16[256,1024]{1,0:T(8,128)(2,1)}, bf16[256,1024]{1,0:T(8,128)(2,1)S(1)}, u32[]{:S(2)}, u32[]{:S(2)}) collective-permute-start(bf16[256,1024]{1,0:T(8,128)(2,1)} %get-tuple-element.27.refs_3_.refs_15_), channel_id=1, source_target_pairs={{0,6},{1,7},{2,4},{3,5},{4,2},{5,3},{6,0},{7,1},{8,14},{9,15},{10,... | collective-permute-start | bytes 1572872 | tf_op jit(solution)/shard_map/ppermute | solution.py:442
  25.2 18.4 %copy-start = (bf16[256,1024]{1,0:T(8,128)(2,1)}, bf16[256,1024]{1,0:T(8,128)(2,1)S(1)}, u32[]{:S(2)}) copy-start(bf16[256,1024]{1,0:T(8,128)(2,1)S(1)} %collective-permute-done.2.refs_2_.refs_16_) | copy-start | bytes 1572868
  25.2 30.5 %collective-permute-start = (bf16[256,1024]{1,0:T(8,128)(2,1)}, bf16[256,1024]{1,0:T(8,128)(2,1)S(1)}, u32[]{:S(2)}, u32[]{:S(2)}) collective-permute-start(bf16[256,1024]{1,0:T(8,128)(2,1)} %get-tuple-element.27.refs_3_.refs_15_), channel_id=1, source_target_pairs={{0,2},{1,3},{2,0},{3,1},{4,6},{5,7},{6,4},{7,5},{8,10},{9,11},{10,... | collective-permute-start | bytes 1572872 | tf_op jit(solution)/shard_map/ppermute | solution.py:442
  26.7 0.7 copy-start.8
  26.7 16.9 %collective-permute-start.3 = (bf16[256,1024]{1,0:T(8,128)(2,1)S(1)}, bf16[256,1024]{1,0:T(8,128)(2,1)S(1)}, u32[]{:S(2)}, u32[]{:S(2)}) collective-permute-start(bf16[256,1024]{1,0:T(8,128)(2,1)S(1)} %collective-permute-done.2.refs_2_.refs_16_), channel_id=1, source_target_pairs={{0,4},{1,5},{2,6},{3,7},{4,0},{5,1},{6,2},{7,3},{8,12},{9,13},{10,... | collective-permute-start | bytes 1572872 | tf_op jit(solution)/shard_map/ppermute | solution.py:442
  27.5 1.0 copy-start.5
  43.6 0.8 copy-start.4
  44.4 11.2 %copy-start.1 = (bf16[256,1024]{1,0:T(8,128)(2,1)S(1)}, bf16[256,1024]{1,0:T(8,128)(2,1)}, u32[]{:S(2)}) copy-start(bf16[256,1024]{1,0:T(8,128)(2,1)} %copy-done) | copy-start | bytes 1572868
  55.6 3.1 %copy-start.2 = (bf16[256,1024]{1,0:T(8,128)(2,1)}, bf16[256,1024]{1,0:T(8,128)(2,1)S(1)}, u32[]{:S(2)}) copy-start(bf16[256,1024]{1,0:T(8,128)(2,1)S(1)} %collective-permute-done.1.refs_3_.refs_19_) | copy-start | bytes 1572868
  55.7 3.0 %copy-start.3 = (bf16[256,1024]{1,0:T(8,128)(2,1)}, bf16[256,1024]{1,0:T(8,128)(2,1)S(1)}, u32[]{:S(2)}) copy-start(bf16[256,1024]{1,0:T(8,128)(2,1)S(1)} %collective-permute-done.refs_2_.refs_17_) | copy-start | bytes 1572868
  55.8 2.1 collective-permute-start.8
  56.4 2.3 collective-permute-start.7
  57.9 0.8 copy-start.6
  58.7 0.8 copy-start.7

commit v4 on v3

v4 whole, which is shorter than its diff:
```python
import functools
import math

import jax
import jax.numpy as jnp
from jax import lax
from jax.experimental import pallas as pl
from jax.experimental.pallas import tpu as pltpu
from jax.sharding import PartitionSpec as P

HEADS = 16
LANES = 128
GROUP = 256
PARTS = 2
NEG = -1e30
FLOOR = -1e25
LOG2E = math.log2(math.e)
SUM_MIN, SUM_MAX = 2.0**-60, 2.0**100
VMEM_LIMIT = 60 * 1024 * 1024
CHUNKS = 4

epsilon = 1e-05


def contract_last(a, b):
    return lax.dot_general(a, b, (((1,), (1,)), ((), ())), preferred_element_type=jnp.float32)


def matmul(a, b):
    return jnp.dot(a, b, preferred_element_type=jnp.float32)


def norm_kernel(bands, tokens_hbm, gain_hbm, halo_rows_hbm, *refs):
    outs = refs[: PARTS + 3]
    tokens_ref, gain_ref, halo_rows_ref, normed_ref, edge_ref, in_sem, out_sem = refs[PARTS + 3 :]
    rows = tokens_ref.shape[0]
    block = rows // CHUNKS

    def chunk(i):
        at = pl.ds(i * block, block)
        return pltpu.make_async_copy(tokens_hbm.at[at], tokens_ref.at[at], in_sem.at[i])

    small = [
        pltpu.make_async_copy(gain_hbm, gain_ref, in_sem.at[CHUNKS]),
        pltpu.make_async_copy(halo_rows_hbm, halo_rows_ref, in_sem.at[CHUNKS + 1]),
    ]
    for copy in [chunk(0)] + small + [chunk(i) for i in range(1, CHUNKS)]:
        copy.start()
    small[0].wait()
    gain = gain_ref[...]
    sent = []
    part = rows // PARTS
    for i in range(CHUNKS):
        chunk(i).wait()
        at = pl.ds(i * block, block)
        values = tokens_ref[at]
        average = jnp.mean(values, axis=-1, keepdims=True)
        centered = values - average
        variance = jnp.mean(centered * centered, axis=-1, keepdims=True)
        normed_ref[at] = (centered * lax.rsqrt(variance + epsilon) * gain).astype(jnp.bfloat16)
        if (i + 1) * PARTS % CHUNKS == 0:
            p = (i + 1) * PARTS // CHUNKS - 1
            sent.append(pltpu.make_async_copy(normed_ref.at[pl.ds(p * part, part)], outs[p], out_sem.at[p]))
            sent[-1].start()
    sent.append(pltpu.make_async_copy(normed_ref, outs[PARTS], out_sem.at[PARTS]))
    sent[-1].start()
    small[1].wait()
    band = lax.axis_index("lat")
    lists = ((jnp.maximum(band - 1, 0), 1), (jnp.minimum(band + 1, bands - 1), 0))
    for which, (owner, side) in enumerate(lists):
        wanted = halo_rows_ref[pl.ds(owner, 1), side, :]
        slots = lax.broadcasted_iota(jnp.int32, (rows, wanted.shape[1]), 0)
        picks = (slots == wanted).astype(jnp.float32).astype(jnp.bfloat16)
        picked = lax.dot_general(
            picks, normed_ref[...], (((0,), (0,)), ((), ())), preferred_element_type=jnp.float32
        )
        edge_ref[which] = picked.astype(jnp.bfloat16)
        place = PARTS + 1 + which
        sent.append(pltpu.make_async_copy(edge_ref.at[which], outs[place], out_sem.at[place]))
        sent[-1].start()
    for copy in sent:
        copy.wait()


def norm_call(tokens, gain, halo_rows):
    rows, width = tokens.shape
    bands, _, halo = halo_rows.shape
    part = jax.ShapeDtypeStruct((rows // PARTS, width), jnp.bfloat16)
    whole = jax.ShapeDtypeStruct((rows, width), jnp.bfloat16)
    edge = jax.ShapeDtypeStruct((halo, width), jnp.bfloat16)
    return pl.pallas_call(
        functools.partial(norm_kernel, bands),
        out_shape=[part] * PARTS + [whole] + [edge] * 2,
        in_specs=[pl.BlockSpec(memory_space=pl.ANY)] * 3,
        out_specs=[pl.BlockSpec(memory_space=pltpu.HBM)] * (PARTS + 3),
        scratch_shapes=[
            pltpu.VMEM((rows, width), jnp.float32),
            pltpu.VMEM((1, width), jnp.float32),
            pltpu.VMEM(halo_rows.shape, jnp.int32),
            pltpu.VMEM((rows, width), jnp.bfloat16),
            pltpu.VMEM((2, halo, width), jnp.bfloat16),
            pltpu.SemaphoreType.DMA((CHUNKS + 2,)),
            pltpu.SemaphoreType.DMA((PARTS + 3,)),
        ],
        compiler_params=pltpu.CompilerParams(vmem_limit_bytes=VMEM_LIMIT),
        cost_estimate=pl.CostEstimate(flops=10 * rows * width, bytes_accessed=6 * rows * width, transcendentals=0),
        name="layer_norm",
    )(tokens, gain.reshape(1, width), halo_rows)


def sector_columns(lon, reach):
    core, odd = lon % 2, (lon // 2) % 2
    return {
        "own": reach,
        "partner": reach + 1 - 2 * core,
        "same": reach + 2 - 4 * odd,
        "across": reach + 4 * odd - 2,
        "near": reach + 2 * core - 1,
    }


def block_bias(mask_ref, column, rows, dtype):
    blocks = mask_ref.shape[0]
    values = [jnp.where(mask_ref[b, column] > 0, 0.0, NEG) for b in range(blocks)]
    return jnp.concatenate([jnp.full((rows // blocks, LANES), v, jnp.float32) for v in values], axis=0).astype(dtype)


def safe_attention(query_ref, weights, sources, counts_ref, mask_ref, att_ref, scratch, head_size):
    rows_ref, key_ref, value_ref, top_ref, sum_ref, acc_ref, flag_ref, limit_ref, sem = scratch
    pairs, rows, _ = query_ref.shape
    wk_ref, wv_ref = weights
    groups = wk_ref.shape[0]
    tile = sources[0][0].shape[0]
    blocks = mask_ref.shape[0]
    low = lax.broadcasted_iota(jnp.int32, (rows, LANES), 1) < head_size

    def group_body(g, carry):
        for t, (ref, column, seen, start) in enumerate(sources):
            size = ref.shape[0]
            copy = pltpu.make_async_copy(ref, rows_ref.at[pl.ds(0, size)], sem)
            copy.start()
            copy.wait()
            key_ref[pl.ds(t * tile, size)] = matmul(rows_ref[pl.ds(0, size)], wk_ref[g]).astype(jnp.bfloat16)
            value_ref[pl.ds(t * tile, size)] = matmul(rows_ref[pl.ds(0, size)], wv_ref[g]).astype(jnp.bfloat16)
            if size < tile:
                rest = pl.ds(t * tile + size, tile - size)
                key_ref[rest] = jnp.zeros((tile - size, key_ref.shape[1]), jnp.bfloat16)
                value_ref[rest] = jnp.zeros((tile - size, key_ref.shape[1]), jnp.bfloat16)
            for b in range(blocks):
                flag_ref[t, b] = mask_ref[b, column] if column is not None else 1
            if column is None:
                limit_ref[t] = jnp.where(seen, size, 0)
            else:
                limit_ref[t] = counts_ref[0] - start
        for pair in range(pairs // groups):
            lanes = slice(pair * LANES, (pair + 1) * LANES)
            place = g * (pairs // groups) + pair
            halves = []
            for head in range(2):
                own = jnp.where(low if head == 0 else ~low, query_ref[place], jnp.zeros((), jnp.bfloat16))
                top_ref[...] = jnp.full_like(top_ref, FLOOR)
                sum_ref[...] = jnp.zeros_like(sum_ref)
                acc_ref[...] = jnp.zeros_like(acc_ref)

                def body(t, carry, own=own, lanes=lanes):
                    at = pl.ds(pl.multiple_of(t * tile, tile), tile)
                    scores = contract_last(own, key_ref[at, lanes]) * (LOG2E * head_size**-0.5)
                    slot = lax.broadcasted_iota(jnp.int32, (1, tile), 1)
                    scores = scores + jnp.where(slot < limit_ref[t], 0.0, NEG)
                    row_bias = jnp.concatenate(
                        [
                            jnp.full((rows // blocks, 1), jnp.where(flag_ref[t, b] > 0, 0.0, NEG), jnp.float32)
                            for b in range(blocks)
                        ],
                        axis=0,
                    )
                    scores = scores + row_bias
                    old = top_ref[...]
                    new = jnp.maximum(old, jnp.max(scores, axis=-1, keepdims=True))
                    scale = jnp.exp2(old - new)
                    weight = jnp.exp2(scores - new[:, :1])
                    sum_ref[...] = sum_ref[...] * scale + jnp.sum(weight, axis=-1, keepdims=True)
                    acc_ref[...] = acc_ref[...] * scale + matmul(weight.astype(jnp.bfloat16), value_ref[at, lanes])
                    top_ref[...] = new
                    return carry

                lax.fori_loop(0, len(sources), body, 0)
                halves.append(acc_ref[...] / sum_ref[...])
            att_ref[place] = jnp.where(low, *halves).astype(jnp.bfloat16)
        return carry

    lax.fori_loop(0, groups, group_body, 0)


def stage_kernel(spec, *refs):
    first, last, sectors, part_starts, halos, head_size = spec
    refs = list(refs)

    def take(count):
        taken = refs[:count]
        del refs[:count]
        return taken

    counts_ref, mask_ref = take(2)
    sector_refs = [take(len(starts)) for starts in part_starts]
    halo_refs = take(2) if halos else []
    (qkv_hbm,) = take(1)
    if not first:
        query_hbm, sums_hbm = take(2)
    if last:
        tokens_hbm, wo_hbm = take(2)
        all_refs = take(1 + 4 * PARTS + 2)
        (out_hbm,) = take(1)
    else:
        if first:
            (query_out,) = take(1)
        (sums_out,) = take(1)
    rows_ref, weight_ref, key_ref, value_ref, ones_ref, query_ref, sums_ref = take(7)
    score_refs, exp_refs = take(2), take(2)
    rows_sem, weight_sem, in_sem, out_sem = take(4)
    if last:
        att_ref, tokens_ref, wo_ref, fine_ref = take(4)

    pairs, rows, _ = query_ref.shape
    groups, model, group = weight_ref.shape[1:]
    each = pairs // groups
    reach = mask_ref.shape[1] // 2
    lon, lat = lax.axis_index("lon"), lax.axis_index("lat")
    bands = lax.axis_size("lat")
    columns = sector_columns(lon, reach)
    count = counts_ref[0]
    thirds = range(0 if first else 1, 3)

    row_copies = []
    at = 0
    for ref in [r for parts in sector_refs for r in parts] + halo_refs:
        here = rows_ref.at[pl.ds(at, ref.shape[0])]
        row_copies.append(pltpu.make_async_copy(ref, here, rows_sem.at[len(row_copies)]))
        at += ref.shape[0]
    keys = at

    def weight_copy(third, g):
        start = third * groups * group + g * group
        if not isinstance(start, int):
            start = pl.multiple_of(start, group)
        t = third - thirds[0]
        return pltpu.make_async_copy(qkv_hbm.at[:, pl.ds(start, group)], weight_ref.at[t, g], weight_sem.at[t, g])

    later = []
    if not first:
        later.append(pltpu.make_async_copy(query_hbm, query_ref, in_sem.at[0]))
        later.append(pltpu.make_async_copy(sums_hbm, sums_ref, in_sem.at[1]))
    if last:
        later.append(pltpu.make_async_copy(tokens_hbm, tokens_ref, in_sem.at[2]))
        later.append(pltpu.make_async_copy(wo_hbm, wo_ref, in_sem.at[3]))
    for copy in row_copies + [weight_copy(t, g) for g in range(groups) for t in thirds] + later:
        copy.start()

    biases, spans, pieces = [], [], []
    at = 0
    for name, parts, starts in zip(sectors, sector_refs, part_starts):
        begin = at
        for ref, start in zip(parts, starts):
            for r in range(0, ref.shape[0], group):
                size = min(group, ref.shape[0] - r)
                if start + r + size <= rows // 2:
                    live = None
                else:
                    slot = start + r + lax.broadcasted_iota(jnp.int32, (size, group), 0)
                    live = jnp.where(slot < count, 1.0, 0.0)
                pieces.append((at, size, live))
                at += size
        spans.append((begin, at))
        biases.append(None if name == "own" else block_bias(mask_ref, columns[name], rows, jnp.bfloat16))
    if halo_refs:
        begin = at
        for ref, seen in zip(halo_refs, (lat > 0, lat < bands - 1)):
            size = ref.shape[0]
            pieces.append((at, size, jnp.full((size, group), jnp.where(seen, 1.0, 0.0), jnp.float32)))
            at += size
        spans.append((begin, at))
        biases.append(None)
    for begin, size, live in pieces:
        ones = jnp.ones((size, LANES), jnp.float32) if live is None else live[:, :LANES]
        ones_ref[pl.ds(begin, size)] = ones.astype(jnp.bfloat16)
    for copy in row_copies:
        copy.wait()

    def project(g, carry):
        for t in thirds:
            weight_copy(t, g).wait()
        for begin, size, live in pieces:
            here = pl.ds(begin, size)
            normed = rows_ref[here]
            if first:
                query = matmul(normed, weight_ref[0, g]).astype(jnp.bfloat16)
                for p in range(each):
                    query_ref[g * each + p, here] = query[:, p * LANES : (p + 1) * LANES]
            key = matmul(normed, weight_ref[1 - thirds[0], g]).astype(jnp.bfloat16).T
            value = matmul(normed, weight_ref[2 - thirds[0], g])
            if live is not None:
                value = jnp.where(live > 0, value, 0.0)
            value = value.astype(jnp.bfloat16)
            for p in range(each):
                lanes = slice(p * LANES, (p + 1) * LANES)
                key_ref[g * each + p, :, here] = key[lanes]
                value_ref[g * each + p, here] = value[:, lanes]
        return carry

    lax.fori_loop(0, groups, project, 0)
    if first:
        sent = pltpu.make_async_copy(query_ref, query_out, in_sem.at[0])
        sent.start()
    else:
        for copy in later[:2]:
            copy.wait()

    zero = jnp.zeros((), jnp.bfloat16)
    one = jnp.ones((), jnp.bfloat16)
    low = lax.broadcasted_iota(jnp.int32, (rows, LANES), 1) < head_size
    low_key = lax.broadcasted_iota(jnp.int32, (LANES, keys), 0) < head_size
    low_value = lax.broadcasted_iota(jnp.int32, (keys, LANES), 1) < head_size

    def score(pair, odd):
        half = ~low if odd else low
        query = query_ref[pair]
        right = jnp.where(~low_key if odd else low_key, key_ref[pair], one)
        for (begin, end), bias in zip(spans, biases):
            left = jnp.where(half, query, zero if bias is None else bias)
            score_refs[odd][:, begin:end] = matmul(left, right[:, begin:end])

    def weigh(odd):
        exp_refs[odd][...] = jnp.exp2(score_refs[odd][...] * (LOG2E * head_size**-0.5)).astype(jnp.bfloat16)

    def gather(pair, odd):
        values = jnp.where(~low_value if odd else low_value, value_ref[pair], ones_ref[...])
        result = matmul(exp_refs[odd][...], values)
        if not first:
            result = result + sums_ref[2 * pair + odd]
        sums_ref[2 * pair + odd] = result

    def finish(pair):
        if not last:
            at = pl.ds(2 * pair, 2)
            pltpu.make_async_copy(sums_ref.at[at], sums_out.at[at], out_sem.at[pair]).start()
            return
        even, odd = sums_ref[2 * pair], sums_ref[2 * pair + 1]
        total = jnp.where(low, odd, even)
        fine = jnp.where((total > SUM_MIN) & (total < SUM_MAX), 1.0, 0.0)
        fine_ref[...] = jnp.minimum(fine_ref[...], fine)
        att_ref[pair] = (jnp.where(low, even, odd) / pltpu.roll(total, head_size, 1)).astype(jnp.bfloat16)

    if last:
        fine_ref[...] = jnp.ones_like(fine_ref)
    score(0, 0)
    score(0, 1)
    weigh(0)

    def attend(pair, carry):
        score(pair, 0)
        weigh(1)
        gather(pair - 1, 0)
        score(pair, 1)
        weigh(0)
        gather(pair - 1, 1)
        finish(pair - 1)
        return carry

    lax.fori_loop(1, pairs, attend, 0)
    weigh(1)
    gather(pairs - 1, 0)
    gather(pairs - 1, 1)
    finish(pairs - 1)

    if not last:
        if first:
            sent.wait()

        def arrived(pair, carry):
            at = pl.ds(2 * pair, 2)
            pltpu.make_async_copy(sums_ref.at[at], sums_out.at[at], out_sem.at[pair]).wait()
            return carry

        lax.fori_loop(0, pairs, arrived, 0)
        return

    @pl.when(jnp.min(fine_ref[...]) < 0.5)
    def _():
        sources = []
        part = rows // PARTS
        for i in range(PARTS):
            sources.append((all_refs[0].at[pl.ds(i * part, part)], columns["partner"], None, i * part))
        for s, name in enumerate(("own", "same", "across", "near")):
            for i, ref in enumerate(all_refs[1 + s * PARTS : 1 + (s + 1) * PARTS]):
                sources.append((ref, columns[name], None, i * part))
        for ref, seen in zip(all_refs[1 + 4 * PARTS :], (lat > 0, lat < bands - 1)):
            sources.append((ref, None, seen, 0))
        weights = (weight_ref.at[0], weight_ref.at[1])
        safe_attention(query_ref, weights, sources, counts_ref, mask_ref, att_ref, refs, head_size)

    for copy in later[2:]:
        copy.wait()
    attended = jnp.concatenate([att_ref[p] for p in range(pairs)], axis=1)
    live = lax.broadcasted_iota(jnp.int32, (rows, group), 0) < count
    sent = []
    for n in range(out_hbm.shape[1] // group):
        lanes = pl.ds(n * group, group)
        result = tokens_ref[:, lanes] + matmul(attended, wo_ref[:, lanes])
        tokens_ref[:, lanes] = jnp.where(live, result, 0.0)
        sent.append(pltpu.make_async_copy(tokens_ref.at[:, lanes], out_hbm.at[:, lanes], out_sem.at[n]))
        sent[-1].start()
    for copy in sent:
        copy.wait()


def stage_call(block_rows, counts, mask, sectors, sector_parts, halos, qkv_weight, query=None, sums=None, final=None, starts=None):
    first, last = query is None, final is not None
    model, width = qkv_weight.shape[0], qkv_weight.shape[1] // 3
    head_size = width // HEADS
    rows = mask.shape[0] * block_rows
    pairs, groups = width // LANES, width // GROUP
    thirds = 3 if first else 2
    smem = pl.BlockSpec(memory_space=pltpu.SMEM)
    hbm = pl.BlockSpec(memory_space=pl.ANY)
    sources = [p for parts in sector_parts for p in parts] + halos
    keys = sum(p.shape[0] for p in sources)
    args = [counts, mask, *sources, qkv_weight]
    if not first:
        args += [query, sums]
    query_shape = jax.ShapeDtypeStruct((pairs, rows, LANES), jnp.bfloat16)
    sums_shape = jax.ShapeDtypeStruct((2 * pairs, rows, LANES), jnp.float32)
    scratch = [
        pltpu.VMEM((keys, model), jnp.bfloat16),
        pltpu.VMEM((thirds, groups, model, GROUP), jnp.bfloat16),
        pltpu.VMEM((pairs, LANES, keys), jnp.bfloat16),
        pltpu.VMEM((pairs, keys, LANES), jnp.bfloat16),
        pltpu.VMEM((keys, LANES), jnp.bfloat16),
        pltpu.VMEM(query_shape.shape, jnp.bfloat16),
        pltpu.VMEM(sums_shape.shape, jnp.float32),
        pltpu.VMEM((rows, keys), jnp.float32),
        pltpu.VMEM((rows, keys), jnp.float32),
        pltpu.VMEM((rows, keys), jnp.bfloat16),
        pltpu.VMEM((rows, keys), jnp.bfloat16),
        pltpu.SemaphoreType.DMA((len(sources),)),
        pltpu.SemaphoreType.DMA((thirds, groups)),
        pltpu.SemaphoreType.DMA((4,)),
        pltpu.SemaphoreType.DMA((pairs,)),
    ]
    if last:
        tokens, out_weight, everything = final
        args += [tokens, out_weight, *everything]
        out_shape = [jax.ShapeDtypeStruct((rows, width), jnp.float32)]
        part = rows // PARTS
        tiles = len(everything) + PARTS - 1
        scratch += [
            pltpu.VMEM((pairs, rows, LANES), jnp.bfloat16),
            pltpu.VMEM(tokens.shape, jnp.float32),
            pltpu.VMEM(out_weight.shape, jnp.bfloat16),
            pltpu.VMEM((rows, LANES), jnp.float32),
            pltpu.VMEM((part, model), jnp.bfloat16),
            pltpu.VMEM((part * tiles, GROUP), jnp.bfloat16),
            pltpu.VMEM((part * tiles, GROUP), jnp.bfloat16),
            pltpu.VMEM((rows, LANES), jnp.float32),
            pltpu.VMEM((rows, LANES), jnp.float32),
            pltpu.VMEM((rows, LANES), jnp.float32),
            pltpu.SMEM((tiles, mask.shape[0]), jnp.int32),
            pltpu.SMEM((tiles,), jnp.int32),
            pltpu.SemaphoreType.DMA,
        ]
    else:
        out_shape = [query_shape, sums_shape] if first else [sums_shape]
    flops = 2 * keys * model * 2 * width + 16 * rows * keys * width
    flops += 2 * rows * model * width * (int(first) + int(last))
    moved = 2 * (thirds * model * width + keys * model) + 4 * rows * width * (2 if first else 5)
    outs = pl.pallas_call(
        functools.partial(stage_kernel, (first, last, sectors, starts, bool(halos), head_size)),
        out_shape=out_shape,
        in_specs=[smem, smem] + [hbm] * (len(args) - 2),
        out_specs=[hbm] * len(out_shape),
        scratch_shapes=scratch,
        compiler_params=pltpu.CompilerParams(vmem_limit_bytes=VMEM_LIMIT),
        cost_estimate=pl.CostEstimate(flops=flops, bytes_accessed=moved, transcendentals=rows * keys * HEADS),
        name="attend_" + "_".join(sectors),
    )(*args)
    return outs if first else outs[0]


def permuted(values, axis, target):
    size = lax.axis_size(axis)
    pairs = [(i, target(i)) for i in range(size) if 0 <= target(i) < size]
    return [lax.ppermute(v, axis, pairs) for v in values]


def on_device(tokens, norm_gain, qkv_weight, out_weight, band_counts, halo_rows, window_mask):
    mask = window_mask[0, 0]
    ring = lax.axis_size("lon")
    assert mask.shape[1] == 5 and ring % 4 == 0 and ring >= 8
    local = tokens[0, 0]
    rows = local.shape[0]
    outs = norm_call(local, norm_gain, halo_rows)
    own, (whole, north_rows, south_rows) = outs[:PARTS], outs[PARTS:]

    same = permuted(own, "lon", lambda i: i ^ 2)
    across = permuted(own[1:], "lon", lambda i: (i + (-2 if (i // 2) % 2 == 0 else 2)) % ring)
    partner = permuted([whole], "lon", lambda i: i ^ 1)
    halos = [
        permuted([south_rows], "lat", lambda b: b + 1)[0],
        permuted([north_rows], "lat", lambda b: b - 1)[0],
    ]
    lon = lax.axis_index("lon")
    gives_same = lon % 2 == (lon // 2) % 2

    def swapped(mine, others):
        return permuted([jnp.where(gives_same, mine, others)], "lon", lambda i: i ^ 1)[0]

    stage = functools.partial(stage_call, rows // mask.shape[0], band_counts, mask)
    half = rows // PARTS
    query, state = stage(["own"], [own], [], qkv_weight, starts=[[0, half]])

    same[0], query, state = lax.optimization_barrier((same[0], query, state))
    across = permuted(same[:1], "lon", lambda i: (i + (4 if (i // 2) % 2 == 0 else -4)) % ring) + across
    state = stage(["partner"], [partner], halos, qkv_weight, query, state, starts=[[0]])

    across[0], state = lax.optimization_barrier((across[0], state))
    near = [swapped(same[0], across[0])]
    state = stage(["same", "across"], [same[:1], across[:1]], [], qkv_weight, query, state, starts=[[0], [0]])

    across[1], state = lax.optimization_barrier((across[1], state))
    near.append(swapped(same[1], across[1]))
    final = (local, out_weight, [*partner, *own, *same, *across, *near, *halos])
    result = stage(
        ["same", "across", "near"],
        [same[1:], across[1:], near],
        [],
        qkv_weight,
        query,
        state,
        final,
        starts=[[half], [half], [0, half]],
    )
    return result[None, None]


def solution(mesh):
    in_specs = (
        P("lat", "lon", None, None),
        P(),
        P(),
        P(),
        P("lat"),
        P(),
        P("lat", "lon", None, None),
    )
    out_specs = P("lat", "lon", None, None)
    return jax.shard_map(
        on_device, mesh=mesh, in_specs=in_specs, out_specs=out_specs, check_vma=False
    )
```

time: 277 us -> 289 us (1.043)
  Pallas kernels: 255 us -> 267 us
    pallas_call x4, Pallas kernels: 252 us -> 264 us  [stage_call(): pl.pallas_call(functools.partial(stage_kernel, (first, last, sectors, sta...]
  transfers between devices with their start and end apart: 9 -> 9, of which waited for: 2 -> 2; matrix products, arithmetic and copies ran while one was open for 0% -> 0% of each run, Pallas kernels for 14% -> 16%
where the time goes in v4:
time: 289 us; the launch traced here: 285 us
  Pallas kernels  267 us (92%)
  starting transfers between devices  12.2 us (4%)
    pallas_call x4, Pallas kernels, stage_call(): pl.pallas_call(functools.partial(stage_kernel, (first, last, sectors, sta...  264 us
    ppermute x9, starting transfers between devices, permuted(): return [lax.ppermute(v, axis, pairs) for v in values]  12.2 us
  transfers between devices with their start and end apart: 9, of which 2 were waited for; matrix products, arithmetic and copies ran while one was open for 0% of the time, Pallas kernels for 16%

profile of v4, /device:TPU:0, one launch (start us, length us, event | category | flops | bytes accessed | tf_op | source)
XLA Modules:
  0.0 285.5 jit_solution(9748622231300420506)
XLA Ops:
  0.0 3.4 %layer_norm.1 = (bf16[256,1024]{1,0:T(8,128)(2,1)}, bf16[256,1024]{1,0:T(8,128)(2,1)}, bf16[512,1024]{1,0:T(8,128)(2,1)}, bf16[128,1024]{1,0:T(8,128)(2,1)}, bf16[128,1024]{1,0:T(8,128)(2,1)}) custom-call(f32[512,1024]{1,0:T(8,128)} %bitcast.4, f32[1,1024]{1,0:T(1,128)} %bitcast.6, s32[4,2,128]{2,1,0:T(2,128)} %halo_rows_hbm.1), custom_call_target="tpu_custom_call" | custom-call | flops 5242880 | bytes 3145728 | tf_op jit(solution)/shard_map/layer_norm/pallas_call | solution.py:91
  3.4 0.5 collective-permute-start.4
  3.9 2.6 collective-permute-start.2
  6.5 3.5 %collective-permute-start.5 = (bf16[128,1024]{1,0:T(8,128)(2,1)}, bf16[128,1024]{1,0:T(8,128)(2,1)S(1)}, u32[]{:S(2)}, u32[]{:S(2)}) collective-permute-start(bf16[128,1024]{1,0:T(8,128)(2,1)} %get-tuple-element.25), channel_id=1, source_target_pairs={{0,8},{8,16},{16,24},{1,9},{9,17},{17,25},{2,10},{10,18},{18,26},{... | collective-permute-start | bytes 786440 | tf_op jit(solution)/shard_map/ppermute | solution.py:491
  10.0 1.3 collective-permute-start.6
  11.3 1.6 collective-permute-start.1
  13.5 14.7 %attend_own.1 = (bf16[8,512,128]{2,1,0:T(8,128)(2,1)}, f32[16,512,128]{2,1,0:T(8,128)}) custom-call(s32[1]{0:T(128)S(6)} %copy.8.refs_0_, s32[4,5]{1,0:T(4,128)} %bitcast.7, bf16[256,1024]{1,0:T(8,128)(2,1)} %get-tuple-element.20.refs_2_.refs_12_, bf16[256,1024]{1,0:T(8,128)(2,1)} %get-tuple-element.19.refs_3_.refs_13_, bf16[1024,3072]{1,0:T(8,128)(2,1)} %refs_6_.1), custom_call_target="tpu_custom_call" | custom-call | flops 7516192768 | bytes 11534336 | tf_op jit(solution)/shard_map/attend_own/pallas_call | solution.py:475
  28.2 0.0 collective-permute-done.2.refs_2_.refs_14_
  28.3 0.0 copy-start
  28.3 1.6 collective-permute-start
  29.8 0.0 collective-permute-done.5.refs_3_.refs_20_
  29.8 0.0 copy-start.8
  29.8 0.5 collective-permute-start.3
  30.3 0.0 collective-permute-done.6.refs_4_.refs_21_
  30.3 0.0 collective-permute-done.4.refs_2_.refs_11_
  30.3 0.2 copy-done.8
  30.6 0.0 copy-start.5
  30.6 1.0 copy-done.5
  31.5 16.8 %attend_partner.1.refs_6_ = f32[16,512,128]{2,1,0:T(8,128)} custom-call(s32[1]{0:T(128)S(6)} %copy.8.refs_0_, s32[4,5]{1,0:T(4,128)} %bitcast.8, bf16[512,1024]{1,0:T(8,128)(2,1)} %copy-done.5, bf16[128,1024]{1,0:T(8,128)(2,1)} %copy-done.8, bf16[128,1024]{1,0:T(8,128)(2,1)} %collective-permute-done.6.refs_4_.refs_21_, bf16[1024,3072]{1,0:T(8,128)(2,1)} %refs_6_.1, ...), custom_call_target="tpu_custom_call" | custom-call | flops 9663676416 | bytes 16252928 | tf_op jit(solution)/shard_map/attend_partner/pallas_call | solution.py:475
  48.4 0.0 copy-done
  48.4 0.0 collective-permute-done.3.refs_3_.refs_16_
  48.4 0.0 copy-start.4
  48.4 0.8 copy-done.4
  49.2 0.0 copy-start.1
  49.2 13.7 %attend_same_across.1.refs_8_ = f32[16,512,128]{2,1,0:T(8,128)} custom-call(s32[1]{0:T(128)S(6)} %copy.8.refs_0_, s32[4,5]{1,0:T(4,128)} %bitcast.9, bf16[256,1024]{1,0:T(8,128)(2,1)} %copy-done, bf16[256,1024]{1,0:T(8,128)(2,1)} %copy-done.4, bf16[1024,3072]{1,0:T(8,128)(2,1)} %refs_6_.1, bf16[8,512,128]{2,1,0:T(8,128)(2,1)} %get-tuple-element.27.refs_6_.refs_5_.refs_7_, ...), custom_call_target="tpu_custom_call" | custom-call | flops 6442450944 | bytes 15728640 | tf_op jit(solution)/shard_map/attend_same_across/pallas_call | solution.py:475
  62.9 0.0 collective-permute-done.1.refs_3_.refs_17_
  62.9 0.0 copy-done.1
  62.9 0.0 copy-start.2
  62.9 0.1 broadcast_select_fusion.1
  63.0 0.0 collective-permute-done.refs_2_.refs_15_
  63.0 0.0 copy-start.3
  63.0 0.1 broadcast_select_fusion
  63.1 0.6 collective-permute-start.8
  63.7 0.1 collective-permute-start.7
  63.8 1.5 collective-permute-done.8.refs_5_.refs_19_
  65.2 0.0 copy-start.6
  65.2 0.7 collective-permute-done.7.refs_4_.refs_18_
  66.0 0.0 copy-done.2
  66.0 0.0 copy-done.3
  66.0 0.1 copy-done.6
  66.1 0.0 copy-start.7
  66.1 0.8 copy-done.7
  66.9 218.4 %attend_same_across_near.1 = f32[512,1024]{1,0:T(8,128)} custom-call(s32[1]{0:T(128)S(6)} %copy.8.refs_0_, s32[4,5]{1,0:T(4,128)} %bitcast.10, bf16[256,1024]{1,0:T(8,128)(2,1)} %copy-done.3, bf16[256,1024]{1,0:T(8,128)(2,1)} %copy-done.2, bf16[256,1024]{1,0:T(8,128)(2,1)} %copy-done.7, bf16[256,1024]{1,0:T(8,128)(2,1)} %copy-done.6, ...), custom_call_target="tpu_custom_call" | custom-call | flops 13958643712 | bytes 16777216 | tf_op jit(solution)/shard_map/attend_same_across_near/pallas_call | solution.py:475
Async XLA Ops:
  3.4 26.9 %collective-permute-start.4 = (bf16[512,1024]{1,0:T(8,128)(2,1)}, bf16[512,1024]{1,0:T(8,128)(2,1)S(1)}, u32[]{:S(2)}, u32[]{:S(2)}) collective-permute-start(bf16[512,1024]{1,0:T(8,128)(2,1)} %get-tuple-element.24), channel_id=1, source_target_pairs={{0,1},{1,0},{2,3},{3,2},{4,5},{5,4},{6,7},{7,6},{8,9},{9,8},{10,11... | collective-permute-start | bytes 3145736 | tf_op jit(solution)/shard_map/ppermute | solution.py:491
  3.9 24.3 %collective-permute-start.2 = (bf16[256,1024]{1,0:T(8,128)(2,1)}, bf16[256,1024]{1,0:T(8,128)(2,1)S(1)}, u32[]{:S(2)}, u32[]{:S(2)}) collective-permute-start(bf16[256,1024]{1,0:T(8,128)(2,1)} %get-tuple-element.20.refs_2_.refs_12_), channel_id=1, source_target_pairs={{0,2},{1,3},{2,0},{3,1},{4,6},{5,7},{6,4},{7,5},{8,10},{9,11},{10,... | collective-permute-start | bytes 1572872 | tf_op jit(solution)/shard_map/ppermute | solution.py:491
  6.5 23.3 %collective-permute-start.5 = (bf16[128,1024]{1,0:T(8,128)(2,1)}, bf16[128,1024]{1,0:T(8,128)(2,1)S(1)}, u32[]{:S(2)}, u32[]{:S(2)}) collective-permute-start(bf16[128,1024]{1,0:T(8,128)(2,1)} %get-tuple-element.25), channel_id=1, source_target_pairs={{0,8},{8,16},{16,24},{1,9},{9,17},{17,25},{2,10},{10,18},{18,26},{... | collective-permute-start | bytes 786440 | tf_op jit(solution)/shard_map/ppermute | solution.py:491
  10.0 20.3 %collective-permute-start.6 = (bf16[128,1024]{1,0:T(8,128)(2,1)}, bf16[128,1024]{1,0:T(8,128)(2,1)}, u32[]{:S(2)}, u32[]{:S(2)}) collective-permute-start(bf16[128,1024]{1,0:T(8,128)(2,1)} %get-tuple-element.26), channel_id=1, source_target_pairs={{8,0},{16,8},{24,16},{9,1},{17,9},{25,17},{10,2},{18,10},{26,18},{... | collective-permute-start | bytes 786440 | tf_op jit(solution)/shard_map/ppermute | solution.py:491
  11.3 51.6 %collective-permute-start.1 = (bf16[256,1024]{1,0:T(8,128)(2,1)}, bf16[256,1024]{1,0:T(8,128)(2,1)S(1)}, u32[]{:S(2)}, u32[]{:S(2)}) collective-permute-start(bf16[256,1024]{1,0:T(8,128)(2,1)} %get-tuple-element.19.refs_3_.refs_13_), channel_id=1, source_target_pairs={{0,6},{1,7},{2,4},{3,5},{4,2},{5,3},{6,0},{7,1},{8,14},{9,15},{10,... | collective-permute-start | bytes 1572872 | tf_op jit(solution)/shard_map/ppermute | solution.py:491
  28.3 20.1 %copy-start = (bf16[256,1024]{1,0:T(8,128)(2,1)}, bf16[256,1024]{1,0:T(8,128)(2,1)S(1)}, u32[]{:S(2)}) copy-start(bf16[256,1024]{1,0:T(8,128)(2,1)S(1)} %collective-permute-done.2.refs_2_.refs_14_) | copy-start | bytes 1572868
  28.3 34.7 %collective-permute-start = (bf16[256,1024]{1,0:T(8,128)(2,1)}, bf16[256,1024]{1,0:T(8,128)(2,1)S(1)}, u32[]{:S(2)}, u32[]{:S(2)}) collective-permute-start(bf16[256,1024]{1,0:T(8,128)(2,1)} %get-tuple-element.19.refs_3_.refs_13_), channel_id=1, source_target_pairs={{0,2},{1,3},{2,0},{3,1},{4,6},{5,7},{6,4},{7,5},{8,10},{9,11},{10,... | collective-permute-start | bytes 1572872 | tf_op jit(solution)/shard_map/ppermute | solution.py:491
  29.8 0.7 copy-start.8
  29.8 18.6 %collective-permute-start.3 = (bf16[256,1024]{1,0:T(8,128)(2,1)S(1)}, bf16[256,1024]{1,0:T(8,128)(2,1)S(1)}, u32[]{:S(2)}, u32[]{:S(2)}) collective-permute-start(bf16[256,1024]{1,0:T(8,128)(2,1)S(1)} %collective-permute-done.2.refs_2_.refs_14_), channel_id=1, source_target_pairs={{0,4},{1,5},{2,6},{3,7},{4,0},{5,1},{6,2},{7,3},{8,12},{9,13},{10,... | collective-permute-start | bytes 1572872 | tf_op jit(solution)/shard_map/ppermute | solution.py:491
  30.6 1.0 copy-start.5
  48.4 0.8 copy-start.4
  49.2 13.7 %copy-start.1 = (bf16[256,1024]{1,0:T(8,128)(2,1)S(1)}, bf16[256,1024]{1,0:T(8,128)(2,1)}, u32[]{:S(2)}) copy-start(bf16[256,1024]{1,0:T(8,128)(2,1)} %copy-done) | copy-start | bytes 1572868
  62.9 3.1 %copy-start.2 = (bf16[256,1024]{1,0:T(8,128)(2,1)}, bf16[256,1024]{1,0:T(8,128)(2,1)S(1)}, u32[]{:S(2)}) copy-start(bf16[256,1024]{1,0:T(8,128)(2,1)S(1)} %collective-permute-done.1.refs_3_.refs_17_) | copy-start | bytes 1572868
  63.0 3.0 %copy-start.3 = (bf16[256,1024]{1,0:T(8,128)(2,1)}, bf16[256,1024]{1,0:T(8,128)(2,1)S(1)}, u32[]{:S(2)}) copy-start(bf16[256,1024]{1,0:T(8,128)(2,1)S(1)} %collective-permute-done.refs_2_.refs_15_) | copy-start | bytes 1572868
  63.1 2.1 collective-permute-start.8
  63.7 2.3 collective-permute-start.7
  65.2 0.8 copy-start.6
  66.1 0.8 copy-start.7

commit v5 on v3

--- a/solution.py
+++ b/solution.py
@@ -212,7 +212,8 @@
         if first:
             query_out = take(1)[0]
         acc_out, sum_out = take(2)
-    key_ref, value_ref, ones_ref, score_ref, weight_ref = take(5)
+    key_ref, value_ref, ones_ref = take(3)
+    score_refs, weight_refs = take(2), take(2)
     if last:
         res_ref, att_ref, acc_out, sum_out = take(4)
 
@@ -229,10 +230,6 @@
     else:
         query = query_in[...]
     rows, width = query.shape
-    scaled = query.astype(jnp.float32) * (LOG2E * head_size**-0.5)
-    query_hi = scaled.astype(jnp.bfloat16)
-    query_lo = (scaled - query_hi.astype(jnp.float32)).astype(jnp.bfloat16)
-
     zero = jnp.zeros((), jnp.bfloat16)
     one = jnp.ones((), jnp.bfloat16)
     biases, spans = [], []
@@ -253,7 +250,7 @@
                 ones_ref[here] = jnp.where(live[:, :LANES], 1.0, 0.0).astype(jnp.bfloat16)
             at += size
         spans.append((begin, at))
-        biases.append(block_bias(mask_ref, columns[name], rows, jnp.bfloat16))
+        biases.append(None if name == "own" else block_bias(mask_ref, columns[name], rows, jnp.bfloat16))
     if halo_refs:
         begin = at
         for ref, seen in zip(halo_refs, (lat > 0, lat < bands - 1)):
@@ -277,22 +274,21 @@
     def score(unit):
         lanes, odd = lanes_of(unit), unit % 2
         half = ~low if odd else low
-        lo = jnp.where(half, query_lo[:, lanes], zero)
-        key = key_ref[lanes, :]
-        right = jnp.concatenate([jnp.where(~low_key if odd else low_key, key, one), key], axis=0)
+        right = jnp.where(~low_key if odd else low_key, key_ref[lanes, :], one)
         for (begin, end), bias in zip(spans, biases):
-            left = jnp.where(half, query_hi[:, lanes], zero if bias is None else bias)
-            score_ref[odd, :, begin:end] = matmul(jnp.concatenate([left, lo], axis=1), right[:, begin:end])
+            left = jnp.where(half, query[:, lanes], zero if bias is None else bias)
+            score_refs[odd][:, begin:end] = matmul(left, right[:, begin:end])
 
     def weigh(unit):
-        weight_ref[unit % 2] = jnp.exp2(score_ref[unit % 2]).astype(jnp.bfloat16)
+        scores = score_refs[unit % 2][...] * (LOG2E * head_size**-0.5)
+        weight_refs[unit % 2][...] = jnp.exp2(scores).astype(jnp.bfloat16)
 
     halves = {}
 
     def gather(unit):
         lanes, odd = lanes_of(unit), unit % 2
         values = jnp.where(~low_value if odd else low_value, value_ref[:, lanes], ones_ref[...])
-        halves[odd] = matmul(weight_ref[odd], values)
+        halves[odd] = matmul(weight_refs[odd][...], values)
         if not odd:
             return
         acc, total = jnp.where(low, halves[0], halves[1]), jnp.where(low, halves[1], halves[0])
@@ -381,8 +377,10 @@
         pltpu.VMEM((GROUP, keys), jnp.bfloat16),
         pltpu.VMEM((keys, GROUP), jnp.bfloat16),
         pltpu.VMEM((keys, LANES), jnp.bfloat16),
-        pltpu.VMEM((2, rows, keys), jnp.float32),
-        pltpu.VMEM((2, rows, keys), jnp.bfloat16),
+        pltpu.VMEM((rows, keys), jnp.float32),
+        pltpu.VMEM((rows, keys), jnp.float32),
+        pltpu.VMEM((rows, keys), jnp.bfloat16),
+        pltpu.VMEM((rows, keys), jnp.bfloat16),
     ]
     wide = jax.ShapeDtypeStruct((rows, width), jnp.float32)
     moved = sum(a.size * a.dtype.itemsize for a in args[2:] if a is not qkv_weight) + 3 * model * width * 2

time: 277 us -> 276 us (level)
  no operation moved by 1% of the time
where the time goes in v5:
time: 276 us; the launch traced here: 273 us
  Pallas kernels  255 us (92%)
  starting transfers between devices  12.2 us (4%)
  local copies, waits for them, and re-layouts  2.89 us (1%)
    pallas_call x4, Pallas kernels, stage_call(): pl.pallas_call(functools.partial(stage_kernel, (first, last, sectors, sta...  252 us
    ppermute x9, starting transfers between devices, permuted(): return [lax.ppermute(v, axis, pairs) for v in values]  12.2 us
  transfers between devices with their start and end apart: 9, of which 2 were waited for; matrix products, arithmetic and copies ran while one was open for 0% of the time, Pallas kernels for 14%

profile of v5, /device:TPU:0, one launch (start us, length us, event | category | flops | bytes accessed | tf_op | source)
XLA Modules:
  0.0 273.3 jit_solution(4082212587123620072)
XLA Ops:
  0.0 3.4 %layer_norm.1 = (bf16[256,1024]{1,0:T(8,128)(2,1)}, bf16[256,1024]{1,0:T(8,128)(2,1)}, bf16[512,1024]{1,0:T(8,128)(2,1)}, bf16[128,1024]{1,0:T(8,128)(2,1)}, bf16[128,1024]{1,0:T(8,128)(2,1)}) custom-call(f32[512,1024]{1,0:T(8,128)} %bitcast.4, f32[1,1024]{1,0:T(1,128)} %bitcast.6, s32[4,2,128]{2,1,0:T(2,128)} %halo_rows_hbm.1), custom_call_target="tpu_custom_call" | custom-call | flops 5242880 | bytes 3145728 | tf_op jit(solution)/shard_map/layer_norm/pallas_call | solution.py:91
  3.4 0.5 collective-permute-start.4
  3.9 2.6 collective-permute-start.2
  6.5 3.5 %collective-permute-start.5 = (bf16[128,1024]{1,0:T(8,128)(2,1)}, bf16[128,1024]{1,0:T(8,128)(2,1)S(1)}, u32[]{:S(2)}, u32[]{:S(2)}) collective-permute-start(bf16[128,1024]{1,0:T(8,128)(2,1)} %get-tuple-element.34), channel_id=1, source_target_pairs={{0,8},{8,16},{16,24},{1,9},{9,17},{17,25},{2,10},{10,18},{18,26},{... | collective-permute-start | bytes 786440 | tf_op jit(solution)/shard_map/ppermute | solution.py:440
  10.0 1.3 collective-permute-start.6
  11.3 1.6 collective-permute-start.1
  13.5 11.8 %attend_own.1 = (bf16[512,1024]{1,0:T(8,128)(2,1)}, f32[512,1024]{1,0:T(8,128)}, f32[512,1024]{1,0:T(8,128)}) custom-call(s32[1]{0:T(128)S(6)} %copy.8.refs_0_, s32[4,5]{1,0:T(4,128)} %bitcast.7, bf16[256,1024]{1,0:T(8,128)(2,1)} %get-tuple-element.28.refs_2_.refs_14_, bf16[256,1024]{1,0:T(8,128)(2,1)} %get-tuple-element.27.refs_3_.refs_15_, ...), custom_call_target="tpu_custom_call" | custom-call | flops 7516192768 | bytes 7340032 | tf_op jit(solution)/shard_map/attend_own/pallas_call | solution.py:419
  25.3 0.0 collective-permute-done.2.refs_2_.refs_16_
  25.3 0.0 copy-start
  25.3 1.6 collective-permute-start
  26.9 0.0 collective-permute-done.5.refs_3_.refs_22_
  26.9 0.0 copy-start.8
  26.9 0.5 collective-permute-start.3
  27.4 0.0 collective-permute-done.6.refs_4_.refs_23_
  27.4 0.0 collective-permute-done.4.refs_2_.refs_13_
  27.4 0.2 copy-done.8
  27.6 0.0 copy-start.5
  27.6 1.0 copy-done.5
  28.6 15.1 %attend_partner.1 = (f32[512,1024]{1,0:T(8,128)}, f32[512,1024]{1,0:T(8,128)}) custom-call(s32[1]{0:T(128)S(6)} %copy.8.refs_0_, s32[4,5]{1,0:T(4,128)} %bitcast.8, bf16[512,1024]{1,0:T(8,128)(2,1)} %copy-done.5, bf16[128,1024]{1,0:T(8,128)(2,1)} %copy-done.8, bf16[128,1024]{1,0:T(8,128)(2,1)} %collective-permute-done.6.refs_4_.refs_23_, ...), custom_call_target="tpu_custom_call" | custom-call | flops 9663676416 | bytes 13107200 | tf_op jit(solution)/shard_map/attend_partner/pallas_call | solution.py:419
  43.7 0.0 copy-done
  43.7 0.0 collective-permute-done.3.refs_3_.refs_18_
  43.7 0.0 copy-start.4
  43.7 0.8 copy-done.4
  44.5 0.0 copy-start.1
  44.5 11.0 %attend_same_across.1 = (f32[512,1024]{1,0:T(8,128)}, f32[512,1024]{1,0:T(8,128)}) custom-call(s32[1]{0:T(128)S(6)} %copy.8.refs_0_, s32[4,5]{1,0:T(4,128)} %bitcast.9, bf16[256,1024]{1,0:T(8,128)(2,1)} %copy-done, bf16[256,1024]{1,0:T(8,128)(2,1)} %copy-done.4, bf16[1024,3072]{1,0:T(8,128)(2,1)} %refs_7_.1, bf16[1024,3072]{1,0:T(8,128)(2,1)} %refs_7_.1, ...), custom_call_target="tpu_custom_call" | custom-call | flops 6442450944 | bytes 12582912 | tf_op jit(solution)/shard_map/attend_same_across/pallas_call | solution.py:419
  55.6 0.0 collective-permute-done.1.refs_3_.refs_19_
  55.6 0.0 copy-start.2
  55.6 0.0 copy-done.1
  55.6 0.1 broadcast_select_fusion.1
  55.7 0.0 collective-permute-done.refs_2_.refs_17_
  55.7 0.0 copy-start.3
  55.7 0.1 broadcast_select_fusion
  55.8 0.6 collective-permute-start.8
  56.4 0.1 collective-permute-start.7
  56.4 1.5 collective-permute-done.8.refs_5_.refs_21_
  57.9 0.0 copy-start.6
  57.9 0.7 collective-permute-done.7.refs_4_.refs_20_
  58.7 0.0 copy-done.2
  58.7 0.0 copy-done.3
  58.7 0.1 copy-done.6
  58.7 0.0 copy-start.7
  58.7 0.8 copy-done.7
  59.5 213.6 %attend_same_across_near.1 = f32[512,1024]{1,0:T(8,128)} custom-call(s32[1]{0:T(128)S(6)} %copy.8.refs_0_, s32[4,5]{1,0:T(4,128)} %bitcast.10, bf16[256,1024]{1,0:T(8,128)(2,1)} %copy-done.3, bf16[256,1024]{1,0:T(8,128)(2,1)} %copy-done.2, bf16[256,1024]{1,0:T(8,128)(2,1)} %copy-done.7, bf16[256,1024]{1,0:T(8,128)(2,1)} %copy-done.6, ...), custom_call_target="tpu_custom_call" | custom-call | flops 13958643712 | bytes 13631488 | tf_op jit(solution)/shard_map/attend_same_across_near/pallas_call | solution.py:419
Async XLA Ops:
  3.4 24.0 %collective-permute-start.4 = (bf16[512,1024]{1,0:T(8,128)(2,1)}, bf16[512,1024]{1,0:T(8,128)(2,1)S(1)}, u32[]{:S(2)}, u32[]{:S(2)}) collective-permute-start(bf16[512,1024]{1,0:T(8,128)(2,1)} %get-tuple-element.33), channel_id=1, source_target_pairs={{0,1},{1,0},{2,3},{3,2},{4,5},{5,4},{6,7},{7,6},{8,9},{9,8},{10,11... | collective-permute-start | bytes 3145736 | tf_op jit(solution)/shard_map/ppermute | solution.py:440
  3.9 21.4 %collective-permute-start.2 = (bf16[256,1024]{1,0:T(8,128)(2,1)}, bf16[256,1024]{1,0:T(8,128)(2,1)S(1)}, u32[]{:S(2)}, u32[]{:S(2)}) collective-permute-start(bf16[256,1024]{1,0:T(8,128)(2,1)} %get-tuple-element.28.refs_2_.refs_14_), channel_id=1, source_target_pairs={{0,2},{1,3},{2,0},{3,1},{4,6},{5,7},{6,4},{7,5},{8,10},{9,11},{10,... | collective-permute-start | bytes 1572872 | tf_op jit(solution)/shard_map/ppermute | solution.py:440
  6.5 20.4 %collective-permute-start.5 = (bf16[128,1024]{1,0:T(8,128)(2,1)}, bf16[128,1024]{1,0:T(8,128)(2,1)S(1)}, u32[]{:S(2)}, u32[]{:S(2)}) collective-permute-start(bf16[128,1024]{1,0:T(8,128)(2,1)} %get-tuple-element.34), channel_id=1, source_target_pairs={{0,8},{8,16},{16,24},{1,9},{9,17},{17,25},{2,10},{10,18},{18,26},{... | collective-permute-start | bytes 786440 | tf_op jit(solution)/shard_map/ppermute | solution.py:440
  10.0 17.4 %collective-permute-start.6 = (bf16[128,1024]{1,0:T(8,128)(2,1)}, bf16[128,1024]{1,0:T(8,128)(2,1)}, u32[]{:S(2)}, u32[]{:S(2)}) collective-permute-start(bf16[128,1024]{1,0:T(8,128)(2,1)} %get-tuple-element.35), channel_id=1, source_target_pairs={{8,0},{16,8},{24,16},{9,1},{17,9},{25,17},{10,2},{18,10},{26,18},{... | collective-permute-start | bytes 786440 | tf_op jit(solution)/shard_map/ppermute | solution.py:440
  11.3 44.3 %collective-permute-start.1 = (bf16[256,1024]{1,0:T(8,128)(2,1)}, bf16[256,1024]{1,0:T(8,128)(2,1)S(1)}, u32[]{:S(2)}, u32[]{:S(2)}) collective-permute-start(bf16[256,1024]{1,0:T(8,128)(2,1)} %get-tuple-element.27.refs_3_.refs_15_), channel_id=1, source_target_pairs={{0,6},{1,7},{2,4},{3,5},{4,2},{5,3},{6,0},{7,1},{8,14},{9,15},{10,... | collective-permute-start | bytes 1572872 | tf_op jit(solution)/shard_map/ppermute | solution.py:440
  25.3 18.4 %copy-start = (bf16[256,1024]{1,0:T(8,128)(2,1)}, bf16[256,1024]{1,0:T(8,128)(2,1)S(1)}, u32[]{:S(2)}) copy-start(bf16[256,1024]{1,0:T(8,128)(2,1)S(1)} %collective-permute-done.2.refs_2_.refs_16_) | copy-start | bytes 1572868
  25.3 30.4 %collective-permute-start = (bf16[256,1024]{1,0:T(8,128)(2,1)}, bf16[256,1024]{1,0:T(8,128)(2,1)S(1)}, u32[]{:S(2)}, u32[]{:S(2)}) collective-permute-start(bf16[256,1024]{1,0:T(8,128)(2,1)} %get-tuple-element.27.refs_3_.refs_15_), channel_id=1, source_target_pairs={{0,2},{1,3},{2,0},{3,1},{4,6},{5,7},{6,4},{7,5},{8,10},{9,11},{10,... | collective-permute-start | bytes 1572872 | tf_op jit(solution)/shard_map/ppermute | solution.py:440
  26.9 0.7 copy-start.8
  26.9 16.8 %collective-permute-start.3 = (bf16[256,1024]{1,0:T(8,128)(2,1)S(1)}, bf16[256,1024]{1,0:T(8,128)(2,1)S(1)}, u32[]{:S(2)}, u32[]{:S(2)}) collective-permute-start(bf16[256,1024]{1,0:T(8,128)(2,1)S(1)} %collective-permute-done.2.refs_2_.refs_16_), channel_id=1, source_target_pairs={{0,4},{1,5},{2,6},{3,7},{4,0},{5,1},{6,2},{7,3},{8,12},{9,13},{10,... | collective-permute-start | bytes 1572872 | tf_op jit(solution)/shard_map/ppermute | solution.py:440
  27.6 1.0 copy-start.5
  43.7 0.8 copy-start.4
  44.5 11.1 %copy-start.1 = (bf16[256,1024]{1,0:T(8,128)(2,1)S(1)}, bf16[256,1024]{1,0:T(8,128)(2,1)}, u32[]{:S(2)}) copy-start(bf16[256,1024]{1,0:T(8,128)(2,1)} %copy-done) | copy-start | bytes 1572868
  55.6 3.1 %copy-start.2 = (bf16[256,1024]{1,0:T(8,128)(2,1)}, bf16[256,1024]{1,0:T(8,128)(2,1)S(1)}, u32[]{:S(2)}) copy-start(bf16[256,1024]{1,0:T(8,128)(2,1)S(1)} %collective-permute-done.1.refs_3_.refs_19_) | copy-start | bytes 1572868
  55.7 3.0 %copy-start.3 = (bf16[256,1024]{1,0:T(8,128)(2,1)}, bf16[256,1024]{1,0:T(8,128)(2,1)S(1)}, u32[]{:S(2)}) copy-start(bf16[256,1024]{1,0:T(8,128)(2,1)S(1)} %collective-permute-done.refs_2_.refs_17_) | copy-start | bytes 1572868
  55.8 2.1 collective-permute-start.8
  56.4 2.3 collective-permute-start.7
  57.9 0.8 copy-start.6
  58.7 0.8 copy-start.7

commit v6 on v4

--- a/solution.py
+++ b/solution.py
@@ -16,7 +16,8 @@
 FLOOR = -1e25
 LOG2E = math.log2(math.e)
 SUM_MIN, SUM_MAX = 2.0**-60, 2.0**100
-VMEM_LIMIT = 60 * 1024 * 1024
+NORM_VMEM = 60 * 1024 * 1024
+STAGE_VMEM = 32 * 1024 * 1024
 CHUNKS = 4
 
 epsilon = 1e-05
@@ -102,7 +103,7 @@
             pltpu.SemaphoreType.DMA((CHUNKS + 2,)),
             pltpu.SemaphoreType.DMA((PARTS + 3,)),
         ],
-        compiler_params=pltpu.CompilerParams(vmem_limit_bytes=VMEM_LIMIT),
+        compiler_params=pltpu.CompilerParams(vmem_limit_bytes=NORM_VMEM),
         cost_estimate=pl.CostEstimate(flops=10 * rows * width, bytes_accessed=6 * rows * width, transcendentals=0),
         name="layer_norm",
     )(tokens, gain.reshape(1, width), halo_rows)
@@ -125,11 +126,9 @@
     return jnp.concatenate([jnp.full((rows // blocks, LANES), v, jnp.float32) for v in values], axis=0).astype(dtype)
 
 
-def safe_attention(query_ref, weights, sources, counts_ref, mask_ref, att_ref, scratch, head_size):
-    rows_ref, key_ref, value_ref, top_ref, sum_ref, acc_ref, flag_ref, limit_ref, sem = scratch
+def safe_attention(query_ref, weight, groups, sources, counts_ref, mask_ref, att_ref, scratch, head_size):
+    key_ref, value_ref, top_ref, sum_ref, acc_ref, flag_ref, limit_ref = scratch
     pairs, rows, _ = query_ref.shape
-    wk_ref, wv_ref = weights
-    groups = wk_ref.shape[0]
     tile = sources[0][0].shape[0]
     blocks = mask_ref.shape[0]
     low = lax.broadcasted_iota(jnp.int32, (rows, LANES), 1) < head_size
@@ -137,11 +136,8 @@
     def group_body(g, carry):
         for t, (ref, column, seen, start) in enumerate(sources):
             size = ref.shape[0]
-            copy = pltpu.make_async_copy(ref, rows_ref.at[pl.ds(0, size)], sem)
-            copy.start()
-            copy.wait()
-            key_ref[pl.ds(t * tile, size)] = matmul(rows_ref[pl.ds(0, size)], wk_ref[g]).astype(jnp.bfloat16)
-            value_ref[pl.ds(t * tile, size)] = matmul(rows_ref[pl.ds(0, size)], wv_ref[g]).astype(jnp.bfloat16)
+            key_ref[pl.ds(t * tile, size)] = matmul(ref[...], weight(1, g)).astype(jnp.bfloat16)
+            value_ref[pl.ds(t * tile, size)] = matmul(ref[...], weight(2, g)).astype(jnp.bfloat16)
             if size < tile:
                 rest = pl.ds(t * tile + size, tile - size)
                 key_ref[rest] = jnp.zeros((tile - size, key_ref.shape[1]), jnp.bfloat16)
@@ -204,56 +200,41 @@
     counts_ref, mask_ref = take(2)
     sector_refs = [take(len(starts)) for starts in part_starts]
     halo_refs = take(2) if halos else []
-    (qkv_hbm,) = take(1)
+    (qkv_ref,) = take(1)
     if not first:
-        query_hbm, sums_hbm = take(2)
+        query_ref, sums_in = take(2)
     if last:
         tokens_hbm, wo_hbm = take(2)
         all_refs = take(1 + 4 * PARTS + 2)
         (out_hbm,) = take(1)
     else:
         if first:
-            (query_out,) = take(1)
-        (sums_out,) = take(1)
-    rows_ref, weight_ref, key_ref, value_ref, ones_ref, query_ref, sums_ref = take(7)
+            (query_ref,) = take(1)
+        (sums_ref,) = take(1)
+    key_ref, value_ref, ones_ref = take(3)
     score_refs, exp_refs = take(2), take(2)
-    rows_sem, weight_sem, in_sem, out_sem = take(4)
     if last:
-        att_ref, tokens_ref, wo_ref, fine_ref = take(4)
+        sums_ref, att_ref, tokens_ref, wo_ref, fine_ref, in_sem, out_sem = take(7)
 
     pairs, rows, _ = query_ref.shape
-    groups, model, group = weight_ref.shape[1:]
-    each = pairs // groups
+    group = GROUP
+    each = group // LANES
+    groups = pairs // each
     reach = mask_ref.shape[1] // 2
     lon, lat = lax.axis_index("lon"), lax.axis_index("lat")
     bands = lax.axis_size("lat")
     columns = sector_columns(lon, reach)
     count = counts_ref[0]
-    thirds = range(0 if first else 1, 3)
-
-    row_copies = []
-    at = 0
-    for ref in [r for parts in sector_refs for r in parts] + halo_refs:
-        here = rows_ref.at[pl.ds(at, ref.shape[0])]
-        row_copies.append(pltpu.make_async_copy(ref, here, rows_sem.at[len(row_copies)]))
-        at += ref.shape[0]
-    keys = at
-
-    def weight_copy(third, g):
-        start = third * groups * group + g * group
-        if not isinstance(start, int):
-            start = pl.multiple_of(start, group)
-        t = third - thirds[0]
-        return pltpu.make_async_copy(qkv_hbm.at[:, pl.ds(start, group)], weight_ref.at[t, g], weight_sem.at[t, g])
+    keys = ones_ref.shape[0]
+
+    def weight(third, g):
+        return qkv_ref[:, pl.ds(pl.multiple_of(third * groups * group + g * group, group), group)]
 
     later = []
-    if not first:
-        later.append(pltpu.make_async_copy(query_hbm, query_ref, in_sem.at[0]))
-        later.append(pltpu.make_async_copy(sums_hbm, sums_ref, in_sem.at[1]))
     if last:
-        later.append(pltpu.make_async_copy(tokens_hbm, tokens_ref, in_sem.at[2]))
-        later.append(pltpu.make_async_copy(wo_hbm, wo_ref, in_sem.at[3]))
-    for copy in row_copies + [weight_copy(t, g) for g in range(groups) for t in thirds] + later:
+        later.append(pltpu.make_async_copy(tokens_hbm, tokens_ref, in_sem.at[0]))
+        later.append(pltpu.make_async_copy(wo_hbm, wo_ref, in_sem.at[1]))
+    for copy in later:
         copy.start()
 
     biases, spans, pieces = [], [], []
@@ -268,7 +249,7 @@
                 else:
                     slot = start + r + lax.broadcasted_iota(jnp.int32, (size, group), 0)
                     live = jnp.where(slot < count, 1.0, 0.0)
-                pieces.append((at, size, live))
+                pieces.append((ref, r, at, size, live))
                 at += size
         spans.append((begin, at))
         biases.append(None if name == "own" else block_bias(mask_ref, columns[name], rows, jnp.bfloat16))
@@ -276,28 +257,24 @@
         begin = at
         for ref, seen in zip(halo_refs, (lat > 0, lat < bands - 1)):
             size = ref.shape[0]
-            pieces.append((at, size, jnp.full((size, group), jnp.where(seen, 1.0, 0.0), jnp.float32)))
+            pieces.append((ref, 0, at, size, jnp.full((size, group), jnp.where(seen, 1.0, 0.0), jnp.float32)))
             at += size
         spans.append((begin, at))
         biases.append(None)
-    for begin, size, live in pieces:
+    for _, _, begin, size, live in pieces:
         ones = jnp.ones((size, LANES), jnp.float32) if live is None else live[:, :LANES]
         ones_ref[pl.ds(begin, size)] = ones.astype(jnp.bfloat16)
-    for copy in row_copies:
-        copy.wait()
 
     def project(g, carry):
-        for t in thirds:
-            weight_copy(t, g).wait()
-        for begin, size, live in pieces:
+        for ref, r, begin, size, live in pieces:
             here = pl.ds(begin, size)
-            normed = rows_ref[here]
+            normed = ref[pl.ds(r, size)]
             if first:
-                query = matmul(normed, weight_ref[0, g]).astype(jnp.bfloat16)
+                query = matmul(normed, weight(0, g)).astype(jnp.bfloat16)
                 for p in range(each):
                     query_ref[g * each + p, here] = query[:, p * LANES : (p + 1) * LANES]
-            key = matmul(normed, weight_ref[1 - thirds[0], g]).astype(jnp.bfloat16).T
-            value = matmul(normed, weight_ref[2 - thirds[0], g])
+            key = matmul(normed, weight(1, g)).astype(jnp.bfloat16).T
+            value = matmul(normed, weight(2, g))
             if live is not None:
                 value = jnp.where(live > 0, value, 0.0)
             value = value.astype(jnp.bfloat16)
@@ -308,12 +285,6 @@
         return carry
 
     lax.fori_loop(0, groups, project, 0)
-    if first:
-        sent = pltpu.make_async_copy(query_ref, query_out, in_sem.at[0])
-        sent.start()
-    else:
-        for copy in later[:2]:
-            copy.wait()
 
     zero = jnp.zeros((), jnp.bfloat16)
     one = jnp.ones((), jnp.bfloat16)
@@ -336,13 +307,11 @@
         values = jnp.where(~low_value if odd else low_value, value_ref[pair], ones_ref[...])
         result = matmul(exp_refs[odd][...], values)
         if not first:
-            result = result + sums_ref[2 * pair + odd]
+            result = result + sums_in[2 * pair + odd]
         sums_ref[2 * pair + odd] = result
 
     def finish(pair):
         if not last:
-            at = pl.ds(2 * pair, 2)
-            pltpu.make_async_copy(sums_ref.at[at], sums_out.at[at], out_sem.at[pair]).start()
             return
         even, odd = sums_ref[2 * pair], sums_ref[2 * pair + 1]
         total = jnp.where(low, odd, even)
@@ -373,15 +342,6 @@
     finish(pairs - 1)
 
     if not last:
-        if first:
-            sent.wait()
-
-        def arrived(pair, carry):
-            at = pl.ds(2 * pair, 2)
-            pltpu.make_async_copy(sums_ref.at[at], sums_out.at[at], out_sem.at[pair]).wait()
-            return carry
-
-        lax.fori_loop(0, pairs, arrived, 0)
         return
 
     @pl.when(jnp.min(fine_ref[...]) < 0.5)
@@ -395,10 +355,9 @@
                 sources.append((ref, columns[name], None, i * part))
         for ref, seen in zip(all_refs[1 + 4 * PARTS :], (lat > 0, lat < bands - 1)):
             sources.append((ref, None, seen, 0))
-        weights = (weight_ref.at[0], weight_ref.at[1])
-        safe_attention(query_ref, weights, sources, counts_ref, mask_ref, att_ref, refs, head_size)
-
-    for copy in later[2:]:
+        safe_attention(query_ref, weight, groups, sources, counts_ref, mask_ref, att_ref, refs, head_size)
+
+    for copy in later:
         copy.wait()
     attended = jnp.concatenate([att_ref[p] for p in range(pairs)], axis=1)
     live = lax.broadcasted_iota(jnp.int32, (rows, group), 0) < count
@@ -419,45 +378,43 @@
     head_size = width // HEADS
     rows = mask.shape[0] * block_rows
     pairs, groups = width // LANES, width // GROUP
-    thirds = 3 if first else 2
     smem = pl.BlockSpec(memory_space=pltpu.SMEM)
-    hbm = pl.BlockSpec(memory_space=pl.ANY)
+    hbm = pl.BlockSpec(memory_space=pltpu.HBM)
+    vmem = pl.BlockSpec(memory_space=pltpu.VMEM)
     sources = [p for parts in sector_parts for p in parts] + halos
     keys = sum(p.shape[0] for p in sources)
     args = [counts, mask, *sources, qkv_weight]
     if not first:
         args += [query, sums]
+    specs = [smem, smem] + [vmem] * (len(args) - 2)
     query_shape = jax.ShapeDtypeStruct((pairs, rows, LANES), jnp.bfloat16)
     sums_shape = jax.ShapeDtypeStruct((2 * pairs, rows, LANES), jnp.float32)
     scratch = [
-        pltpu.VMEM((keys, model), jnp.bfloat16),
-        pltpu.VMEM((thirds, groups, model, GROUP), jnp.bfloat16),
         pltpu.VMEM((pairs, LANES, keys), jnp.bfloat16),
         pltpu.VMEM((pairs, keys, LANES), jnp.bfloat16),
         pltpu.VMEM((keys, LANES), jnp.bfloat16),
-        pltpu.VMEM(query_shape.shape, jnp.bfloat16),
-        pltpu.VMEM(sums_shape.shape, jnp.float32),
         pltpu.VMEM((rows, keys), jnp.float32),
         pltpu.VMEM((rows, keys), jnp.float32),
         pltpu.VMEM((rows, keys), jnp.bfloat16),
         pltpu.VMEM((rows, keys), jnp.bfloat16),
-        pltpu.SemaphoreType.DMA((len(sources),)),
-        pltpu.SemaphoreType.DMA((thirds, groups)),
-        pltpu.SemaphoreType.DMA((4,)),
-        pltpu.SemaphoreType.DMA((pairs,)),
     ]
+    out_specs = [vmem]
     if last:
         tokens, out_weight, everything = final
         args += [tokens, out_weight, *everything]
+        specs += [hbm, hbm] + [vmem] * len(everything)
         out_shape = [jax.ShapeDtypeStruct((rows, width), jnp.float32)]
+        out_specs = [hbm]
         part = rows // PARTS
         tiles = len(everything) + PARTS - 1
         scratch += [
+            pltpu.VMEM(sums_shape.shape, jnp.float32),
             pltpu.VMEM((pairs, rows, LANES), jnp.bfloat16),
             pltpu.VMEM(tokens.shape, jnp.float32),
             pltpu.VMEM(out_weight.shape, jnp.bfloat16),
             pltpu.VMEM((rows, LANES), jnp.float32),
-            pltpu.VMEM((part, model), jnp.bfloat16),
+            pltpu.SemaphoreType.DMA((2,)),
+            pltpu.SemaphoreType.DMA((groups,)),
             pltpu.VMEM((part * tiles, GROUP), jnp.bfloat16),
             pltpu.VMEM((part * tiles, GROUP), jnp.bfloat16),
             pltpu.VMEM((rows, LANES), jnp.float32),
@@ -465,20 +422,22 @@
             pltpu.VMEM((rows, LANES), jnp.float32),
             pltpu.SMEM((tiles, mask.shape[0]), jnp.int32),
             pltpu.SMEM((tiles,), jnp.int32),
-            pltpu.SemaphoreType.DMA,
         ]
+    elif first:
+        out_shape = [query_shape, sums_shape]
+        out_specs = [vmem, vmem]
     else:
-        out_shape = [query_shape, sums_shape] if first else [sums_shape]
+        out_shape = [sums_shape]
     flops = 2 * keys * model * 2 * width + 16 * rows * keys * width
     flops += 2 * rows * model * width * (int(first) + int(last))
-    moved = 2 * (thirds * model * width + keys * model) + 4 * rows * width * (2 if first else 5)
+    moved = 2 * (3 * model * width + keys * model) + 4 * rows * width
     outs = pl.pallas_call(
         functools.partial(stage_kernel, (first, last, sectors, starts, bool(halos), head_size)),
         out_shape=out_shape,
-        in_specs=[smem, smem] + [hbm] * (len(args) - 2),
-        out_specs=[hbm] * len(out_shape),
+        in_specs=specs,
+        out_specs=out_specs,
         scratch_shapes=scratch,
-        compiler_params=pltpu.CompilerParams(vmem_limit_bytes=VMEM_LIMIT),
+        compiler_params=pltpu.CompilerParams(vmem_limit_bytes=STAGE_VMEM),
         cost_estimate=pl.CostEstimate(flops=flops, bytes_accessed=moved, transcendentals=rows * keys * HEADS),
         name="attend_" + "_".join(sectors),
     )(*args)

time: 289 us -> 238 us (0.82)
  Pallas kernels: 267 us -> 203 us
  local copies, waits for them, and re-layouts: 2.88 us -> 19 us
    pallas_call x4, Pallas kernels: 264 us -> 199 us  [stage_call(): pl.pallas_call(functools.partial(stage_kernel, (first, last, sectors, sta...]
    unnamed x18 -> x34, local copies, waits for them, and re-layouts: 2.88 us -> 19 us
  transfers between devices with their start and end apart: 9 -> 9, of which waited for: 2 -> 2; matrix products, arithmetic and copies ran while one was open for 0% -> 0% of each run, Pallas kernels for 16% -> 14%
where the time goes in v6:
time: 238 us; the launch traced here: 237 us
  Pallas kernels  203 us (85%)
  local copies, waits for them, and re-layouts  19 us (8%)
  starting transfers between devices  12 us (5%)
    pallas_call x4, Pallas kernels, stage_call(): pl.pallas_call(functools.partial(stage_kernel, (first, last, sectors, sta...  199 us
    unnamed x34, local copies, waits for them, and re-layouts  19 us
    ppermute x9, starting transfers between devices, permuted(): return [lax.ppermute(v, axis, pairs) for v in values]  12 us
  transfers between devices with their start and end apart: 9, of which 2 were waited for; matrix products, arithmetic and copies ran while one was open for 0% of the time, Pallas kernels for 14%

profile of v6, /device:TPU:0, one launch (start us, length us, event | category | flops | bytes accessed | tf_op | source)
XLA Modules:
  0.0 237.1 jit_solution(9504691556110342011)
XLA Ops:
  0.0 3.4 %layer_norm.1 = (bf16[256,1024]{1,0:T(8,128)(2,1)}, bf16[256,1024]{1,0:T(8,128)(2,1)}, bf16[512,1024]{1,0:T(8,128)(2,1)}, bf16[128,1024]{1,0:T(8,128)(2,1)}, bf16[128,1024]{1,0:T(8,128)(2,1)}) custom-call(f32[512,1024]{1,0:T(8,128)} %bitcast.4, f32[1,1024]{1,0:T(1,128)} %bitcast.10, s32[4,2,128]{2,1,0:T(2,128)} %halo_rows_hbm.1), custom_call_target="tpu_custom_call" | custom-call | flops 5242880 | bytes 3145728 | tf_op jit(solution)/shard_map/layer_norm/pallas_call | solution.py:92
  3.4 0.5 collective-permute-start.4
  3.9 2.6 %collective-permute-start.2 = (bf16[256,1024]{1,0:T(8,128)(2,1)}, bf16[256,1024]{1,0:T(8,128)(2,1)S(1)}, u32[]{:S(2)}, u32[]{:S(2)}) collective-permute-start(bf16[256,1024]{1,0:T(8,128)(2,1)} %get-tuple-element.20.refs_2_.refs_12_), channel_id=1, source_target_pairs={{0,2},{1,3},{2,0},{3,1},{4,6},{5,7},{6,4},{7,5},{8,10},{9,11},{10,... | collective-permute-start | bytes 1572872 | tf_op jit(solution)/shard_map/ppermute | solution.py:450
  6.5 3.5 %collective-permute-start.5 = (bf16[128,1024]{1,0:T(8,128)(2,1)}, bf16[128,1024]{1,0:T(8,128)(2,1)S(1)}, u32[]{:S(2)}, u32[]{:S(2)}) collective-permute-start(bf16[128,1024]{1,0:T(8,128)(2,1)} %get-tuple-element.25), channel_id=1, source_target_pairs={{0,8},{8,16},{16,24},{1,9},{9,17},{17,25},{2,10},{10,18},{18,26},{... | collective-permute-start | bytes 786440 | tf_op jit(solution)/shard_map/ppermute | solution.py:450
  10.0 1.3 collective-permute-start.6
  11.3 1.6 collective-permute-start.1
  13.5 0.0 copy-start.1
  13.5 2.8 %copy-done.1 = bf16[1024,3072]{1,0:T(8,128)(2,1)S(1)} copy-done((bf16[1024,3072]{1,0:T(8,128)(2,1)S(1)}, bf16[1024,3072]{1,0:T(8,128)(2,1)}, u32[]{:S(2)}) %copy-start.1) | copy-done | bytes 6291480
  16.3 0.0 copy-start.5
  16.3 1.0 copy-done.5
  17.3 0.0 copy-start.7
  17.3 1.0 copy-done.7
  18.4 0.0 copy-start.9
  18.4 0.7 copy-done.9
  19.1 0.0 copy-start.8
  19.1 0.0 copy-start.10
  19.1 10.7 %attend_own.1 = (bf16[8,512,128]{2,1,0:T(8,128)(2,1)S(1)}, f32[16,512,128]{2,1,0:T(8,128)S(1)}) custom-call(s32[1]{0:T(128)S(6)} %copy.8.refs_0_, s32[4,5]{1,0:T(4,128)S(1)} %bitcast.6, bf16[256,1024]{1,0:T(8,128)(2,1)S(1)} %copy-done.5, bf16[256,1024]{1,0:T(8,128)(2,1)S(1)} %copy-done.7, bf16[1024,3072]{1,0:T(8,128)(2,1)S(1)} %copy-done.1), custom_call_target="tpu_custom_call" | custom-call | flops 7516192768 | bytes 9437184 | tf_op jit(solution)/shard_map/attend_own/pallas_call | solution.py:434
  29.8 0.0 copy-start.13
  29.8 1.0 copy-done.13
  30.8 0.0 copy-start.15
  30.8 1.9 copy-done.15
  32.8 0.0 collective-permute-done.2.refs_2_.refs_14_
  32.8 0.0 copy-done.8
  32.8 1.5 collective-permute-start
  34.3 0.0 collective-permute-done.5.refs_3_.refs_20_
  34.3 0.5 collective-permute-start.3
  34.8 0.0 collective-permute-done.6.refs_4_.refs_21_
  34.8 0.0 collective-permute-done.4.refs_2_.refs_11_
  34.8 0.0 copy-done.10
  34.8 0.0 copy-start.2
  34.8 2.8 %copy-done.2 = bf16[1024,3072]{1,0:T(8,128)(2,1)S(1)} copy-done((bf16[1024,3072]{1,0:T(8,128)(2,1)S(1)}, bf16[1024,3072]{1,0:T(8,128)(2,1)}, u32[]{:S(2)}) %copy-start.2) | copy-done | bytes 6291480
  37.6 0.0 copy-start.14
  37.6 1.2 copy-done.14
  38.8 0.0 copy-start.16
  38.8 2.2 copy-done.16
  41.0 13.1 %attend_partner.1.refs_6_ = f32[16,512,128]{2,1,0:T(8,128)S(1)} custom-call(s32[1]{0:T(128)S(6)} %copy.8.refs_0_, s32[4,5]{1,0:T(4,128)S(1)} %bitcast.7, bf16[512,1024]{1,0:T(8,128)(2,1)S(1)} %collective-permute-done.4.refs_2_.refs_11_, bf16[128,1024]{1,0:T(8,128)(2,1)S(1)} %collective-permute-done.5.refs_3_.refs_20_, ...), custom_call_target="tpu_custom_call" | custom-call | flops 9663676416 | bytes 9961472 | tf_op jit(solution)/shard_map/attend_partner/pallas_call | solution.py:434
  54.1 0.0 copy-start.11
  54.1 1.9 copy-done.11
  56.1 0.0 copy-start
  56.1 0.0 copy-start.3
  56.1 0.0 copy-start.4
  56.1 0.0 copy-start.6
  56.1 0.0 collective-permute-done.3.refs_3_.refs_16_
  56.1 0.0 copy-start.12
  56.1 2.3 copy-done.12
  58.4 9.7 %attend_same_across.1.refs_8_ = f32[16,512,128]{2,1,0:T(8,128)S(1)} custom-call(s32[1]{0:T(128)S(6)} %copy.8.refs_0_, s32[4,5]{1,0:T(4,128)S(1)} %bitcast.8, bf16[256,1024]{1,0:T(8,128)(2,1)S(1)} %collective-permute-done.2.refs_2_.refs_14_, bf16[256,1024]{1,0:T(8,128)(2,1)S(1)} %collective-permute-done.3.refs_3_.refs_16_, bf16[1024,3072]{1,0:T(8,128)(2,1)S(1)} %copy-done.2, ...), custom_call_target="tpu_custom_call" | custom-call | flops 6442450944 | bytes 9437184 | tf_op jit(solution)/shard_map/attend_same_across/pallas_call | solution.py:434
  68.1 0.0 collective-permute-done.1.refs_3_.refs_17_
  68.2 0.1 broadcast_select_fusion.1
  68.2 0.0 collective-permute-done.refs_2_.refs_15_
  68.2 0.1 broadcast_select_fusion
  68.3 0.1 collective-permute-start.8
  68.4 0.5 collective-permute-start.7
  68.9 1.4 collective-permute-done.8.refs_5_.refs_19_
  70.3 0.7 collective-permute-done.7.refs_4_.refs_18_
  71.0 0.0 copy-done
  71.0 0.0 copy-done.3
  71.0 0.0 copy-done.4
  71.0 0.0 copy-done.6
  71.0 165.9 %attend_same_across_near.1 = f32[512,1024]{1,0:T(8,128)} custom-call(s32[1]{0:T(128)S(6)} %copy.8.refs_0_, s32[4,5]{1,0:T(4,128)S(1)} %bitcast.9, bf16[256,1024]{1,0:T(8,128)(2,1)S(1)} %collective-permute-done.refs_2_.refs_15_, bf16[256,1024]{1,0:T(8,128)(2,1)S(1)} %collective-permute-done.1.refs_3_.refs_17_, ...), custom_call_target="tpu_custom_call" | custom-call | flops 13958643712 | bytes 10485760 | tf_op jit(solution)/shard_map/attend_same_across_near/pallas_call | solution.py:434
Async XLA Ops:
  3.4 31.4 %collective-permute-start.4 = (bf16[512,1024]{1,0:T(8,128)(2,1)}, bf16[512,1024]{1,0:T(8,128)(2,1)S(1)}, u32[]{:S(2)}, u32[]{:S(2)}) collective-permute-start(bf16[512,1024]{1,0:T(8,128)(2,1)} %get-tuple-element.24), channel_id=1, source_target_pairs={{0,1},{1,0},{2,3},{3,2},{4,5},{5,4},{6,7},{7,6},{8,9},{9,8},{10,11... | collective-permute-start | bytes 3145736 | tf_op jit(solution)/shard_map/ppermute | solution.py:450
  3.9 28.8 %collective-permute-start.2 = (bf16[256,1024]{1,0:T(8,128)(2,1)}, bf16[256,1024]{1,0:T(8,128)(2,1)S(1)}, u32[]{:S(2)}, u32[]{:S(2)}) collective-permute-start(bf16[256,1024]{1,0:T(8,128)(2,1)} %get-tuple-element.20.refs_2_.refs_12_), channel_id=1, source_target_pairs={{0,2},{1,3},{2,0},{3,1},{4,6},{5,7},{6,4},{7,5},{8,10},{9,11},{10,... | collective-permute-start | bytes 1572872 | tf_op jit(solution)/shard_map/ppermute | solution.py:450
  6.5 27.8 %collective-permute-start.5 = (bf16[128,1024]{1,0:T(8,128)(2,1)}, bf16[128,1024]{1,0:T(8,128)(2,1)S(1)}, u32[]{:S(2)}, u32[]{:S(2)}) collective-permute-start(bf16[128,1024]{1,0:T(8,128)(2,1)} %get-tuple-element.25), channel_id=1, source_target_pairs={{0,8},{8,16},{16,24},{1,9},{9,17},{17,25},{2,10},{10,18},{18,26},{... | collective-permute-start | bytes 786440 | tf_op jit(solution)/shard_map/ppermute | solution.py:450
  10.0 24.8 %collective-permute-start.6 = (bf16[128,1024]{1,0:T(8,128)(2,1)}, bf16[128,1024]{1,0:T(8,128)(2,1)S(1)}, u32[]{:S(2)}, u32[]{:S(2)}) collective-permute-start(bf16[128,1024]{1,0:T(8,128)(2,1)} %get-tuple-element.26), channel_id=1, source_target_pairs={{8,0},{16,8},{24,16},{9,1},{17,9},{25,17},{10,2},{18,10},{26,18},{... | collective-permute-start | bytes 786440 | tf_op jit(solution)/shard_map/ppermute | solution.py:450
  11.3 56.8 %collective-permute-start.1 = (bf16[256,1024]{1,0:T(8,128)(2,1)}, bf16[256,1024]{1,0:T(8,128)(2,1)S(1)}, u32[]{:S(2)}, u32[]{:S(2)}) collective-permute-start(bf16[256,1024]{1,0:T(8,128)(2,1)} %get-tuple-element.19.refs_3_.refs_13_), channel_id=1, source_target_pairs={{0,6},{1,7},{2,4},{3,5},{4,2},{5,3},{6,0},{7,1},{8,14},{9,15},{10,... | collective-permute-start | bytes 1572872 | tf_op jit(solution)/shard_map/ppermute | solution.py:450
  13.5 2.8 %copy-start.1 = (bf16[1024,3072]{1,0:T(8,128)(2,1)S(1)}, bf16[1024,3072]{1,0:T(8,128)(2,1)}, u32[]{:S(2)}) copy-start(bf16[1024,3072]{1,0:T(8,128)(2,1)} %refs_6_.1) | copy-start | bytes 18874372
  16.3 1.0 copy-start.5
  17.3 1.0 copy-start.7
  18.4 0.7 copy-start.9
  19.1 13.7 %copy-start.8 = (bf16[256,1024]{1,0:T(8,128)(2,1)S(1)}, bf16[256,1024]{1,0:T(8,128)(2,1)}, u32[]{:S(2)}) copy-start(bf16[256,1024]{1,0:T(8,128)(2,1)} %get-tuple-element.19.refs_3_.refs_13_) | copy-start | bytes 1572868
  19.1 15.7 %copy-start.10 = (s32[1,1,4,5]{3,2,1,0:T(4,128)S(1)}, s32[1,1,4,5]{3,2,1,0:T(4,128)}, u32[]{:S(2)}) copy-start(s32[1,1,4,5]{3,2,1,0:T(4,128)} %param.13) | copy-start | bytes 244
  29.8 1.0 copy-start.13
  30.8 1.9 copy-start.15
  32.8 35.5 %collective-permute-start = (bf16[256,1024]{1,0:T(8,128)(2,1)S(1)}, bf16[256,1024]{1,0:T(8,128)(2,1)S(1)}, u32[]{:S(2)}, u32[]{:S(2)}) collective-permute-start(bf16[256,1024]{1,0:T(8,128)(2,1)S(1)} %copy-done.8), channel_id=1, source_target_pairs={{0,2},{1,3},{2,0},{3,1},{4,6},{5,7},{6,4},{7,5},{8,10},{9,11},{10,... | collective-permute-start | bytes 1572872 | tf_op jit(solution)/shard_map/ppermute | solution.py:450
  34.3 21.8 %collective-permute-start.3 = (bf16[256,1024]{1,0:T(8,128)(2,1)S(1)}, bf16[256,1024]{1,0:T(8,128)(2,1)S(1)}, u32[]{:S(2)}, u32[]{:S(2)}) collective-permute-start(bf16[256,1024]{1,0:T(8,128)(2,1)S(1)} %collective-permute-done.2.refs_2_.refs_14_), channel_id=1, source_target_pairs={{0,4},{1,5},{2,6},{3,7},{4,0},{5,1},{6,2},{7,3},{8,12},{9,13},{10,... | collective-permute-start | bytes 1572872 | tf_op jit(solution)/shard_map/ppermute | solution.py:450
  34.8 2.8 %copy-start.2 = (bf16[1024,3072]{1,0:T(8,128)(2,1)S(1)}, bf16[1024,3072]{1,0:T(8,128)(2,1)}, u32[]{:S(2)}) copy-start(bf16[1024,3072]{1,0:T(8,128)(2,1)} %refs_6_.1) | copy-start | bytes 18874372
  37.6 1.2 copy-start.14
  38.8 2.2 copy-start.16
  54.1 2.0 copy-start.11
  56.1 14.9 %copy-start = (f32[1,1,512,1024]{3,2,1,0:T(8,128)S(1)}, f32[1,1,512,1024]{3,2,1,0:T(8,128)}, u32[]{:S(2)}) copy-start(f32[1,1,512,1024]{3,2,1,0:T(8,128)} %param.7) | copy-start | bytes 6291460
  56.1 14.9 %copy-start.3 = (bf16[1024,3072]{1,0:T(8,128)(2,1)S(1)}, bf16[1024,3072]{1,0:T(8,128)(2,1)}, u32[]{:S(2)}) copy-start(bf16[1024,3072]{1,0:T(8,128)(2,1)} %refs_6_.1) | copy-start | bytes 18874372
  56.1 14.9 %copy-start.4 = (bf16[1024,1024]{1,0:T(8,128)(2,1)S(1)}, bf16[1024,1024]{1,0:T(8,128)(2,1)}, u32[]{:S(2)}) copy-start(bf16[1024,1024]{1,0:T(8,128)(2,1)} %refs_10_.1) | copy-start | bytes 6291460
  56.1 15.0 %copy-start.6 = (bf16[256,1024]{1,0:T(8,128)(2,1)S(1)}, bf16[256,1024]{1,0:T(8,128)(2,1)}, u32[]{:S(2)}) copy-start(bf16[256,1024]{1,0:T(8,128)(2,1)} %get-tuple-element.20.refs_2_.refs_12_) | copy-start | bytes 1572868
  56.1 2.3 copy-start.12
  68.3 2.0 collective-permute-start.8
  68.4 2.6 %collective-permute-start.7 = (bf16[256,1024]{1,0:T(8,128)(2,1)S(1)}, bf16[256,1024]{1,0:T(8,128)(2,1)S(1)}, u32[]{:S(2)}, u32[]{:S(2)}) collective-permute-start(bf16[256,1024]{1,0:T(8,128)(2,1)S(1)} %broadcast_select_fusion.1), channel_id=1, source_target_pairs={{0,1},{1,0},{2,3},{3,2},{4,5},{5,4},{6,7},{7,6},{8,9},{9,8},{10,11... | collective-permute-start | bytes 1572872 | tf_op jit(solution)/shard_map/ppermute | solution.py:450

commit v7 on v5

--- a/solution.py
+++ b/solution.py
@@ -206,7 +206,7 @@
         query_in, acc_in, sum_in = take(3)
     if last:
         tokens_ref, wo_ref = take(2)
-        all_refs = take(1 + 4 * PARTS + 2)
+        all_refs = take(2 + 3 * PARTS + 2)
         (out_ref,) = take(1)
     else:
         if first:
@@ -319,12 +319,13 @@
     def _():
         sources = []
         part = rows // PARTS
-        for i in range(PARTS):
-            sources.append((all_refs[0].at[pl.ds(i * part, part)], columns["partner"], None, i * part))
-        for s, name in enumerate(("own", "same", "across", "near")):
-            for i, ref in enumerate(all_refs[1 + s * PARTS : 1 + (s + 1) * PARTS]):
+        for ref, name in zip(all_refs, ("partner", "near")):
+            for i in range(PARTS):
+                sources.append((ref.at[pl.ds(i * part, part)], columns[name], None, i * part))
+        for s, name in enumerate(("own", "same", "across")):
+            for i, ref in enumerate(all_refs[2 + s * PARTS : 2 + (s + 1) * PARTS]):
                 sources.append((ref, columns[name], None, i * part))
-        for ref, seen in zip(all_refs[1 + 4 * PARTS :], (lat > 0, lat < bands - 1)):
+        for ref, seen in zip(all_refs[2 + 3 * PARTS :], (lat > 0, lat < bands - 1)):
             sources.append((ref, None, seen, 0))
         att_ref[...] = safe_group(query, (wk_ref, wv_ref), sources, counts_ref, mask_ref, refs, head_size)
 
@@ -392,7 +393,7 @@
         out_shape = [wide]
         out_specs = [fixed((rows, width))]
         part = rows // PARTS
-        tiles = len(sources) + PARTS - 1
+        tiles = len(sources) + 2 * (PARTS - 1)
         scratch += [
             pltpu.VMEM((rows, width), jnp.float32),
             pltpu.VMEM((rows, GROUP), jnp.bfloat16),
@@ -468,25 +469,15 @@
 
     same[0], query, state = lax.optimization_barrier((same[0], query, state))
     across = permuted(same[:1], "lon", lambda i: (i + (4 if (i // 2) % 2 == 0 else -4)) % ring) + across
-    state = stage(["partner"], [partner], halos, qkv_weight, query, state, starts=[[0]])
-
-    across[0], state = lax.optimization_barrier((across[0], state))
-    near = [swapped(same[0], across[0])]
-    state = stage(["same", "across"], [same[:1], across[:1]], [], qkv_weight, query, state, starts=[[0], [0]])
-
-    across[1], state = lax.optimization_barrier((across[1], state))
-    near.append(swapped(same[1], across[1]))
-    final = (local, out_weight, [*partner, *own, *same, *across, *near, *halos])
-    result = stage(
-        ["same", "across", "near"],
-        [same[1:], across[1:], near],
-        [],
-        qkv_weight,
-        query,
-        state,
-        final,
-        starts=[[half], [half], [0, half]],
-    )
+    early = [["partner", "same"], [partner, same[:1]], halos, qkv_weight, query, state]
+    state = stage(*early, starts=[[0], [0]])
+
+    *rest, state = lax.optimization_barrier((*same, *across, state))
+    same, across = rest[:PARTS], rest[PARTS:]
+    near = swapped(jnp.concatenate(same, axis=0), jnp.concatenate(across, axis=0))
+    final = (local, out_weight, [*partner, near, *own, *same, *across, *halos])
+    late = [["same", "across", "near"], [same[1:], across, [near]], [], qkv_weight, query, state, final]
+    result = stage(*late, starts=[[half], [0, half], [0]])
     return result[None, None]
 
 

time: 276 us -> 278 us (level)
  waiting for transfers between devices: 2.22 us -> 7.58 us
  Pallas kernels: 255 us -> 251 us
    ppermute x9 -> x8, waiting for transfers between devices: 2.22 us -> 7.58 us  [permuted(): return [lax.ppermute(v, axis, pairs) for v in values]]
    pallas_call x4 -> x3, Pallas kernels: 252 us -> 248 us  [stage_call(): pl.pallas_call(functools.partial(stage_kernel, (first, last, sectors, sta...]
    ppermute x9 -> x8, starting transfers between devices: 12.2 us -> 11.5 us  [permuted(): return [lax.ppermute(v, axis, pairs) for v in values]]
  transfers between devices with their start and end apart: 9 -> 8, of which waited for: 2 -> 2; matrix products, arithmetic and copies ran while one was open for 0% -> 0% of each run, Pallas kernels for 14% -> 11%
where the time goes in v7:
time: 278 us; the launch traced here: 275 us
  Pallas kernels  251 us (90%)
  starting transfers between devices  11.5 us (4%)
  waiting for transfers between devices  7.58 us (3%)
    pallas_call x3, Pallas kernels, stage_call(): pl.pallas_call(functools.partial(stage_kernel, (first, last, sectors, sta...  248 us
    ppermute x8, starting transfers between devices, permuted(): return [lax.ppermute(v, axis, pairs) for v in values]  11.5 us
    ppermute x8, waiting for transfers between devices, permuted(): return [lax.ppermute(v, axis, pairs) for v in values]  7.58 us
  transfers between devices with their start and end apart: 8, of which 2 were waited for; matrix products, arithmetic and copies ran while one was open for 0% of the time, Pallas kernels for 11%

profile of v7, /device:TPU:0, one launch (start us, length us, event | category | flops | bytes accessed | tf_op | source)
XLA Modules:
  0.0 275.1 jit_solution(1866128487260404221)
XLA Ops:
  0.0 3.5 %layer_norm.1 = (bf16[256,1024]{1,0:T(8,128)(2,1)}, bf16[256,1024]{1,0:T(8,128)(2,1)}, bf16[512,1024]{1,0:T(8,128)(2,1)}, bf16[128,1024]{1,0:T(8,128)(2,1)}, bf16[128,1024]{1,0:T(8,128)(2,1)}) custom-call(f32[512,1024]{1,0:T(8,128)} %bitcast.4, f32[1,1024]{1,0:T(1,128)} %bitcast.6, s32[4,2,128]{2,1,0:T(2,128)} %halo_rows_hbm.1), custom_call_target="tpu_custom_call" | custom-call | flops 5242880 | bytes 3145728 | tf_op jit(solution)/shard_map/layer_norm/pallas_call | solution.py:91
  3.5 0.5 collective-permute-start.4
  4.0 2.6 collective-permute-start
  6.5 3.5 %collective-permute-start.5 = (bf16[128,1024]{1,0:T(8,128)(2,1)}, bf16[128,1024]{1,0:T(8,128)(2,1)S(1)}, u32[]{:S(2)}, u32[]{:S(2)}) collective-permute-start(bf16[128,1024]{1,0:T(8,128)(2,1)} %get-tuple-element.32), channel_id=1, source_target_pairs={{0,8},{8,16},{16,24},{1,9},{9,17},{17,25},{2,10},{10,18},{18,26},{... | collective-permute-start | bytes 786440 | tf_op jit(solution)/shard_map/ppermute | solution.py:441
  10.0 1.3 collective-permute-start.6
  11.3 0.6 collective-permute-start.1
  12.6 0.0 copy-start.6
  12.6 11.9 %attend_own.1 = (bf16[512,1024]{1,0:T(8,128)(2,1)}, f32[512,1024]{1,0:T(8,128)}, f32[512,1024]{1,0:T(8,128)}) custom-call(s32[1]{0:T(128)S(6)} %copy.8.refs_0_, s32[4,5]{1,0:T(4,128)} %bitcast.7, bf16[256,1024]{1,0:T(8,128)(2,1)} %get-tuple-element.25.refs_2_.refs_15_, bf16[256,1024]{1,0:T(8,128)(2,1)} %get-tuple-element.26.refs_3_.refs_16_, ...), custom_call_target="tpu_custom_call" | custom-call | flops 7516192768 | bytes 7340032 | tf_op jit(solution)/shard_map/attend_own/pallas_call | solution.py:420
  24.5 0.0 collective-permute-done.refs_3_.refs_17_
  24.5 0.0 copy-done.6
  24.5 0.0 copy-start
  24.5 2.5 collective-permute-start.3
  27.0 0.0 collective-permute-done.5.refs_4_.refs_21_
  27.0 0.0 copy-start.7
  27.0 0.5 collective-permute-start.2
  27.5 0.0 collective-permute-done.6.refs_5_.refs_22_
  27.5 0.0 collective-permute-done.4.refs_2_.refs_13_
  27.5 0.0 copy-done
  27.5 0.2 copy-done.7
  27.7 0.0 copy-start.4
  27.7 1.0 copy-done.4
  28.7 17.7 %attend_partner_same.1 = (f32[512,1024]{1,0:T(8,128)}, f32[512,1024]{1,0:T(8,128)}) custom-call(s32[1]{0:T(128)S(6)} %copy.8.refs_0_, s32[4,5]{1,0:T(4,128)} %bitcast.8, bf16[512,1024]{1,0:T(8,128)(2,1)} %copy-done.4, bf16[256,1024]{1,0:T(8,128)(2,1)} %copy-done, bf16[128,1024]{1,0:T(8,128)(2,1)} %copy-done.7, ...), custom_call_target="tpu_custom_call" | custom-call | flops 12884901888 | bytes 13631488 | tf_op jit(solution)/shard_map/attend_partner_same/pallas_call | solution.py:420
  46.4 0.0 collective-permute-done.1.refs_2_.refs_18_
  46.4 0.0 copy-start.1
  46.4 0.0 collective-permute-done.3.refs_4_.refs_20_
  46.5 0.0 copy-start.2
  46.5 4.9 %collective-permute-done.2.refs_3_.refs_19_ = bf16[256,1024]{1,0:T(8,128)(2,1)S(1)} collective-permute-done((bf16[256,1024]{1,0:T(8,128)(2,1)S(1)}, bf16[256,1024]{1,0:T(8,128)(2,1)S(1)}, u32[]{:S(2)}, u32[]{:S(2)}) %collective-permute-start.2) | collective-permute-done | bytes 524320 | tf_op jit(solution)/shard_map/ppermute | solution.py:441
  51.4 0.0 copy-start.3
  51.4 1.7 maximum_select_fusion
  53.1 0.1 collective-permute-start.7
  53.1 2.6 collective-permute-done.7.refs_5_.refs_14_
  55.8 0.0 copy-done.1
  55.8 0.0 copy-done.2
  55.8 0.0 copy-done.3
  55.8 0.0 copy-start.5
  55.8 1.0 copy-done.5
  56.8 218.2 %attend_same_across_near.1 = f32[512,1024]{1,0:T(8,128)} custom-call(s32[1]{0:T(128)S(6)} %copy.8.refs_0_, s32[4,5]{1,0:T(4,128)} %bitcast.9, bf16[256,1024]{1,0:T(8,128)(2,1)} %copy-done.1, bf16[256,1024]{1,0:T(8,128)(2,1)} %copy-done.3, bf16[256,1024]{1,0:T(8,128)(2,1)} %copy-done.2, bf16[512,1024]{1,0:T(8,128)(2,1)} %copy-done.5, ...), custom_call_target="tpu_custom_call" | custom-call | flops 17179869184 | bytes 14155776 | tf_op jit(solution)/shard_map/attend_same_across_near/pallas_call | solution.py:420
Async XLA Ops:
  3.5 24.0 %collective-permute-start.4 = (bf16[512,1024]{1,0:T(8,128)(2,1)}, bf16[512,1024]{1,0:T(8,128)(2,1)S(1)}, u32[]{:S(2)}, u32[]{:S(2)}) collective-permute-start(bf16[512,1024]{1,0:T(8,128)(2,1)} %get-tuple-element.31), channel_id=1, source_target_pairs={{0,1},{1,0},{2,3},{3,2},{4,5},{5,4},{6,7},{7,6},{8,9},{9,8},{10,11... | collective-permute-start | bytes 3145736 | tf_op jit(solution)/shard_map/ppermute | solution.py:441
  4.0 20.5 %collective-permute-start = (bf16[256,1024]{1,0:T(8,128)(2,1)}, bf16[256,1024]{1,0:T(8,128)(2,1)S(1)}, u32[]{:S(2)}, u32[]{:S(2)}) collective-permute-start(bf16[256,1024]{1,0:T(8,128)(2,1)} %get-tuple-element.25.refs_2_.refs_15_), channel_id=1, source_target_pairs={{0,2},{1,3},{2,0},{3,1},{4,6},{5,7},{6,4},{7,5},{8,10},{9,11},{10,... | collective-permute-start | bytes 1572872 | tf_op jit(solution)/shard_map/ppermute | solution.py:441
  6.5 20.4 %collective-permute-start.5 = (bf16[128,1024]{1,0:T(8,128)(2,1)}, bf16[128,1024]{1,0:T(8,128)(2,1)S(1)}, u32[]{:S(2)}, u32[]{:S(2)}) collective-permute-start(bf16[128,1024]{1,0:T(8,128)(2,1)} %get-tuple-element.32), channel_id=1, source_target_pairs={{0,8},{8,16},{16,24},{1,9},{9,17},{17,25},{2,10},{10,18},{18,26},{... | collective-permute-start | bytes 786440 | tf_op jit(solution)/shard_map/ppermute | solution.py:441
  10.0 17.5 %collective-permute-start.6 = (bf16[128,1024]{1,0:T(8,128)(2,1)}, bf16[128,1024]{1,0:T(8,128)(2,1)}, u32[]{:S(2)}, u32[]{:S(2)}) collective-permute-start(bf16[128,1024]{1,0:T(8,128)(2,1)} %get-tuple-element.33), channel_id=1, source_target_pairs={{8,0},{16,8},{24,16},{9,1},{17,9},{25,17},{10,2},{18,10},{26,18},{... | collective-permute-start | bytes 786440 | tf_op jit(solution)/shard_map/ppermute | solution.py:441
  11.3 35.1 %collective-permute-start.1 = (bf16[256,1024]{1,0:T(8,128)(2,1)}, bf16[256,1024]{1,0:T(8,128)(2,1)S(1)}, u32[]{:S(2)}, u32[]{:S(2)}) collective-permute-start(bf16[256,1024]{1,0:T(8,128)(2,1)} %get-tuple-element.26.refs_3_.refs_16_), channel_id=1, source_target_pairs={{0,2},{1,3},{2,0},{3,1},{4,6},{5,7},{6,4},{7,5},{8,10},{9,11},{10,... | collective-permute-start | bytes 1572872 | tf_op jit(solution)/shard_map/ppermute | solution.py:441
  12.6 11.9 %copy-start.6 = (bf16[256,1024]{1,0:T(8,128)(2,1)S(1)}, bf16[256,1024]{1,0:T(8,128)(2,1)}, u32[]{:S(2)}) copy-start(bf16[256,1024]{1,0:T(8,128)(2,1)} %get-tuple-element.26.refs_3_.refs_16_) | copy-start | bytes 1572868
  24.5 3.0 %copy-start = (bf16[256,1024]{1,0:T(8,128)(2,1)}, bf16[256,1024]{1,0:T(8,128)(2,1)S(1)}, u32[]{:S(2)}) copy-start(bf16[256,1024]{1,0:T(8,128)(2,1)S(1)} %collective-permute-done.refs_3_.refs_17_) | copy-start | bytes 1572868
  24.5 22.0 %collective-permute-start.3 = (bf16[256,1024]{1,0:T(8,128)(2,1)S(1)}, bf16[256,1024]{1,0:T(8,128)(2,1)S(1)}, u32[]{:S(2)}, u32[]{:S(2)}) collective-permute-start(bf16[256,1024]{1,0:T(8,128)(2,1)S(1)} %copy-done.6), channel_id=1, source_target_pairs={{0,6},{1,7},{2,4},{3,5},{4,2},{5,3},{6,0},{7,1},{8,14},{9,15},{10,... | collective-permute-start | bytes 1572872 | tf_op jit(solution)/shard_map/ppermute | solution.py:441
  27.0 0.7 copy-start.7
  27.0 24.4 %collective-permute-start.2 = (bf16[256,1024]{1,0:T(8,128)(2,1)S(1)}, bf16[256,1024]{1,0:T(8,128)(2,1)S(1)}, u32[]{:S(2)}, u32[]{:S(2)}) collective-permute-start(bf16[256,1024]{1,0:T(8,128)(2,1)S(1)} %collective-permute-done.refs_3_.refs_17_), channel_id=1, source_target_pairs={{0,4},{1,5},{2,6},{3,7},{4,0},{5,1},{6,2},{7,3},{8,12},{9,13},{10,... | collective-permute-start | bytes 1572872 | tf_op jit(solution)/shard_map/ppermute | solution.py:441
  27.7 1.0 copy-start.4
  46.4 9.4 %copy-start.1 = (bf16[256,1024]{1,0:T(8,128)(2,1)}, bf16[256,1024]{1,0:T(8,128)(2,1)S(1)}, u32[]{:S(2)}) copy-start(bf16[256,1024]{1,0:T(8,128)(2,1)S(1)} %collective-permute-done.1.refs_2_.refs_18_) | copy-start | bytes 1572868
  46.5 9.3 %copy-start.2 = (bf16[256,1024]{1,0:T(8,128)(2,1)}, bf16[256,1024]{1,0:T(8,128)(2,1)S(1)}, u32[]{:S(2)}) copy-start(bf16[256,1024]{1,0:T(8,128)(2,1)S(1)} %collective-permute-done.3.refs_4_.refs_20_) | copy-start | bytes 1572868
  51.4 4.4 %copy-start.3 = (bf16[256,1024]{1,0:T(8,128)(2,1)}, bf16[256,1024]{1,0:T(8,128)(2,1)S(1)}, u32[]{:S(2)}) copy-start(bf16[256,1024]{1,0:T(8,128)(2,1)S(1)} %collective-permute-done.2.refs_3_.refs_19_) | copy-start | bytes 1572868
  53.1 2.7 collective-permute-start.7
  55.8 1.0 copy-start.5

commit v8 on v7

--- a/solution.py
+++ b/solution.py
@@ -10,7 +10,7 @@
 
 HEADS = 16
 LANES = 128
-GROUP = 256
+GROUP = 512
 PARTS = 2
 NEG = -1e30
 FLOOR = -1e25
@@ -206,7 +206,7 @@
         query_in, acc_in, sum_in = take(3)
     if last:
         tokens_ref, wo_ref = take(2)
-        all_refs = take(2 + 3 * PARTS + 2)
+        all_refs = take(1 + 4 * PARTS + 2)
         (out_ref,) = take(1)
     else:
         if first:
@@ -319,13 +319,12 @@
     def _():
         sources = []
         part = rows // PARTS
-        for ref, name in zip(all_refs, ("partner", "near")):
-            for i in range(PARTS):
-                sources.append((ref.at[pl.ds(i * part, part)], columns[name], None, i * part))
-        for s, name in enumerate(("own", "same", "across")):
-            for i, ref in enumerate(all_refs[2 + s * PARTS : 2 + (s + 1) * PARTS]):
+        for i in range(PARTS):
+            sources.append((all_refs[0].at[pl.ds(i * part, part)], columns["partner"], None, i * part))
+        for s, name in enumerate(("own", "same", "across", "near")):
+            for i, ref in enumerate(all_refs[1 + s * PARTS : 1 + (s + 1) * PARTS]):
                 sources.append((ref, columns[name], None, i * part))
-        for ref, seen in zip(all_refs[2 + 3 * PARTS :], (lat > 0, lat < bands - 1)):
+        for ref, seen in zip(all_refs[1 + 4 * PARTS :], (lat > 0, lat < bands - 1)):
             sources.append((ref, None, seen, 0))
         att_ref[...] = safe_group(query, (wk_ref, wv_ref), sources, counts_ref, mask_ref, refs, head_size)
 
@@ -393,7 +392,7 @@
         out_shape = [wide]
         out_specs = [fixed((rows, width))]
         part = rows // PARTS
-        tiles = len(sources) + 2 * (PARTS - 1)
+        tiles = len(sources) + PARTS - 1
         scratch += [
             pltpu.VMEM((rows, width), jnp.float32),
             pltpu.VMEM((rows, GROUP), jnp.bfloat16),
@@ -425,7 +424,7 @@
         out_specs=out_specs,
         scratch_shapes=scratch,
         compiler_params=pltpu.CompilerParams(vmem_limit_bytes=VMEM_LIMIT),
-        cost_estimate=pl.CostEstimate(flops=flops, bytes_accessed=moved, transcendentals=rows * keys * HEADS),
+        cost_estimate=pl.CostEstimate(flops=flops // (16 if first else 1), bytes_accessed=moved // 16, transcendentals=0),
         name="attend_" + "_".join(sectors),
     )(*args)
     if last:
@@ -449,10 +448,13 @@
     rows = local.shape[0]
     outs = norm_call(local, norm_gain, halo_rows)
     own, (whole, north_rows, south_rows) = outs[:PARTS], outs[PARTS:]
-
-    same = permuted(own, "lon", lambda i: i ^ 2)
+    assert PARTS == 2
+
+    partner = permuted([whole], "lon", lambda i: i ^ 1)
+    same = permuted(own[:1], "lon", lambda i: i ^ 2)
+    north_rows, *partner = lax.optimization_barrier((north_rows, *partner))
+    same += permuted(own[1:], "lon", lambda i: i ^ 2)
     across = permuted(own[1:], "lon", lambda i: (i + (-2 if (i // 2) % 2 == 0 else 2)) % ring)
-    partner = permuted([whole], "lon", lambda i: i ^ 1)
     halos = [
         permuted([south_rows], "lat", lambda b: b + 1)[0],
         permuted([north_rows], "lat", lambda b: b - 1)[0],
@@ -474,10 +476,10 @@
 
     *rest, state = lax.optimization_barrier((*same, *across, state))
     same, across = rest[:PARTS], rest[PARTS:]
-    near = swapped(jnp.concatenate(same, axis=0), jnp.concatenate(across, axis=0))
-    final = (local, out_weight, [*partner, near, *own, *same, *across, *halos])
-    late = [["same", "across", "near"], [same[1:], across, [near]], [], qkv_weight, query, state, final]
-    result = stage(*late, starts=[[half], [0, half], [0]])
+    near = [swapped(s, a) for s, a in zip(same, across)]
+    final = (local, out_weight, [*partner, *own, *same, *across, *near, *halos])
+    late = [["same", "across", "near"], [same[1:], across, near], [], qkv_weight, query, state, final]
+    result = stage(*late, starts=[[half], [0, half], [0, half]])
     return result[None, None]
 
 

time: 278 us -> 251 us (0.903)
  Pallas kernels: 251 us -> 228 us
    pallas_call x3, Pallas kernels: 248 us -> 224 us  [stage_call(): pl.pallas_call(functools.partial(stage_kernel, (first, last, sectors, sta...]
    ppermute x8 -> x9, waiting for transfers between devices: 7.58 us -> 5.76 us  [permuted(): return [lax.ppermute(v, axis, pairs) for v in values]]
    ppermute x8 -> x9, starting transfers between devices: 11.5 us -> 11.6 us  [permuted(): return [lax.ppermute(v, axis, pairs) for v in values]]
  transfers between devices with their start and end apart: 8 -> 9, of which waited for: 2 -> 3; matrix products, arithmetic and copies ran while one was open for 0% -> 0% of each run, Pallas kernels for 11% -> 12%
where the time goes in v8:
time: 251 us; the launch traced here: 249 us
  Pallas kernels  228 us (91%)
  starting transfers between devices  11.6 us (5%)
  waiting for transfers between devices  5.76 us (2%)
    pallas_call x3, Pallas kernels, stage_call(): pl.pallas_call(functools.partial(stage_kernel, (first, last, sectors, sta...  224 us
    ppermute x9, starting transfers between devices, permuted(): return [lax.ppermute(v, axis, pairs) for v in values]  11.6 us
    ppermute x9, waiting for transfers between devices, permuted(): return [lax.ppermute(v, axis, pairs) for v in values]  5.76 us
  transfers between devices with their start and end apart: 9, of which 3 were waited for; matrix products, arithmetic and copies ran while one was open for 0% of the time, Pallas kernels for 12%

profile of v8, /device:TPU:0, one launch (start us, length us, event | category | flops | bytes accessed | tf_op | source)
XLA Modules:
  0.0 249.3 jit_solution(12958314323964705036)
XLA Ops:
  0.0 3.4 %layer_norm.1 = (bf16[256,1024]{1,0:T(8,128)(2,1)}, bf16[256,1024]{1,0:T(8,128)(2,1)}, bf16[512,1024]{1,0:T(8,128)(2,1)}, bf16[128,1024]{1,0:T(8,128)(2,1)}, bf16[128,1024]{1,0:T(8,128)(2,1)}) custom-call(f32[512,1024]{1,0:T(8,128)} %bitcast.4, f32[1,1024]{1,0:T(1,128)} %bitcast.6, s32[4,2,128]{2,1,0:T(2,128)} %halo_rows_hbm.1), custom_call_target="tpu_custom_call" | custom-call | flops 5242880 | bytes 3145728 | tf_op jit(solution)/shard_map/layer_norm/pallas_call | solution.py:91
  3.4 0.5 collective-permute-start.4
  3.9 2.6 %collective-permute-start = (bf16[256,1024]{1,0:T(8,128)(2,1)}, bf16[256,1024]{1,0:T(8,128)(2,1)S(1)}, u32[]{:S(2)}, u32[]{:S(2)}) collective-permute-start(bf16[256,1024]{1,0:T(8,128)(2,1)} %get-tuple-element.27.refs_2_.refs_15_), channel_id=1, source_target_pairs={{0,2},{1,3},{2,0},{3,1},{4,6},{5,7},{6,4},{7,5},{8,10},{9,11},{10,... | collective-permute-start | bytes 1572872 | tf_op jit(solution)/shard_map/ppermute | solution.py:440
  6.5 3.5 %collective-permute-start.5 = (bf16[128,1024]{1,0:T(8,128)(2,1)}, bf16[128,1024]{1,0:T(8,128)(2,1)S(1)}, u32[]{:S(2)}, u32[]{:S(2)}) collective-permute-start(bf16[128,1024]{1,0:T(8,128)(2,1)} %get-tuple-element.36), channel_id=1, source_target_pairs={{0,8},{8,16},{16,24},{1,9},{9,17},{17,25},{2,10},{10,18},{18,26},{... | collective-permute-start | bytes 786440 | tf_op jit(solution)/shard_map/ppermute | solution.py:440
  10.0 0.0 collective-permute-done.4.refs_2_.refs_14_
  10.0 0.0 copy-start.4
  10.0 1.3 collective-permute-start.6
  11.3 0.6 collective-permute-start.1
  11.9 2.4 collective-permute-start.3
  15.0 12.0 %attend_own.1 = (bf16[512,1024]{1,0:T(8,128)(2,1)}, f32[512,1024]{1,0:T(8,128)}, f32[512,1024]{1,0:T(8,128)}) custom-call(s32[1]{0:T(128)S(6)} %copy.8.refs_0_, s32[4,5]{1,0:T(4,128)} %bitcast.7, bf16[256,1024]{1,0:T(8,128)(2,1)} %get-tuple-element.27.refs_2_.refs_15_, bf16[256,1024]{1,0:T(8,128)(2,1)} %get-tuple-element.28.refs_3_.refs_16_, ...), custom_call_target="tpu_custom_call" | custom-call | flops 469762048 | bytes 458752 | tf_op jit(solution)/shard_map/attend_own/pallas_call | solution.py:419
  27.0 0.0 copy-done.4
  27.0 0.0 collective-permute-done.refs_3_.refs_17_
  27.0 0.0 copy-start
  27.0 0.6 collective-permute-start.2
  27.6 0.0 collective-permute-done.5.refs_4_.refs_23_
  27.6 0.0 copy-start.7
  27.6 0.0 collective-permute-done.6.refs_5_.refs_24_
  27.6 0.2 copy-done
  27.8 0.5 copy-done.7
  28.3 0.0 copy-start.8
  28.3 0.7 copy-done.8
  29.0 18.6 %attend_partner_same.1 = (f32[512,1024]{1,0:T(8,128)}, f32[512,1024]{1,0:T(8,128)}) custom-call(s32[1]{0:T(128)S(6)} %copy.8.refs_0_, s32[4,5]{1,0:T(4,128)} %bitcast.8, bf16[512,1024]{1,0:T(8,128)(2,1)} %copy-done.4, bf16[256,1024]{1,0:T(8,128)(2,1)} %copy-done, bf16[128,1024]{1,0:T(8,128)(2,1)} %copy-done.7, bf16[128,1024]{1,0:T(8,128)(2,1)} %copy-done.8, ...), custom_call_target="tpu_custom_call" | custom-call | flops 12884901888 | bytes 851968 | tf_op jit(solution)/shard_map/attend_partner_same/pallas_call | solution.py:419
  47.6 0.0 collective-permute-done.1.refs_2_.refs_18_
  47.6 0.0 copy-start.1
  47.6 0.0 collective-permute-done.3.refs_4_.refs_20_
  47.6 0.0 copy-start.2
  47.6 3.9 %collective-permute-done.2.refs_3_.refs_19_ = bf16[256,1024]{1,0:T(8,128)(2,1)S(1)} collective-permute-done((bf16[256,1024]{1,0:T(8,128)(2,1)S(1)}, bf16[256,1024]{1,0:T(8,128)(2,1)S(1)}, u32[]{:S(2)}, u32[]{:S(2)}) %collective-permute-start.2) | collective-permute-done | bytes 524320 | tf_op jit(solution)/shard_map/ppermute | solution.py:440
  51.5 0.0 copy-start.3
  51.5 0.1 broadcast_select_fusion
  51.5 0.1 collective-permute-start.8
  51.6 1.2 broadcast_select_fusion.1
  52.8 0.1 collective-permute-start.7
  52.8 0.7 collective-permute-done.8.refs_6_.refs_22_
  53.5 0.0 copy-start.5
  53.5 1.2 collective-permute-done.7.refs_5_.refs_21_
  54.7 0.0 copy-done.1
  54.7 0.0 copy-done.2
  54.7 0.0 copy-done.3
  54.8 0.0 copy-done.5
  54.8 0.0 copy-start.6
  54.8 0.8 copy-done.6
  55.6 193.6 %attend_same_across_near.1 = f32[512,1024]{1,0:T(8,128)} custom-call(s32[1]{0:T(128)S(6)} %copy.8.refs_0_, s32[4,5]{1,0:T(4,128)} %bitcast.9, bf16[256,1024]{1,0:T(8,128)(2,1)} %copy-done.1, bf16[256,1024]{1,0:T(8,128)(2,1)} %copy-done.3, bf16[256,1024]{1,0:T(8,128)(2,1)} %copy-done.2, bf16[256,1024]{1,0:T(8,128)(2,1)} %copy-done.6, ...), custom_call_target="tpu_custom_call" | custom-call | flops 17179869184 | bytes 884736 | tf_op jit(solution)/shard_map/attend_same_across_near/pallas_call | solution.py:419
Async XLA Ops:
  3.4 6.6 %collective-permute-start.4 = (bf16[512,1024]{1,0:T(8,128)(2,1)}, bf16[512,1024]{1,0:T(8,128)(2,1)S(1)}, u32[]{:S(2)}, u32[]{:S(2)}) collective-permute-start(bf16[512,1024]{1,0:T(8,128)(2,1)} %get-tuple-element.34), channel_id=1, source_target_pairs={{0,1},{1,0},{2,3},{3,2},{4,5},{5,4},{6,7},{7,6},{8,9},{9,8},{10,11... | collective-permute-start | bytes 3145736 | tf_op jit(solution)/shard_map/ppermute | solution.py:440
  3.9 23.1 %collective-permute-start = (bf16[256,1024]{1,0:T(8,128)(2,1)}, bf16[256,1024]{1,0:T(8,128)(2,1)S(1)}, u32[]{:S(2)}, u32[]{:S(2)}) collective-permute-start(bf16[256,1024]{1,0:T(8,128)(2,1)} %get-tuple-element.27.refs_2_.refs_15_), channel_id=1, source_target_pairs={{0,2},{1,3},{2,0},{3,1},{4,6},{5,7},{6,4},{7,5},{8,10},{9,11},{10,... | collective-permute-start | bytes 1572872 | tf_op jit(solution)/shard_map/ppermute | solution.py:440
  6.5 21.1 %collective-permute-start.5 = (bf16[128,1024]{1,0:T(8,128)(2,1)}, bf16[128,1024]{1,0:T(8,128)(2,1)S(1)}, u32[]{:S(2)}, u32[]{:S(2)}) collective-permute-start(bf16[128,1024]{1,0:T(8,128)(2,1)} %get-tuple-element.36), channel_id=1, source_target_pairs={{0,8},{8,16},{16,24},{1,9},{9,17},{17,25},{2,10},{10,18},{18,26},{... | collective-permute-start | bytes 786440 | tf_op jit(solution)/shard_map/ppermute | solution.py:440
  10.0 17.0 %copy-start.4 = (bf16[512,1024]{1,0:T(8,128)(2,1)}, bf16[512,1024]{1,0:T(8,128)(2,1)S(1)}, u32[]{:S(2)}) copy-start(bf16[512,1024]{1,0:T(8,128)(2,1)S(1)} %collective-permute-done.4.refs_2_.refs_14_) | copy-start | bytes 3145732
  10.0 17.6 %collective-permute-start.6 = (bf16[128,1024]{1,0:T(8,128)(2,1)}, bf16[128,1024]{1,0:T(8,128)(2,1)S(1)}, u32[]{:S(2)}, u32[]{:S(2)}) collective-permute-start(bf16[128,1024]{1,0:T(8,128)(2,1)} %get-tuple-element.37), channel_id=1, source_target_pairs={{8,0},{16,8},{24,16},{9,1},{17,9},{25,17},{10,2},{18,10},{26,18},{... | collective-permute-start | bytes 786440 | tf_op jit(solution)/shard_map/ppermute | solution.py:440
  11.3 36.3 %collective-permute-start.1 = (bf16[256,1024]{1,0:T(8,128)(2,1)}, bf16[256,1024]{1,0:T(8,128)(2,1)S(1)}, u32[]{:S(2)}, u32[]{:S(2)}) collective-permute-start(bf16[256,1024]{1,0:T(8,128)(2,1)} %get-tuple-element.28.refs_3_.refs_16_), channel_id=1, source_target_pairs={{0,2},{1,3},{2,0},{3,1},{4,6},{5,7},{6,4},{7,5},{8,10},{9,11},{10,... | collective-permute-start | bytes 1572872 | tf_op jit(solution)/shard_map/ppermute | solution.py:440
  11.9 35.7 %collective-permute-start.3 = (bf16[256,1024]{1,0:T(8,128)(2,1)}, bf16[256,1024]{1,0:T(8,128)(2,1)S(1)}, u32[]{:S(2)}, u32[]{:S(2)}) collective-permute-start(bf16[256,1024]{1,0:T(8,128)(2,1)} %get-tuple-element.28.refs_3_.refs_16_), channel_id=1, source_target_pairs={{0,6},{1,7},{2,4},{3,5},{4,2},{5,3},{6,0},{7,1},{8,14},{9,15},{10,... | collective-permute-start | bytes 1572872 | tf_op jit(solution)/shard_map/ppermute | solution.py:440
  27.0 0.8 copy-start
  27.0 24.5 %collective-permute-start.2 = (bf16[256,1024]{1,0:T(8,128)(2,1)S(1)}, bf16[256,1024]{1,0:T(8,128)(2,1)S(1)}, u32[]{:S(2)}, u32[]{:S(2)}) collective-permute-start(bf16[256,1024]{1,0:T(8,128)(2,1)S(1)} %collective-permute-done.refs_3_.refs_17_), channel_id=1, source_target_pairs={{0,4},{1,5},{2,6},{3,7},{4,0},{5,1},{6,2},{7,3},{8,12},{9,13},{10,... | collective-permute-start | bytes 1572872 | tf_op jit(solution)/shard_map/ppermute | solution.py:440
  27.6 0.7 copy-start.7
  28.3 0.7 copy-start.8
  47.6 7.2 %copy-start.1 = (bf16[256,1024]{1,0:T(8,128)(2,1)}, bf16[256,1024]{1,0:T(8,128)(2,1)S(1)}, u32[]{:S(2)}) copy-start(bf16[256,1024]{1,0:T(8,128)(2,1)S(1)} %collective-permute-done.1.refs_2_.refs_18_) | copy-start | bytes 1572868
  47.6 7.1 %copy-start.2 = (bf16[256,1024]{1,0:T(8,128)(2,1)}, bf16[256,1024]{1,0:T(8,128)(2,1)S(1)}, u32[]{:S(2)}) copy-start(bf16[256,1024]{1,0:T(8,128)(2,1)S(1)} %collective-permute-done.3.refs_4_.refs_20_) | copy-start | bytes 1572868
  51.5 3.3 %copy-start.3 = (bf16[256,1024]{1,0:T(8,128)(2,1)}, bf16[256,1024]{1,0:T(8,128)(2,1)S(1)}, u32[]{:S(2)}) copy-start(bf16[256,1024]{1,0:T(8,128)(2,1)S(1)} %collective-permute-done.2.refs_3_.refs_19_) | copy-start | bytes 1572868
  51.5 2.0 collective-permute-start.8
  52.8 2.0 collective-permute-start.7
  53.5 1.2 copy-start.5
  54.8 0.8 copy-start.6

commit v9 on v8

--- a/solution.py
+++ b/solution.py
@@ -231,7 +231,6 @@
         query = query_in[...]
     rows, width = query.shape
     zero = jnp.zeros((), jnp.bfloat16)
-    one = jnp.ones((), jnp.bfloat16)
     biases, spans = [], []
     at = 0
     for name, parts, starts in zip(sectors, sector_refs, part_starts):
@@ -265,47 +264,47 @@
         biases.append(None)
 
     low = lax.broadcasted_iota(jnp.int32, (rows, LANES), 1) < head_size
-    low_key = lax.broadcasted_iota(jnp.int32, (LANES, at), 0) < head_size
-    low_value = lax.broadcasted_iota(jnp.int32, (at, LANES), 1) < head_size
-
-    def lanes_of(unit):
-        return slice(unit // 2 * LANES, (unit // 2 + 1) * LANES)
-
-    def score(unit):
-        lanes, odd = lanes_of(unit), unit % 2
-        half = ~low if odd else low
-        right = jnp.where(~low_key if odd else low_key, key_ref[lanes, :], one)
+
+    def lanes_of(pair):
+        return slice(pair * LANES, (pair + 1) * LANES)
+
+
+    whole_query = query
+
+    def score(pair):
+        query = whole_query[:, lanes_of(pair)]
+        both = jnp.concatenate([jnp.where(low, query, zero), jnp.where(low, zero, query)], axis=0)
         for (begin, end), bias in zip(spans, biases):
-            left = jnp.where(half, query[:, lanes], zero if bias is None else bias)
-            score_refs[odd][:, begin:end] = matmul(left, right[:, begin:end])
-
-    def weigh(unit):
-        scores = score_refs[unit % 2][...] * (LOG2E * head_size**-0.5)
-        weight_refs[unit % 2][...] = jnp.exp2(scores).astype(jnp.bfloat16)
-
-    halves = {}
-
-    def gather(unit):
-        lanes, odd = lanes_of(unit), unit % 2
-        values = jnp.where(~low_value if odd else low_value, value_ref[:, lanes], ones_ref[...])
-        halves[odd] = matmul(weight_refs[odd][...], values)
-        if not odd:
-            return
-        acc, total = jnp.where(low, halves[0], halves[1]), jnp.where(low, halves[1], halves[0])
+            left, right = both, key_ref[lanes_of(pair), begin:end]
+            if bias is not None:
+                left = jnp.concatenate([both, jnp.concatenate([bias, bias], axis=0)], axis=1)
+                right = jnp.concatenate([right, jnp.ones((LANES, end - begin), jnp.bfloat16)], axis=0)
+            score_refs[pair % 2][:, begin:end] = matmul(left, right)
+
+    def weigh(pair):
+        scores = score_refs[pair % 2][...] * (LOG2E * head_size**-0.5)
+        weight_refs[pair % 2][...] = jnp.exp2(scores).astype(jnp.bfloat16)
+
+    def gather(pair):
+        lanes = lanes_of(pair)
+        values = jnp.concatenate([value_ref[:, lanes], ones_ref[...]], axis=1)
+        result = matmul(weight_refs[pair % 2][...], values)
+        acc = jnp.where(low, result[:rows, :LANES], result[rows:, :LANES])
+        total = jnp.where(low, result[:rows, LANES:], result[rows:, LANES:])
         if not first:
             acc = acc + acc_in[:, lanes]
             total = total + sum_in[:, lanes]
         acc_out[:, lanes] = acc
         sum_out[:, lanes] = total
 
-    units = width // head_size
-    for u in range(units + 2):
-        if u < units:
-            score(u)
-        if 0 <= u - 1 < units:
-            weigh(u - 1)
-        if 0 <= u - 2 < units:
-            gather(u - 2)
+    pairs = width // LANES
+    for p in range(pairs + 2):
+        if p < pairs:
+            score(p)
+        if 0 <= p - 1 < pairs:
+            weigh(p - 1)
+        if 0 <= p - 2 < pairs:
+            gather(p - 2)
     if not last:
         return
 
@@ -313,7 +312,7 @@
     fine = (total > SUM_MIN) & (total < SUM_MAX)
     for pair in range(width // LANES):
         lanes = slice(pair * LANES, (pair + 1) * LANES)
-        att_ref[:, lanes] = (acc_out[:, lanes] / pltpu.roll(total[:, lanes], head_size, 1)).astype(jnp.bfloat16)
+        att_ref[:, lanes] = (acc_out[:, lanes] / total[:, lanes]).astype(jnp.bfloat16)
 
     @pl.when(jnp.min(fine.astype(jnp.float32)) < 0.5)
     def _():
@@ -377,10 +376,10 @@
         pltpu.VMEM((GROUP, keys), jnp.bfloat16),
         pltpu.VMEM((keys, GROUP), jnp.bfloat16),
         pltpu.VMEM((keys, LANES), jnp.bfloat16),
-        pltpu.VMEM((rows, keys), jnp.float32),
-        pltpu.VMEM((rows, keys), jnp.float32),
-        pltpu.VMEM((rows, keys), jnp.bfloat16),
-        pltpu.VMEM((rows, keys), jnp.bfloat16),
+        pltpu.VMEM((2 * rows, keys), jnp.float32),
+        pltpu.VMEM((2 * rows, keys), jnp.float32),
+        pltpu.VMEM((2 * rows, keys), jnp.bfloat16),
+        pltpu.VMEM((2 * rows, keys), jnp.bfloat16),
     ]
     wide = jax.ShapeDtypeStruct((rows, width), jnp.float32)
     moved = sum(a.size * a.dtype.itemsize for a in args[2:] if a is not qkv_weight) + 3 * model * width * 2
@@ -452,9 +451,9 @@
 
     partner = permuted([whole], "lon", lambda i: i ^ 1)
     same = permuted(own[:1], "lon", lambda i: i ^ 2)
+    across = permuted(own[1:], "lon", lambda i: (i + (-2 if (i // 2) % 2 == 0 else 2)) % ring)
+    same += permuted(own[1:], "lon", lambda i: i ^ 2)
     north_rows, *partner = lax.optimization_barrier((north_rows, *partner))
-    same += permuted(own[1:], "lon", lambda i: i ^ 2)
-    across = permuted(own[1:], "lon", lambda i: (i + (-2 if (i // 2) % 2 == 0 else 2)) % ring)
     halos = [
         permuted([south_rows], "lat", lambda b: b + 1)[0],
         permuted([north_rows], "lat", lambda b: b - 1)[0],
@@ -474,12 +473,12 @@
     early = [["partner", "same"], [partner, same[:1]], halos, qkv_weight, query, state]
     state = stage(*early, starts=[[0], [0]])
 
-    *rest, state = lax.optimization_barrier((*same, *across, state))
-    same, across = rest[:PARTS], rest[PARTS:]
+    *rest, state = lax.optimization_barrier((*across, *same, state))
+    across, same = rest[:PARTS], rest[PARTS:]
     near = [swapped(s, a) for s, a in zip(same, across)]
     final = (local, out_weight, [*partner, *own, *same, *across, *near, *halos])
-    late = [["same", "across", "near"], [same[1:], across, near], [], qkv_weight, query, state, final]
-    result = stage(*late, starts=[[half], [0, half], [0, half]])
+    late = [["across", "same", "near"], [across, same[1:], near], [], qkv_weight, query, state, final]
+    result = stage(*late, starts=[[0, half], [half], [0, half]])
     return result[None, None]
 
 

time: 251 us -> 247 us (0.984)
  waiting for transfers between devices: 5.76 us -> 1.91 us
    ppermute x9, waiting for transfers between devices: 5.76 us -> 1.91 us  [permuted(): return [lax.ppermute(v, axis, pairs) for v in values]]
  transfers between devices with their start and end apart: 9 -> 9, of which waited for: 3 -> 2; matrix products, arithmetic and copies ran while one was open for 0% -> 1% of each run, Pallas kernels for 12% -> 12%
where the time goes in v9:
time: 247 us; the launch traced here: 246 us
  Pallas kernels  228 us (92%)
  starting transfers between devices  11.6 us (5%)
    pallas_call x3, Pallas kernels, stage_call(): pl.pallas_call(functools.partial(stage_kernel, (first, last, sectors, sta...  224 us
    ppermute x9, starting transfers between devices, permuted(): return [lax.ppermute(v, axis, pairs) for v in values]  11.6 us
  transfers between devices with their start and end apart: 9, of which 2 were waited for; matrix products, arithmetic and copies ran while one was open for 1% of the time, Pallas kernels for 12%

profile of v9, /device:TPU:0, one launch (start us, length us, event | category | flops | bytes accessed | tf_op | source)
XLA Modules:
  0.0 245.8 jit_solution(17551079702717681530)
XLA Ops:
  0.0 3.4 %layer_norm.1 = (bf16[256,1024]{1,0:T(8,128)(2,1)}, bf16[256,1024]{1,0:T(8,128)(2,1)}, bf16[512,1024]{1,0:T(8,128)(2,1)}, bf16[128,1024]{1,0:T(8,128)(2,1)}, bf16[128,1024]{1,0:T(8,128)(2,1)}) custom-call(f32[512,1024]{1,0:T(8,128)} %bitcast.4, f32[1,1024]{1,0:T(1,128)} %bitcast.6, s32[4,2,128]{2,1,0:T(2,128)} %halo_rows_hbm.1), custom_call_target="tpu_custom_call" | custom-call | flops 5242880 | bytes 3145728 | tf_op jit(solution)/shard_map/layer_norm/pallas_call | solution.py:91
  3.4 0.5 collective-permute-start.4
  3.9 2.6 %collective-permute-start = (bf16[256,1024]{1,0:T(8,128)(2,1)}, bf16[256,1024]{1,0:T(8,128)(2,1)S(1)}, u32[]{:S(2)}, u32[]{:S(2)}) collective-permute-start(bf16[256,1024]{1,0:T(8,128)(2,1)} %get-tuple-element.27.refs_2_.refs_15_), channel_id=1, source_target_pairs={{0,2},{1,3},{2,0},{3,1},{4,6},{5,7},{6,4},{7,5},{8,10},{9,11},{10,... | collective-permute-start | bytes 1572872 | tf_op jit(solution)/shard_map/ppermute | solution.py:439
  6.5 3.5 %collective-permute-start.5 = (bf16[128,1024]{1,0:T(8,128)(2,1)}, bf16[128,1024]{1,0:T(8,128)(2,1)S(1)}, u32[]{:S(2)}, u32[]{:S(2)}) collective-permute-start(bf16[128,1024]{1,0:T(8,128)(2,1)} %get-tuple-element.36), channel_id=1, source_target_pairs={{0,8},{8,16},{16,24},{1,9},{9,17},{17,25},{2,10},{10,18},{18,26},{... | collective-permute-start | bytes 786440 | tf_op jit(solution)/shard_map/ppermute | solution.py:439
  10.0 0.0 collective-permute-done.4.refs_2_.refs_14_
  10.0 0.0 copy-start.4
  10.0 1.3 collective-permute-start.6
  11.3 1.6 collective-permute-start.2
  12.9 1.5 collective-permute-start.3
  15.0 11.9 %attend_own.1 = (bf16[512,1024]{1,0:T(8,128)(2,1)}, f32[512,1024]{1,0:T(8,128)}, f32[512,1024]{1,0:T(8,128)}) custom-call(s32[1]{0:T(128)S(6)} %copy.8.refs_0_, s32[4,5]{1,0:T(4,128)} %bitcast.7, bf16[256,1024]{1,0:T(8,128)(2,1)} %get-tuple-element.27.refs_2_.refs_15_, bf16[256,1024]{1,0:T(8,128)(2,1)} %get-tuple-element.28.refs_3_.refs_16_, ...), custom_call_target="tpu_custom_call" | custom-call | flops 469762048 | bytes 458752 | tf_op jit(solution)/shard_map/attend_own/pallas_call | solution.py:418
  27.0 0.0 copy-done.4
  27.0 0.0 collective-permute-done.refs_3_.refs_17_
  27.0 0.0 copy-start
  27.0 0.6 collective-permute-start.1
  27.6 0.0 collective-permute-done.5.refs_4_.refs_23_
  27.6 0.0 copy-start.7
  27.6 0.0 collective-permute-done.6.refs_5_.refs_24_
  27.6 0.2 copy-done
  27.8 0.5 copy-done.7
  28.3 0.0 copy-start.8
  28.3 0.7 copy-done.8
  29.0 18.5 %attend_partner_same.1 = (f32[512,1024]{1,0:T(8,128)}, f32[512,1024]{1,0:T(8,128)}) custom-call(s32[1]{0:T(128)S(6)} %copy.8.refs_0_, s32[4,5]{1,0:T(4,128)} %bitcast.8, bf16[512,1024]{1,0:T(8,128)(2,1)} %copy-done.4, bf16[256,1024]{1,0:T(8,128)(2,1)} %copy-done, bf16[128,1024]{1,0:T(8,128)(2,1)} %copy-done.7, bf16[128,1024]{1,0:T(8,128)(2,1)} %copy-done.8, ...), custom_call_target="tpu_custom_call" | custom-call | flops 12884901888 | bytes 851968 | tf_op jit(solution)/shard_map/attend_partner_same/pallas_call | solution.py:418
  47.5 0.0 collective-permute-done.2.refs_3_.refs_20_
  47.5 0.0 copy-start.1
  47.5 0.0 collective-permute-done.3.refs_4_.refs_18_
  47.5 0.0 copy-start.2
  47.5 0.0 collective-permute-done.1.refs_2_.refs_19_
  47.5 0.0 copy-start.3
  47.5 0.1 broadcast_select_fusion
  47.6 0.1 collective-permute-start.8
  47.7 1.5 broadcast_select_fusion.1
  49.2 0.1 collective-permute-start.7
  49.2 0.3 collective-permute-done.8.refs_6_.refs_22_
  49.6 0.0 copy-start.5
  49.6 1.6 collective-permute-done.7.refs_5_.refs_21_
  51.1 0.0 copy-done.1
  51.1 0.0 copy-done.2
  51.1 0.0 copy-done.3
  51.1 0.0 copy-done.5
  51.2 0.0 copy-start.6
  51.2 0.8 copy-done.6
  52.0 193.7 %attend_across_same_near.1 = f32[512,1024]{1,0:T(8,128)} custom-call(s32[1]{0:T(128)S(6)} %copy.8.refs_0_, s32[4,5]{1,0:T(4,128)} %bitcast.9, bf16[256,1024]{1,0:T(8,128)(2,1)} %copy-done.3, bf16[256,1024]{1,0:T(8,128)(2,1)} %copy-done.1, bf16[256,1024]{1,0:T(8,128)(2,1)} %copy-done.2, bf16[256,1024]{1,0:T(8,128)(2,1)} %copy-done.6, ...), custom_call_target="tpu_custom_call" | custom-call | flops 17179869184 | bytes 884736 | tf_op jit(solution)/shard_map/attend_across_same_near/pallas_call | solution.py:418
Async XLA Ops:
  3.4 6.6 %collective-permute-start.4 = (bf16[512,1024]{1,0:T(8,128)(2,1)}, bf16[512,1024]{1,0:T(8,128)(2,1)S(1)}, u32[]{:S(2)}, u32[]{:S(2)}) collective-permute-start(bf16[512,1024]{1,0:T(8,128)(2,1)} %get-tuple-element.34), channel_id=1, source_target_pairs={{0,1},{1,0},{2,3},{3,2},{4,5},{5,4},{6,7},{7,6},{8,9},{9,8},{10,11... | collective-permute-start | bytes 3145736 | tf_op jit(solution)/shard_map/ppermute | solution.py:439
  3.9 23.0 %collective-permute-start = (bf16[256,1024]{1,0:T(8,128)(2,1)}, bf16[256,1024]{1,0:T(8,128)(2,1)S(1)}, u32[]{:S(2)}, u32[]{:S(2)}) collective-permute-start(bf16[256,1024]{1,0:T(8,128)(2,1)} %get-tuple-element.27.refs_2_.refs_15_), channel_id=1, source_target_pairs={{0,2},{1,3},{2,0},{3,1},{4,6},{5,7},{6,4},{7,5},{8,10},{9,11},{10,... | collective-permute-start | bytes 1572872 | tf_op jit(solution)/shard_map/ppermute | solution.py:439
  6.5 21.1 %collective-permute-start.5 = (bf16[128,1024]{1,0:T(8,128)(2,1)}, bf16[128,1024]{1,0:T(8,128)(2,1)S(1)}, u32[]{:S(2)}, u32[]{:S(2)}) collective-permute-start(bf16[128,1024]{1,0:T(8,128)(2,1)} %get-tuple-element.36), channel_id=1, source_target_pairs={{0,8},{8,16},{16,24},{1,9},{9,17},{17,25},{2,10},{10,18},{18,26},{... | collective-permute-start | bytes 786440 | tf_op jit(solution)/shard_map/ppermute | solution.py:439
  10.0 17.0 %copy-start.4 = (bf16[512,1024]{1,0:T(8,128)(2,1)}, bf16[512,1024]{1,0:T(8,128)(2,1)S(1)}, u32[]{:S(2)}) copy-start(bf16[512,1024]{1,0:T(8,128)(2,1)S(1)} %collective-permute-done.4.refs_2_.refs_14_) | copy-start | bytes 3145732
  10.0 17.6 %collective-permute-start.6 = (bf16[128,1024]{1,0:T(8,128)(2,1)}, bf16[128,1024]{1,0:T(8,128)(2,1)S(1)}, u32[]{:S(2)}, u32[]{:S(2)}) collective-permute-start(bf16[128,1024]{1,0:T(8,128)(2,1)} %get-tuple-element.37), channel_id=1, source_target_pairs={{8,0},{16,8},{24,16},{9,1},{17,9},{25,17},{10,2},{18,10},{26,18},{... | collective-permute-start | bytes 786440 | tf_op jit(solution)/shard_map/ppermute | solution.py:439
  11.3 36.2 %collective-permute-start.2 = (bf16[256,1024]{1,0:T(8,128)(2,1)}, bf16[256,1024]{1,0:T(8,128)(2,1)S(1)}, u32[]{:S(2)}, u32[]{:S(2)}) collective-permute-start(bf16[256,1024]{1,0:T(8,128)(2,1)} %get-tuple-element.28.refs_3_.refs_16_), channel_id=1, source_target_pairs={{0,6},{1,7},{2,4},{3,5},{4,2},{5,3},{6,0},{7,1},{8,14},{9,15},{10,... | collective-permute-start | bytes 1572872 | tf_op jit(solution)/shard_map/ppermute | solution.py:439
  12.9 34.6 %collective-permute-start.3 = (bf16[256,1024]{1,0:T(8,128)(2,1)}, bf16[256,1024]{1,0:T(8,128)(2,1)S(1)}, u32[]{:S(2)}, u32[]{:S(2)}) collective-permute-start(bf16[256,1024]{1,0:T(8,128)(2,1)} %get-tuple-element.28.refs_3_.refs_16_), channel_id=1, source_target_pairs={{0,2},{1,3},{2,0},{3,1},{4,6},{5,7},{6,4},{7,5},{8,10},{9,11},{10,... | collective-permute-start | bytes 1572872 | tf_op jit(solution)/shard_map/ppermute | solution.py:439
  27.0 0.8 copy-start
  27.0 20.5 %collective-permute-start.1 = (bf16[256,1024]{1,0:T(8,128)(2,1)S(1)}, bf16[256,1024]{1,0:T(8,128)(2,1)S(1)}, u32[]{:S(2)}, u32[]{:S(2)}) collective-permute-start(bf16[256,1024]{1,0:T(8,128)(2,1)S(1)} %collective-permute-done.refs_3_.refs_17_), channel_id=1, source_target_pairs={{0,4},{1,5},{2,6},{3,7},{4,0},{5,1},{6,2},{7,3},{8,12},{9,13},{10,... | collective-permute-start | bytes 1572872 | tf_op jit(solution)/shard_map/ppermute | solution.py:439
  27.6 0.7 copy-start.7
  28.3 0.7 copy-start.8
  47.5 3.6 %copy-start.1 = (bf16[256,1024]{1,0:T(8,128)(2,1)}, bf16[256,1024]{1,0:T(8,128)(2,1)S(1)}, u32[]{:S(2)}) copy-start(bf16[256,1024]{1,0:T(8,128)(2,1)S(1)} %collective-permute-done.2.refs_3_.refs_20_) | copy-start | bytes 1572868
  47.5 3.6 %copy-start.2 = (bf16[256,1024]{1,0:T(8,128)(2,1)}, bf16[256,1024]{1,0:T(8,128)(2,1)S(1)}, u32[]{:S(2)}) copy-start(bf16[256,1024]{1,0:T(8,128)(2,1)S(1)} %collective-permute-done.3.refs_4_.refs_18_) | copy-start | bytes 1572868
  47.5 3.6 %copy-start.3 = (bf16[256,1024]{1,0:T(8,128)(2,1)}, bf16[256,1024]{1,0:T(8,128)(2,1)S(1)}, u32[]{:S(2)}) copy-start(bf16[256,1024]{1,0:T(8,128)(2,1)S(1)} %collective-permute-done.1.refs_2_.refs_19_) | copy-start | bytes 1572868
  47.6 2.0 collective-permute-start.8
  49.2 2.0 collective-permute-start.7
  49.6 1.6 copy-start.5
  51.2 0.8 copy-start.6

commit v10 on v9

--- a/solution.py
+++ b/solution.py
@@ -17,6 +17,7 @@
 LOG2E = math.log2(math.e)
 SUM_MIN, SUM_MAX = 2.0**-60, 2.0**100
 VMEM_LIMIT = 60 * 1024 * 1024
+STAGE_VMEM = 57 * 1024 * 1024
 CHUNKS = 4
 
 epsilon = 1e-05
@@ -31,8 +32,8 @@
 
 
 def norm_kernel(bands, tokens_hbm, gain_hbm, halo_rows_hbm, *refs):
-    outs = refs[: PARTS + 3]
-    tokens_ref, gain_ref, halo_rows_ref, normed_ref, edge_ref, in_sem, out_sem = refs[PARTS + 3 :]
+    outs = refs[: PARTS + 2]
+    tokens_ref, gain_ref, halo_rows_ref, normed_ref, edge_ref, in_sem, out_sem = refs[PARTS + 2 :]
     rows = tokens_ref.shape[0]
     block = rows // CHUNKS
 
@@ -75,9 +76,8 @@
             picks, normed_ref[...], (((0,), (0,)), ((), ())), preferred_element_type=jnp.float32
         )
         edge_ref[which] = picked.astype(jnp.bfloat16)
-        place = PARTS + 1 + which
-        sent.append(pltpu.make_async_copy(edge_ref.at[which], outs[place], out_sem.at[place]))
-        sent[-1].start()
+    sent.append(pltpu.make_async_copy(edge_ref, outs[PARTS + 1], out_sem.at[PARTS + 1]))
+    sent[-1].start()
     for copy in sent:
         copy.wait()
 
@@ -87,12 +87,12 @@
     bands, _, halo = halo_rows.shape
     part = jax.ShapeDtypeStruct((rows // PARTS, width), jnp.bfloat16)
     whole = jax.ShapeDtypeStruct((rows, width), jnp.bfloat16)
-    edge = jax.ShapeDtypeStruct((halo, width), jnp.bfloat16)
+    edge = jax.ShapeDtypeStruct((2, halo, width), jnp.bfloat16)
     return pl.pallas_call(
         functools.partial(norm_kernel, bands),
-        out_shape=[part] * PARTS + [whole] + [edge] * 2,
+        out_shape=[part] * PARTS + [whole, edge],
         in_specs=[pl.BlockSpec(memory_space=pl.ANY)] * 3,
-        out_specs=[pl.BlockSpec(memory_space=pltpu.HBM)] * (PARTS + 3),
+        out_specs=[pl.BlockSpec(memory_space=pltpu.HBM)] * (PARTS + 2),
         scratch_shapes=[
             pltpu.VMEM((rows, width), jnp.float32),
             pltpu.VMEM((1, width), jnp.float32),
@@ -100,7 +100,7 @@
             pltpu.VMEM((rows, width), jnp.bfloat16),
             pltpu.VMEM((2, halo, width), jnp.bfloat16),
             pltpu.SemaphoreType.DMA((CHUNKS + 2,)),
-            pltpu.SemaphoreType.DMA((PARTS + 3,)),
+            pltpu.SemaphoreType.DMA((PARTS + 2,)),
         ],
         compiler_params=pltpu.CompilerParams(vmem_limit_bytes=VMEM_LIMIT),
         cost_estimate=pl.CostEstimate(flops=10 * rows * width, bytes_accessed=6 * rows * width, transcendentals=0),
@@ -199,14 +199,15 @@
 
     counts_ref, mask_ref = take(2)
     sector_refs = [take(len(starts)) for starts in part_starts]
-    halo_refs = take(2) if halos else []
+    edges_hbm = take(1)[0] if halos else None
     wq_ref = take(1)[0] if first else None
     wk_ref, wv_ref = take(2)
     if not first:
         query_in, acc_in, sum_in = take(3)
     if last:
         tokens_ref, wo_ref = take(2)
-        all_refs = take(1 + 4 * PARTS + 2)
+        all_refs = take(1 + 4 * PARTS)
+        (all_edges,) = take(1)
         (out_ref,) = take(1)
     else:
         if first:
@@ -214,6 +215,8 @@
         acc_out, sum_out = take(2)
     key_ref, value_ref, ones_ref = take(3)
     score_refs, weight_refs = take(2), take(2)
+    if halos:
+        halo_ref, halo_sem = take(2)
     if last:
         res_ref, att_ref, acc_out, sum_out = take(4)
 
@@ -222,6 +225,19 @@
     bands = lax.axis_size("lat")
     columns = sector_columns(lon, reach)
     count = counts_ref[0]
+
+    lists = ((jnp.maximum(lat - 1, 0), 1, lat > 0), (jnp.minimum(lat + 1, bands - 1), 0, lat < bands - 1))
+    halo_copies = []
+    if halos:
+        halo_copies = [
+            pltpu.make_async_copy(edges_hbm.at[band, side], halo_ref.at[i], halo_sem.at[i])
+            for i, (band, side, _) in enumerate(lists)
+        ]
+
+        @pl.when(pl.program_id(0) == 0)
+        def _():
+            for copy in halo_copies:
+                copy.start()
 
     wk, wv = wk_ref[...], wv_ref[...]
     if first:
@@ -250,14 +266,20 @@
             at += size
         spans.append((begin, at))
         biases.append(None if name == "own" else block_bias(mask_ref, columns[name], rows, jnp.bfloat16))
-    if halo_refs:
+    if halos:
+
+        @pl.when(pl.program_id(0) == 0)
+        def _():
+            for copy in halo_copies:
+                copy.wait()
+
         begin = at
-        for ref, seen in zip(halo_refs, (lat > 0, lat < bands - 1)):
-            size = ref.shape[0]
+        for i, (_, _, seen) in enumerate(lists):
+            size = halo_ref.shape[1]
             here = pl.ds(at, size)
             there = jnp.where(seen, 1.0, 0.0)
-            key_ref[:, here] = matmul(ref[...], wk).astype(jnp.bfloat16).T
-            value_ref[here] = (matmul(ref[...], wv) * there).astype(jnp.bfloat16)
+            key_ref[:, here] = matmul(halo_ref[i], wk).astype(jnp.bfloat16).T
+            value_ref[here] = (matmul(halo_ref[i], wv) * there).astype(jnp.bfloat16)
             ones_ref[here] = jnp.full((size, LANES), there, jnp.float32).astype(jnp.bfloat16)
             at += size
         spans.append((begin, at))
@@ -323,8 +345,8 @@
         for s, name in enumerate(("own", "same", "across", "near")):
             for i, ref in enumerate(all_refs[1 + s * PARTS : 1 + (s + 1) * PARTS]):
                 sources.append((ref, columns[name], None, i * part))
-        for ref, seen in zip(all_refs[1 + 4 * PARTS :], (lat > 0, lat < bands - 1)):
-            sources.append((ref, None, seen, 0))
+        for band, side, seen in lists:
+            sources.append((all_edges.at[band, side], None, seen, 0))
         att_ref[...] = safe_group(query, (wk_ref, wv_ref), sources, counts_ref, mask_ref, refs, head_size)
 
     step = pl.program_id(0)
@@ -362,16 +384,18 @@
     for parts in sector_parts:
         args += parts
         specs += [fixed(p.shape) for p in parts]
-    for halo in halos:
-        args.append(halo)
-        specs.append(fixed(halo.shape))
+    if halos is not None:
+        args.append(halos)
+        specs.append(pl.BlockSpec(memory_space=pl.ANY))
     for third in range(0 if first else 1, 3):
         args.append(qkv_weight)
         specs.append(weight(third))
     if not first:
         args += [query, *state]
         specs += [columns] * 3
-    keys = sum(p.shape[0] for parts in sector_parts for p in parts) + sum(h.shape[0] for h in halos)
+    keys = sum(p.shape[0] for parts in sector_parts for p in parts)
+    if halos is not None:
+        keys += 2 * halos.shape[2]
     scratch = [
         pltpu.VMEM((GROUP, keys), jnp.bfloat16),
         pltpu.VMEM((keys, GROUP), jnp.bfloat16),
@@ -381,6 +405,8 @@
         pltpu.VMEM((2 * rows, keys), jnp.bfloat16),
         pltpu.VMEM((2 * rows, keys), jnp.bfloat16),
     ]
+    if halos is not None:
+        scratch += [pltpu.VMEM((2, *halos.shape[2:]), jnp.bfloat16), pltpu.SemaphoreType.DMA((2,))]
     wide = jax.ShapeDtypeStruct((rows, width), jnp.float32)
     moved = sum(a.size * a.dtype.itemsize for a in args[2:] if a is not qkv_weight) + 3 * model * width * 2
     if last:
@@ -391,7 +417,7 @@
         out_shape = [wide]
         out_specs = [fixed((rows, width))]
         part = rows // PARTS
-        tiles = len(sources) + PARTS - 1
+        tiles = len(sources) + PARTS
         scratch += [
             pltpu.VMEM((rows, width), jnp.float32),
             pltpu.VMEM((rows, GROUP), jnp.bfloat16),
@@ -416,13 +442,13 @@
     flops = 2 * keys * model * 2 * width + 16 * rows * keys * width
     flops += 2 * rows * model * width * (int(first) + int(last))
     outs = pl.pallas_call(
-        functools.partial(stage_kernel, (first, last, sectors, starts, bool(halos), head_size)),
+        functools.partial(stage_kernel, (first, last, sectors, starts, halos is not None, head_size)),
         out_shape=out_shape,
         grid=(steps,),
         in_specs=specs,
         out_specs=out_specs,
         scratch_shapes=scratch,
-        compiler_params=pltpu.CompilerParams(vmem_limit_bytes=VMEM_LIMIT),
+        compiler_params=pltpu.CompilerParams(vmem_limit_bytes=VMEM_LIMIT if first else STAGE_VMEM),
         cost_estimate=pl.CostEstimate(flops=flops // (16 if first else 1), bytes_accessed=moved // 16, transcendentals=0),
         name="attend_" + "_".join(sectors),
     )(*args)
@@ -446,18 +472,14 @@
     local = tokens[0, 0]
     rows = local.shape[0]
     outs = norm_call(local, norm_gain, halo_rows)
-    own, (whole, north_rows, south_rows) = outs[:PARTS], outs[PARTS:]
+    own, (whole, edges) = outs[:PARTS], outs[PARTS:]
     assert PARTS == 2
 
     partner = permuted([whole], "lon", lambda i: i ^ 1)
     same = permuted(own[:1], "lon", lambda i: i ^ 2)
     across = permuted(own[1:], "lon", lambda i: (i + (-2 if (i // 2) % 2 == 0 else 2)) % ring)
     same += permuted(own[1:], "lon", lambda i: i ^ 2)
-    north_rows, *partner = lax.optimization_barrier((north_rows, *partner))
-    halos = [
-        permuted([south_rows], "lat", lambda b: b + 1)[0],
-        permuted([north_rows], "lat", lambda b: b - 1)[0],
-    ]
+    halos = lax.all_gather(edges, "lat")
     lon = lax.axis_index("lon")
     gives_same = lon % 2 == (lon // 2) % 2
 
@@ -466,7 +488,7 @@
 
     stage = functools.partial(stage_call, rows // mask.shape[0], band_counts, mask)
     half = rows // PARTS
-    query, state = stage(["own"], [own], [], qkv_weight, starts=[[0, half]])
+    query, state = stage(["own"], [own], None, qkv_weight, starts=[[0, half]])
 
     same[0], query, state = lax.optimization_barrier((same[0], query, state))
     across = permuted(same[:1], "lon", lambda i: (i + (4 if (i // 2) % 2 == 0 else -4)) % ring) + across
@@ -476,8 +498,8 @@
     *rest, state = lax.optimization_barrier((*across, *same, state))
     across, same = rest[:PARTS], rest[PARTS:]
     near = [swapped(s, a) for s, a in zip(same, across)]
-    final = (local, out_weight, [*partner, *own, *same, *across, *near, *halos])
-    late = [["across", "same", "near"], [across, same[1:], near], [], qkv_weight, query, state, final]
+    final = (local, out_weight, [*partner, *own, *same, *across, *near, halos])
+    late = [["across", "same", "near"], [across, same[1:], near], None, qkv_weight, query, state, final]
     result = stage(*late, starts=[[0, half], [half], [0, half]])
     return result[None, None]
 

time: 247 us -> 285 us (1.15)
  waiting for transfers between devices: 1.91 us -> 31.4 us
  between operations: 0.98 us -> 14.2 us
  starting transfers between devices: 11.6 us -> 6.75 us
    all_gather x0 -> x1, waiting for transfers between devices: none -> 29.5 us  [on_device(): halos = lax.all_gather(edges, 'lat')]
    ppermute x9 -> x7, starting transfers between devices: 11.6 us -> 6.75 us  [permuted(): return [lax.ppermute(v, axis, pairs) for v in values]]
  transfers between devices with their start and end apart: 9 -> 8, of which waited for: 2 -> 3; matrix products, arithmetic and copies ran while one was open for 1% -> 1% of each run, Pallas kernels for 12% -> 11%
where the time goes in v10:
time: 285 us; the launch traced here: 284 us
  Pallas kernels  229 us (80%)
  waiting for transfers between devices  31.4 us (11%)
  between operations  14.2 us (5%)
  starting transfers between devices  6.75 us (2%)
    pallas_call x3, Pallas kernels, stage_call(): pl.pallas_call(functools.partial(stage_kernel, (first, last, sectors, sta...  225 us
    all_gather x1, waiting for transfers between devices, on_device(): halos = lax.all_gather(edges, 'lat')  29.5 us
    ppermute x7, starting transfers between devices, permuted(): return [lax.ppermute(v, axis, pairs) for v in values]  6.75 us
  transfers between devices with their start and end apart: 8, of which 3 were waited for; matrix products, arithmetic and copies ran while one was open for 1% of the time, Pallas kernels for 11%

profile of v10, /device:TPU:0, one launch (start us, length us, event | category | flops | bytes accessed | tf_op | source)
XLA Modules:
  0.0 283.5 jit_solution(10659940747033483957)
XLA Ops:
  6.5 0.0 all-gather.3.cloned.1.call-start
  6.5 3.4 %layer_norm.1 = (bf16[256,1024]{1,0:T(8,128)(2,1)}, bf16[256,1024]{1,0:T(8,128)(2,1)}, bf16[512,1024]{1,0:T(8,128)(2,1)}, bf16[2,128,1024]{2,1,0:T(8,128)(2,1)}) custom-call(f32[512,1024]{1,0:T(8,128)} %bitcast.5, f32[1,1024]{1,0:T(1,128)} %bitcast.7, s32[4,2,128]{2,1,0:T(2,128)} %halo_rows_hbm.1), custom_call_target="tpu_custom_call" | custom-call | flops 5242880 | bytes 3145728 | tf_op jit(solution)/shard_map/layer_norm/pallas_call | solution.py:91
  9.9 0.0 all-gather.3.cloned.1.call-update
  10.0 0.5 collective-permute-start.4
  10.5 2.6 collective-permute-start
  13.1 1.5 collective-permute-start.2
  14.5 1.5 collective-permute-start.3
  16.7 12.0 %attend_own.1 = (bf16[512,1024]{1,0:T(8,128)(2,1)}, f32[512,1024]{1,0:T(8,128)}, f32[512,1024]{1,0:T(8,128)}) custom-call(s32[1]{0:T(128)S(6)} %copy.8.refs_0_, s32[4,5]{1,0:T(4,128)} %bitcast.8, bf16[256,1024]{1,0:T(8,128)(2,1)} %get-tuple-element.24.refs_2_.refs_15_, bf16[256,1024]{1,0:T(8,128)(2,1)} %get-tuple-element.25.refs_3_.refs_16_, ...), custom_call_target="tpu_custom_call" | custom-call | flops 469762048 | bytes 458752 | tf_op jit(solution)/shard_map/attend_own/pallas_call | solution.py:444
  28.7 0.0 collective-permute-done.refs_3_.refs_17_
  28.7 0.0 copy-start
  28.7 0.5 collective-permute-start.1
  29.3 0.0 collective-permute-done.4.refs_2_.refs_14_
  29.3 0.0 copy-start.4
  29.3 29.5 %all-gather.3.cloned.1.call-done = bf16[8,128,1024]{2,1,0:T(8,128)(2,1)} async-done(((bf16[2,128,1024]{2,1,0:T(8,128)(2,1)}), bf16[8,128,1024]{2,1,0:T(8,128)(2,1)}) %all-gather.3.cloned.1.call-update) | async-done | bytes 2097168 | tf_op jit(solution)/shard_map/all_gather | solution.py:482
  58.8 0.0 copy-done
  58.8 0.0 copy-done.4
  58.8 19.6 %attend_partner_same.1 = (f32[512,1024]{1,0:T(8,128)}, f32[512,1024]{1,0:T(8,128)}) custom-call(s32[1]{0:T(128)S(6)} %copy.8.refs_0_, s32[4,5]{1,0:T(4,128)} %bitcast.9, bf16[512,1024]{1,0:T(8,128)(2,1)} %copy-done.4, bf16[256,1024]{1,0:T(8,128)(2,1)} %copy-done, bf16[4,2,128,1024]{3,2,1,0:T(8,128)(2,1)} %bitcast.11, bf16[1024,3072]{1,0:T(8,128)(2,1)} %refs_8_.1, ...), custom_call_target="tpu_custom_call" | custom-call | flops 12884901888 | bytes 950272 | tf_op jit(solution)/shard_map/attend_partner_same/pallas_call | solution.py:444
  78.4 0.0 collective-permute-done.2.refs_3_.refs_20_
  78.4 0.0 copy-start.1
  78.4 0.0 collective-permute-done.3.refs_4_.refs_18_
  78.4 0.0 copy-start.2
  78.4 0.0 collective-permute-done.1.refs_2_.refs_19_
  78.4 0.0 copy-start.3
  78.4 0.1 broadcast_select_fusion
  78.5 0.1 collective-permute-start.6
  78.6 1.5 broadcast_select_fusion.1
  80.0 0.1 collective-permute-start.5
  80.1 0.3 collective-permute-done.6.refs_6_.refs_22_
  80.5 0.0 copy-start.5
  80.5 1.6 collective-permute-done.5.refs_5_.refs_21_
  82.0 0.0 copy-done.1
  82.0 0.0 copy-done.2
  82.0 0.0 copy-done.3
  82.0 0.0 copy-done.5
  82.0 0.0 copy-start.6
  82.1 0.8 copy-done.6
  82.9 193.8 %attend_across_same_near.1 = f32[512,1024]{1,0:T(8,128)} custom-call(s32[1]{0:T(128)S(6)} %copy.8.refs_0_, s32[4,5]{1,0:T(4,128)} %bitcast.10, bf16[256,1024]{1,0:T(8,128)(2,1)} %copy-done.3, bf16[256,1024]{1,0:T(8,128)(2,1)} %copy-done.1, bf16[256,1024]{1,0:T(8,128)(2,1)} %copy-done.2, bf16[256,1024]{1,0:T(8,128)(2,1)} %copy-done.6, ...), custom_call_target="tpu_custom_call" | custom-call | flops 17179869184 | bytes 884736 | tf_op jit(solution)/shard_map/attend_across_same_near/pallas_call | solution.py:444
Async XLA Ops:
  6.5 52.2 %all-gather.3.cloned.1.call-start = ((), (), s32[]{:S(2)}) async-start(), calls=%async_computation | async-start | bytes 2621440 | tf_op jit(solution)/shard_map/all_gather | solution.py:482
  10.0 19.3 %collective-permute-start.4 = (bf16[512,1024]{1,0:T(8,128)(2,1)}, bf16[512,1024]{1,0:T(8,128)(2,1)S(1)}, u32[]{:S(2)}, u32[]{:S(2)}) collective-permute-start(bf16[512,1024]{1,0:T(8,128)(2,1)} %get-tuple-element.30), channel_id=1, source_target_pairs={{0,1},{1,0},{2,3},{3,2},{4,5},{5,4},{6,7},{7,6},{8,9},{9,8},{10,11... | collective-permute-start | bytes 3145736 | tf_op jit(solution)/shard_map/ppermute | solution.py:465
  10.5 18.2 %collective-permute-start = (bf16[256,1024]{1,0:T(8,128)(2,1)}, bf16[256,1024]{1,0:T(8,128)(2,1)S(1)}, u32[]{:S(2)}, u32[]{:S(2)}) collective-permute-start(bf16[256,1024]{1,0:T(8,128)(2,1)} %get-tuple-element.24.refs_2_.refs_15_), channel_id=1, source_target_pairs={{0,2},{1,3},{2,0},{3,1},{4,6},{5,7},{6,4},{7,5},{8,10},{9,11},{10,... | collective-permute-start | bytes 1572872 | tf_op jit(solution)/shard_map/ppermute | solution.py:465
  13.1 65.3 %collective-permute-start.2 = (bf16[256,1024]{1,0:T(8,128)(2,1)}, bf16[256,1024]{1,0:T(8,128)(2,1)S(1)}, u32[]{:S(2)}, u32[]{:S(2)}) collective-permute-start(bf16[256,1024]{1,0:T(8,128)(2,1)} %get-tuple-element.25.refs_3_.refs_16_), channel_id=1, source_target_pairs={{0,6},{1,7},{2,4},{3,5},{4,2},{5,3},{6,0},{7,1},{8,14},{9,15},{10,... | collective-permute-start | bytes 1572872 | tf_op jit(solution)/shard_map/ppermute | solution.py:465
  14.5 63.8 %collective-permute-start.3 = (bf16[256,1024]{1,0:T(8,128)(2,1)}, bf16[256,1024]{1,0:T(8,128)(2,1)S(1)}, u32[]{:S(2)}, u32[]{:S(2)}) collective-permute-start(bf16[256,1024]{1,0:T(8,128)(2,1)} %get-tuple-element.25.refs_3_.refs_16_), channel_id=1, source_target_pairs={{0,2},{1,3},{2,0},{3,1},{4,6},{5,7},{6,4},{7,5},{8,10},{9,11},{10,... | collective-permute-start | bytes 1572872 | tf_op jit(solution)/shard_map/ppermute | solution.py:465
  28.7 30.1 %copy-start = (bf16[256,1024]{1,0:T(8,128)(2,1)}, bf16[256,1024]{1,0:T(8,128)(2,1)S(1)}, u32[]{:S(2)}) copy-start(bf16[256,1024]{1,0:T(8,128)(2,1)S(1)} %collective-permute-done.refs_3_.refs_17_) | copy-start | bytes 1572868
  28.7 49.7 %collective-permute-start.1 = (bf16[256,1024]{1,0:T(8,128)(2,1)S(1)}, bf16[256,1024]{1,0:T(8,128)(2,1)S(1)}, u32[]{:S(2)}, u32[]{:S(2)}) collective-permute-start(bf16[256,1024]{1,0:T(8,128)(2,1)S(1)} %collective-permute-done.refs_3_.refs_17_), channel_id=1, source_target_pairs={{0,4},{1,5},{2,6},{3,7},{4,0},{5,1},{6,2},{7,3},{8,12},{9,13},{10,... | collective-permute-start | bytes 1572872 | tf_op jit(solution)/shard_map/ppermute | solution.py:465
  29.3 29.5 %copy-start.4 = (bf16[512,1024]{1,0:T(8,128)(2,1)}, bf16[512,1024]{1,0:T(8,128)(2,1)S(1)}, u32[]{:S(2)}) copy-start(bf16[512,1024]{1,0:T(8,128)(2,1)S(1)} %collective-permute-done.4.refs_2_.refs_14_) | copy-start | bytes 3145732
  78.4 3.6 %copy-start.1 = (bf16[256,1024]{1,0:T(8,128)(2,1)}, bf16[256,1024]{1,0:T(8,128)(2,1)S(1)}, u32[]{:S(2)}) copy-start(bf16[256,1024]{1,0:T(8,128)(2,1)S(1)} %collective-permute-done.2.refs_3_.refs_20_) | copy-start | bytes 1572868
  78.4 3.6 %copy-start.2 = (bf16[256,1024]{1,0:T(8,128)(2,1)}, bf16[256,1024]{1,0:T(8,128)(2,1)S(1)}, u32[]{:S(2)}) copy-start(bf16[256,1024]{1,0:T(8,128)(2,1)S(1)} %collective-permute-done.3.refs_4_.refs_18_) | copy-start | bytes 1572868
  78.4 3.6 %copy-start.3 = (bf16[256,1024]{1,0:T(8,128)(2,1)}, bf16[256,1024]{1,0:T(8,128)(2,1)S(1)}, u32[]{:S(2)}) copy-start(bf16[256,1024]{1,0:T(8,128)(2,1)S(1)} %collective-permute-done.1.refs_2_.refs_19_) | copy-start | bytes 1572868
  78.5 2.0 collective-permute-start.6
  80.0 2.0 collective-permute-start.5
  80.5 1.6 copy-start.5
  82.0 0.8 copy-start.6
Sparse Core Ops, SparseCore 0:
  10.1 48.6 all-gather.2

commit v11 on v9

--- a/solution.py
+++ b/solution.py
@@ -66,9 +66,14 @@
     sent[-1].start()
     small[1].wait()
     band = lax.axis_index("lat")
-    lists = ((jnp.maximum(band - 1, 0), 1), (jnp.minimum(band + 1, bands - 1), 0))
+    even = band % 2 == 0
+    south, north = jnp.minimum(band + 1, bands - 1), jnp.maximum(band - 1, 0)
+    lists = (
+        (jnp.where(even, south, north), jnp.where(even, 0, 1)),
+        (jnp.where(even, north, south), jnp.where(even, 1, 0)),
+    )
     for which, (owner, side) in enumerate(lists):
-        wanted = halo_rows_ref[pl.ds(owner, 1), side, :]
+        wanted = halo_rows_ref[pl.ds(2 * owner + side, 1), :]
         slots = lax.broadcasted_iota(jnp.int32, (rows, wanted.shape[1]), 0)
         picks = (slots == wanted).astype(jnp.float32).astype(jnp.bfloat16)
         picked = lax.dot_general(
@@ -85,6 +90,7 @@
 def norm_call(tokens, gain, halo_rows):
     rows, width = tokens.shape
     bands, _, halo = halo_rows.shape
+    halo_rows = halo_rows.reshape(2 * bands, halo)
     part = jax.ShapeDtypeStruct((rows // PARTS, width), jnp.bfloat16)
     whole = jax.ShapeDtypeStruct((rows, width), jnp.bfloat16)
     edge = jax.ShapeDtypeStruct((halo, width), jnp.bfloat16)
@@ -215,11 +221,13 @@
     key_ref, value_ref, ones_ref = take(3)
     score_refs, weight_refs = take(2), take(2)
     if last:
-        res_ref, att_ref, acc_out, sum_out = take(4)
+        res_ref, att_ref, acc_out, sum_out, out_sem = take(5)
 
     reach = mask_ref.shape[1] // 2
     lon, lat = lax.axis_index("lon"), lax.axis_index("lat")
     bands = lax.axis_size("lat")
+    north_there, south_there, even = lat > 0, lat < bands - 1, lat % 2 == 0
+    halo_seen = (even & south_there | ~even & north_there, even & north_there | ~even & south_there)
     columns = sector_columns(lon, reach)
     count = counts_ref[0]
 
@@ -252,7 +260,7 @@
         biases.append(None if name == "own" else block_bias(mask_ref, columns[name], rows, jnp.bfloat16))
     if halo_refs:
         begin = at
-        for ref, seen in zip(halo_refs, (lat > 0, lat < bands - 1)):
+        for ref, seen in zip(halo_refs, halo_seen):
             size = ref.shape[0]
             here = pl.ds(at, size)
             there = jnp.where(seen, 1.0, 0.0)
@@ -323,7 +331,7 @@
         for s, name in enumerate(("own", "same", "across", "near")):
             for i, ref in enumerate(all_refs[1 + s * PARTS : 1 + (s + 1) * PARTS]):
                 sources.append((ref, columns[name], None, i * part))
-        for ref, seen in zip(all_refs[1 + 4 * PARTS :], (lat > 0, lat < bands - 1)):
+        for ref, seen in zip(all_refs[1 + 4 * PARTS :], halo_seen):
             sources.append((ref, None, seen, 0))
         att_ref[...] = safe_group(query, (wk_ref, wv_ref), sources, counts_ref, mask_ref, refs, head_size)
 
@@ -335,12 +343,25 @@
 
     at = pl.ds(pl.multiple_of(step * width, width), width)
     res_ref[:, at] += tokens_ref[...]
-    res_ref[...] += matmul(att_ref[...], wo_ref[...])
-
-    @pl.when(step == pl.num_programs(0) - 1)
+    last_step = step == pl.num_programs(0) - 1
+
+    @pl.when(~last_step)
     def _():
-        slot = lax.broadcasted_iota(jnp.int32, res_ref.shape, 0)
-        out_ref[...] = jnp.where(slot < count, res_ref[...], 0.0)
+        res_ref[...] += matmul(att_ref[...], wo_ref[...])
+
+    @pl.when(last_step)
+    def _():
+        size = res_ref.shape[1] // out_sem.shape[0]
+        live = lax.broadcasted_iota(jnp.int32, (rows, size), 0) < count
+        copies = []
+        for n in range(out_sem.shape[0]):
+            block = pl.ds(n * size, size)
+            result = res_ref[:, block] + matmul(att_ref[...], wo_ref[:, block])
+            res_ref[:, block] = jnp.where(live, result, 0.0)
+            copies.append(pltpu.make_async_copy(res_ref.at[:, block], out_ref.at[:, block], out_sem.at[n]))
+            copies[-1].start()
+        for copy in copies:
+            copy.wait()
 
 
 def stage_call(block_rows, counts, mask, sectors, sector_parts, halos, qkv_weight, query=None, state=None, final=None, starts=None):
@@ -389,7 +410,7 @@
         specs += [columns, pl.BlockSpec((GROUP, out_weight.shape[1]), lambda g: (g, 0))]
         specs += [pl.BlockSpec(memory_space=pl.ANY)] * len(sources)
         out_shape = [wide]
-        out_specs = [fixed((rows, width))]
+        out_specs = [pl.BlockSpec(memory_space=pl.ANY)]
         part = rows // PARTS
         tiles = len(sources) + PARTS - 1
         scratch += [
@@ -397,6 +418,7 @@
             pltpu.VMEM((rows, GROUP), jnp.bfloat16),
             pltpu.VMEM((rows, GROUP), jnp.float32),
             pltpu.VMEM((rows, GROUP), jnp.float32),
+            pltpu.SemaphoreType.DMA((4,)),
             pltpu.VMEM((part, model), jnp.bfloat16),
             pltpu.VMEM((part * tiles, GROUP), jnp.bfloat16),
             pltpu.VMEM((part * tiles, GROUP), jnp.bfloat16),
@@ -446,17 +468,17 @@
     local = tokens[0, 0]
     rows = local.shape[0]
     outs = norm_call(local, norm_gain, halo_rows)
-    own, (whole, north_rows, south_rows) = outs[:PARTS], outs[PARTS:]
+    own, (whole, first_rows, second_rows) = outs[:PARTS], outs[PARTS:]
     assert PARTS == 2
 
     partner = permuted([whole], "lon", lambda i: i ^ 1)
     same = permuted(own[:1], "lon", lambda i: i ^ 2)
     across = permuted(own[1:], "lon", lambda i: (i + (-2 if (i // 2) % 2 == 0 else 2)) % ring)
     same += permuted(own[1:], "lon", lambda i: i ^ 2)
-    north_rows, *partner = lax.optimization_barrier((north_rows, *partner))
+    second_rows, *partner = lax.optimization_barrier((second_rows, *partner))
     halos = [
-        permuted([south_rows], "lat", lambda b: b + 1)[0],
-        permuted([north_rows], "lat", lambda b: b - 1)[0],
+        permuted([first_rows], "lat", lambda b: b ^ 1)[0],
+        permuted([second_rows], "lat", lambda b: ((b + 1) ^ 1) - 1)[0],
     ]
     lon = lax.axis_index("lon")
     gives_same = lon % 2 == (lon // 2) % 2

time: 247 us -> 246 us (level)
  starting transfers between devices: 11.6 us -> 9.09 us
    ppermute x9, starting transfers between devices: 11.6 us -> 9.09 us  [permuted(): return [lax.ppermute(v, axis, pairs) for v in values]]
  transfers between devices with their start and end apart: 9 -> 9, of which waited for: 2 -> 2; matrix products, arithmetic and copies ran while one was open for 1% -> 1% of each run, Pallas kernels for 12% -> 13%
where the time goes in v11:
time: 246 us; the launch traced here: 243 us
  Pallas kernels  227 us (92%)
  starting transfers between devices  9.09 us (4%)
    pallas_call x3, Pallas kernels, stage_call(): pl.pallas_call(functools.partial(stage_kernel, (first, last, sectors, sta...  224 us
    ppermute x9, starting transfers between devices, permuted(): return [lax.ppermute(v, axis, pairs) for v in values]  9.09 us
  transfers between devices with their start and end apart: 9, of which 2 were waited for; matrix products, arithmetic and copies ran while one was open for 1% of the time, Pallas kernels for 13%

profile of v11, /device:TPU:0, one launch (start us, length us, event | category | flops | bytes accessed | tf_op | source)
XLA Modules:
  0.0 243.0 jit_solution(18191244891849221354)
XLA Ops:
  0.0 3.4 %layer_norm.1 = (bf16[256,1024]{1,0:T(8,128)(2,1)}, bf16[256,1024]{1,0:T(8,128)(2,1)}, bf16[512,1024]{1,0:T(8,128)(2,1)}, bf16[128,1024]{1,0:T(8,128)(2,1)}, bf16[128,1024]{1,0:T(8,128)(2,1)}) custom-call(f32[512,1024]{1,0:T(8,128)} %bitcast.5, f32[1,1024]{1,0:T(1,128)} %bitcast.7, s32[8,128]{1,0:T(8,128)} %bitcast.8), custom_call_target="tpu_custom_call" | custom-call | flops 5242880 | bytes 3145728 | tf_op jit(solution)/shard_map/layer_norm/pallas_call | solution.py:97
  3.4 0.5 collective-permute-start.4
  3.9 2.6 %collective-permute-start = (bf16[256,1024]{1,0:T(8,128)(2,1)}, bf16[256,1024]{1,0:T(8,128)(2,1)S(1)}, u32[]{:S(2)}, u32[]{:S(2)}) collective-permute-start(bf16[256,1024]{1,0:T(8,128)(2,1)} %get-tuple-element.27.refs_2_.refs_15_), channel_id=1, source_target_pairs={{0,2},{1,3},{2,0},{3,1},{4,6},{5,7},{6,4},{7,5},{8,10},{9,11},{10,... | collective-permute-start | bytes 1572872 | tf_op jit(solution)/shard_map/ppermute | solution.py:461
  6.5 1.6 collective-permute-start.5
  8.1 0.0 collective-permute-done.4.refs_2_.refs_14_
  8.1 0.0 copy-start.4
  8.1 0.7 collective-permute-start.6
  8.8 2.2 collective-permute-start.2
  11.0 0.8 collective-permute-start.3
  12.5 11.9 %attend_own.1 = (bf16[512,1024]{1,0:T(8,128)(2,1)}, f32[512,1024]{1,0:T(8,128)}, f32[512,1024]{1,0:T(8,128)}) custom-call(s32[1]{0:T(128)S(6)} %copy.8.refs_0_, s32[4,5]{1,0:T(4,128)} %bitcast.9, bf16[256,1024]{1,0:T(8,128)(2,1)} %get-tuple-element.27.refs_2_.refs_15_, bf16[256,1024]{1,0:T(8,128)(2,1)} %get-tuple-element.28.refs_3_.refs_16_, ...), custom_call_target="tpu_custom_call" | custom-call | flops 469762048 | bytes 458752 | tf_op jit(solution)/shard_map/attend_own/pallas_call | solution.py:440
  24.4 0.0 copy-done.4
  24.4 0.0 collective-permute-done.refs_3_.refs_17_
  24.4 0.0 copy-start
  24.4 0.6 collective-permute-start.1
  25.0 0.0 collective-permute-done.5.refs_4_.refs_23_
  25.0 0.0 copy-start.7
  25.0 0.0 collective-permute-done.6.refs_5_.refs_24_
  25.0 0.2 copy-done
  25.2 0.5 copy-done.7
  25.7 0.0 copy-start.8
  25.7 0.7 copy-done.8
  26.4 18.5 %attend_partner_same.1 = (f32[512,1024]{1,0:T(8,128)}, f32[512,1024]{1,0:T(8,128)}) custom-call(s32[1]{0:T(128)S(6)} %copy.8.refs_0_, s32[4,5]{1,0:T(4,128)} %bitcast.10, bf16[512,1024]{1,0:T(8,128)(2,1)} %copy-done.4, bf16[256,1024]{1,0:T(8,128)(2,1)} %copy-done, bf16[128,1024]{1,0:T(8,128)(2,1)} %copy-done.7, bf16[128,1024]{1,0:T(8,128)(2,1)} %copy-done.8, ...), custom_call_target="tpu_custom_call" | custom-call | flops 12884901888 | bytes 851968 | tf_op jit(solution)/shard_map/attend_partner_same/pallas_call | solution.py:440
  44.9 0.0 collective-permute-done.2.refs_3_.refs_20_
  44.9 0.0 copy-start.1
  44.9 0.0 collective-permute-done.3.refs_4_.refs_18_
  44.9 0.0 copy-start.2
  45.0 0.0 collective-permute-done.1.refs_2_.refs_19_
  45.0 0.0 copy-start.3
  45.0 0.1 broadcast_select_fusion
  45.0 0.1 collective-permute-start.8
  45.1 1.5 broadcast_select_fusion.1
  46.6 0.1 collective-permute-start.7
  46.7 0.3 collective-permute-done.8.refs_6_.refs_22_
  47.0 0.0 copy-start.5
  47.0 1.6 collective-permute-done.7.refs_5_.refs_21_
  48.6 0.0 copy-done.1
  48.6 0.0 copy-done.2
  48.6 0.0 copy-done.3
  48.6 0.0 copy-done.5
  48.6 0.0 copy-start.6
  48.6 0.8 copy-done.6
  49.4 193.4 %attend_across_same_near.1 = f32[512,1024]{1,0:T(8,128)} custom-call(s32[1]{0:T(128)S(6)} %copy.8.refs_0_, s32[4,5]{1,0:T(4,128)} %bitcast.11, bf16[256,1024]{1,0:T(8,128)(2,1)} %copy-done.3, bf16[256,1024]{1,0:T(8,128)(2,1)} %copy-done.1, bf16[256,1024]{1,0:T(8,128)(2,1)} %copy-done.2, bf16[256,1024]{1,0:T(8,128)(2,1)} %copy-done.6, ...), custom_call_target="tpu_custom_call" | custom-call | flops 17179869184 | bytes 884736 | tf_op jit(solution)/shard_map/attend_across_same_near/pallas_call | solution.py:440
Async XLA Ops:
  3.4 4.7 %collective-permute-start.4 = (bf16[512,1024]{1,0:T(8,128)(2,1)}, bf16[512,1024]{1,0:T(8,128)(2,1)S(1)}, u32[]{:S(2)}, u32[]{:S(2)}) collective-permute-start(bf16[512,1024]{1,0:T(8,128)(2,1)} %get-tuple-element.34), channel_id=1, source_target_pairs={{0,1},{1,0},{2,3},{3,2},{4,5},{5,4},{6,7},{7,6},{8,9},{9,8},{10,11... | collective-permute-start | bytes 3145736 | tf_op jit(solution)/shard_map/ppermute | solution.py:461
  3.9 20.5 %collective-permute-start = (bf16[256,1024]{1,0:T(8,128)(2,1)}, bf16[256,1024]{1,0:T(8,128)(2,1)S(1)}, u32[]{:S(2)}, u32[]{:S(2)}) collective-permute-start(bf16[256,1024]{1,0:T(8,128)(2,1)} %get-tuple-element.27.refs_2_.refs_15_), channel_id=1, source_target_pairs={{0,2},{1,3},{2,0},{3,1},{4,6},{5,7},{6,4},{7,5},{8,10},{9,11},{10,... | collective-permute-start | bytes 1572872 | tf_op jit(solution)/shard_map/ppermute | solution.py:461
  6.5 18.5 %collective-permute-start.5 = (bf16[128,1024]{1,0:T(8,128)(2,1)}, bf16[128,1024]{1,0:T(8,128)(2,1)S(1)}, u32[]{:S(2)}, u32[]{:S(2)}) collective-permute-start(bf16[128,1024]{1,0:T(8,128)(2,1)} %get-tuple-element.36), channel_id=1, source_target_pairs={{0,8},{8,0},{16,24},{24,16},{1,9},{9,1},{17,25},{25,17},{2,10},{10... | collective-permute-start | bytes 786440 | tf_op jit(solution)/shard_map/ppermute | solution.py:461
  8.1 16.3 %copy-start.4 = (bf16[512,1024]{1,0:T(8,128)(2,1)}, bf16[512,1024]{1,0:T(8,128)(2,1)S(1)}, u32[]{:S(2)}) copy-start(bf16[512,1024]{1,0:T(8,128)(2,1)S(1)} %collective-permute-done.4.refs_2_.refs_14_) | copy-start | bytes 3145732
  8.1 16.9 %collective-permute-start.6 = (bf16[128,1024]{1,0:T(8,128)(2,1)}, bf16[128,1024]{1,0:T(8,128)(2,1)S(1)}, u32[]{:S(2)}, u32[]{:S(2)}) collective-permute-start(bf16[128,1024]{1,0:T(8,128)(2,1)} %get-tuple-element.37), channel_id=1, source_target_pairs={{8,16},{16,8},{9,17},{17,9},{10,18},{18,10},{11,19},{19,11},{12,20... | collective-permute-start | bytes 786440 | tf_op jit(solution)/shard_map/ppermute | solution.py:461
  8.8 36.2 %collective-permute-start.2 = (bf16[256,1024]{1,0:T(8,128)(2,1)}, bf16[256,1024]{1,0:T(8,128)(2,1)S(1)}, u32[]{:S(2)}, u32[]{:S(2)}) collective-permute-start(bf16[256,1024]{1,0:T(8,128)(2,1)} %get-tuple-element.28.refs_3_.refs_16_), channel_id=1, source_target_pairs={{0,6},{1,7},{2,4},{3,5},{4,2},{5,3},{6,0},{7,1},{8,14},{9,15},{10,... | collective-permute-start | bytes 1572872 | tf_op jit(solution)/shard_map/ppermute | solution.py:461
  11.0 33.9 %collective-permute-start.3 = (bf16[256,1024]{1,0:T(8,128)(2,1)}, bf16[256,1024]{1,0:T(8,128)(2,1)S(1)}, u32[]{:S(2)}, u32[]{:S(2)}) collective-permute-start(bf16[256,1024]{1,0:T(8,128)(2,1)} %get-tuple-element.28.refs_3_.refs_16_), channel_id=1, source_target_pairs={{0,2},{1,3},{2,0},{3,1},{4,6},{5,7},{6,4},{7,5},{8,10},{9,11},{10,... | collective-permute-start | bytes 1572872 | tf_op jit(solution)/shard_map/ppermute | solution.py:461
  24.4 0.8 copy-start
  24.4 20.5 %collective-permute-start.1 = (bf16[256,1024]{1,0:T(8,128)(2,1)S(1)}, bf16[256,1024]{1,0:T(8,128)(2,1)S(1)}, u32[]{:S(2)}, u32[]{:S(2)}) collective-permute-start(bf16[256,1024]{1,0:T(8,128)(2,1)S(1)} %collective-permute-done.refs_3_.refs_17_), channel_id=1, source_target_pairs={{0,4},{1,5},{2,6},{3,7},{4,0},{5,1},{6,2},{7,3},{8,12},{9,13},{10,... | collective-permute-start | bytes 1572872 | tf_op jit(solution)/shard_map/ppermute | solution.py:461
  25.0 0.7 copy-start.7
  25.7 0.7 copy-start.8
  44.9 3.6 %copy-start.1 = (bf16[256,1024]{1,0:T(8,128)(2,1)}, bf16[256,1024]{1,0:T(8,128)(2,1)S(1)}, u32[]{:S(2)}) copy-start(bf16[256,1024]{1,0:T(8,128)(2,1)S(1)} %collective-permute-done.2.refs_3_.refs_20_) | copy-start | bytes 1572868
  44.9 3.6 %copy-start.2 = (bf16[256,1024]{1,0:T(8,128)(2,1)}, bf16[256,1024]{1,0:T(8,128)(2,1)S(1)}, u32[]{:S(2)}) copy-start(bf16[256,1024]{1,0:T(8,128)(2,1)S(1)} %collective-permute-done.3.refs_4_.refs_18_) | copy-start | bytes 1572868
  45.0 3.6 %copy-start.3 = (bf16[256,1024]{1,0:T(8,128)(2,1)}, bf16[256,1024]{1,0:T(8,128)(2,1)S(1)}, u32[]{:S(2)}) copy-start(bf16[256,1024]{1,0:T(8,128)(2,1)S(1)} %collective-permute-done.1.refs_2_.refs_19_) | copy-start | bytes 1572868
  45.0 2.0 collective-permute-start.8
  46.6 2.0 collective-permute-start.7
  47.0 1.6 copy-start.5
  48.6 0.8 copy-start.6

commit v12 on v11

--- a/solution.py
+++ b/solution.py
@@ -15,7 +15,7 @@
 NEG = -1e30
 FLOOR = -1e25
 LOG2E = math.log2(math.e)
-SUM_MIN, SUM_MAX = 2.0**-60, 2.0**100
+SUM_MIN, SUM_MAX = 2.0**-8, 2.0**24
 VMEM_LIMIT = 60 * 1024 * 1024
 CHUNKS = 4
 
@@ -209,9 +209,9 @@
     wq_ref = take(1)[0] if first else None
     wk_ref, wv_ref = take(2)
     if not first:
-        query_in, acc_in, sum_in = take(3)
+        query_in, acc_hbm, sum_hbm = take(3)
     if last:
-        tokens_ref, wo_ref = take(2)
+        tokens_hbm, wo_hbm = take(2)
         all_refs = take(1 + 4 * PARTS + 2)
         (out_ref,) = take(1)
     else:
@@ -220,8 +220,10 @@
         acc_out, sum_out = take(2)
     key_ref, value_ref, ones_ref = take(3)
     score_refs, weight_refs = take(2), take(2)
+    if not first:
+        acc_in, sum_in, state_sem = take(3)
     if last:
-        res_ref, att_ref, acc_out, sum_out, out_sem = take(5)
+        res_ref, att_ref, acc_out, sum_out, out_sem, wo_ref, final_sem = take(7)
 
     reach = mask_ref.shape[1] // 2
     lon, lat = lax.axis_index("lon"), lax.axis_index("lat")
@@ -230,6 +232,25 @@
     halo_seen = (even & south_there | ~even & north_there, even & north_there | ~even & south_there)
     columns = sector_columns(lon, reach)
     count = counts_ref[0]
+
+    step = pl.program_id(0)
+    state_copies, final_copies = [], []
+    if not first:
+        state_copies = [
+            pltpu.make_async_copy(acc_hbm, acc_in, state_sem.at[0]),
+            pltpu.make_async_copy(sum_hbm, sum_in, state_sem.at[1]),
+        ]
+    if last:
+        final_copies = [
+            pltpu.make_async_copy(tokens_hbm, res_ref, final_sem.at[0]),
+            pltpu.make_async_copy(wo_hbm, wo_ref, final_sem.at[1]),
+        ]
+    if state_copies:
+
+        @pl.when(step == 0)
+        def _():
+            for copy in state_copies + final_copies:
+                copy.start()
 
     wk, wv = wk_ref[...], wv_ref[...]
     if first:
@@ -276,6 +297,13 @@
     def lanes_of(pair):
         return slice(pair * LANES, (pair + 1) * LANES)
 
+    if state_copies:
+
+        @pl.when(step == 0)
+        def _():
+            for copy in state_copies:
+                copy.wait()
+
 
     whole_query = query
 
@@ -300,8 +328,9 @@
         acc = jnp.where(low, result[:rows, :LANES], result[rows:, :LANES])
         total = jnp.where(low, result[:rows, LANES:], result[rows:, LANES:])
         if not first:
-            acc = acc + acc_in[:, lanes]
-            total = total + sum_in[:, lanes]
+            place = pl.ds(pl.multiple_of(step * width + pair * LANES, LANES), LANES)
+            acc = acc + acc_in[:, place]
+            total = total + sum_in[:, place]
         acc_out[:, lanes] = acc
         sum_out[:, lanes] = total
 
@@ -335,19 +364,17 @@
             sources.append((ref, None, seen, 0))
         att_ref[...] = safe_group(query, (wk_ref, wv_ref), sources, counts_ref, mask_ref, refs, head_size)
 
-    step = pl.program_id(0)
-
     @pl.when(step == 0)
     def _():
-        res_ref[...] = jnp.zeros_like(res_ref)
-
-    at = pl.ds(pl.multiple_of(step * width, width), width)
-    res_ref[:, at] += tokens_ref[...]
+        for copy in final_copies:
+            copy.wait()
+
+    rows_of = pl.ds(pl.multiple_of(step * width, width), width)
     last_step = step == pl.num_programs(0) - 1
 
     @pl.when(~last_step)
     def _():
-        res_ref[...] += matmul(att_ref[...], wo_ref[...])
+        res_ref[...] += matmul(att_ref[...], wo_ref[rows_of])
 
     @pl.when(last_step)
     def _():
@@ -356,7 +383,7 @@
         copies = []
         for n in range(out_sem.shape[0]):
             block = pl.ds(n * size, size)
-            result = res_ref[:, block] + matmul(att_ref[...], wo_ref[:, block])
+            result = res_ref[:, block] + matmul(att_ref[...], wo_ref[rows_of, block])
             res_ref[:, block] = jnp.where(live, result, 0.0)
             copies.append(pltpu.make_async_copy(res_ref.at[:, block], out_ref.at[:, block], out_sem.at[n]))
             copies[-1].start()
@@ -391,7 +418,7 @@
         specs.append(weight(third))
     if not first:
         args += [query, *state]
-        specs += [columns] * 3
+        specs += [columns] + [pl.BlockSpec(memory_space=pl.ANY)] * 2
     keys = sum(p.shape[0] for parts in sector_parts for p in parts) + sum(h.shape[0] for h in halos)
     scratch = [
         pltpu.VMEM((GROUP, keys), jnp.bfloat16),
@@ -402,12 +429,14 @@
         pltpu.VMEM((2 * rows, keys), jnp.bfloat16),
         pltpu.VMEM((2 * rows, keys), jnp.bfloat16),
     ]
+    if not first:
+        scratch += [pltpu.VMEM((rows, width), jnp.float32)] * 2 + [pltpu.SemaphoreType.DMA((2,))]
     wide = jax.ShapeDtypeStruct((rows, width), jnp.float32)
     moved = sum(a.size * a.dtype.itemsize for a in args[2:] if a is not qkv_weight) + 3 * model * width * 2
     if last:
         tokens, out_weight, sources = final
         args += [tokens, out_weight, *sources]
-        specs += [columns, pl.BlockSpec((GROUP, out_weight.shape[1]), lambda g: (g, 0))]
+        specs += [pl.BlockSpec(memory_space=pl.ANY)] * 2
         specs += [pl.BlockSpec(memory_space=pl.ANY)] * len(sources)
         out_shape = [wide]
         out_specs = [pl.BlockSpec(memory_space=pl.ANY)]
@@ -419,6 +448,8 @@
             pltpu.VMEM((rows, GROUP), jnp.float32),
             pltpu.VMEM((rows, GROUP), jnp.float32),
             pltpu.SemaphoreType.DMA((4,)),
+            pltpu.VMEM(out_weight.shape, jnp.bfloat16),
+            pltpu.SemaphoreType.DMA((2,)),
             pltpu.VMEM((part, model), jnp.bfloat16),
             pltpu.VMEM((part * tiles, GROUP), jnp.bfloat16),
             pltpu.VMEM((part * tiles, GROUP), jnp.bfloat16),

time: 246 us -> 247 us (level)
  no operation moved by 1% of the time
where the time goes in v12:
time: 247 us; the launch traced here: 244 us
  Pallas kernels  228 us (92%)
  starting transfers between devices  9.09 us (4%)
    pallas_call x3, Pallas kernels, stage_call(): pl.pallas_call(functools.partial(stage_kernel, (first, last, sectors, sta...  225 us
    ppermute x9, starting transfers between devices, permuted(): return [lax.ppermute(v, axis, pairs) for v in values]  9.09 us
  transfers between devices with their start and end apart: 9, of which 2 were waited for; matrix products, arithmetic and copies ran while one was open for 1% of the time, Pallas kernels for 13%

profile of v12, /device:TPU:0, one launch (start us, length us, event | category | flops | bytes accessed | tf_op | source)
XLA Modules:
  0.0 244.0 jit_solution(17999973678695499782)
XLA Ops:
  0.0 3.4 %layer_norm.1 = (bf16[256,1024]{1,0:T(8,128)(2,1)}, bf16[256,1024]{1,0:T(8,128)(2,1)}, bf16[512,1024]{1,0:T(8,128)(2,1)}, bf16[128,1024]{1,0:T(8,128)(2,1)}, bf16[128,1024]{1,0:T(8,128)(2,1)}) custom-call(f32[512,1024]{1,0:T(8,128)} %bitcast.5, f32[1,1024]{1,0:T(1,128)} %bitcast.7, s32[8,128]{1,0:T(8,128)} %bitcast.8), custom_call_target="tpu_custom_call" | custom-call | flops 5242880 | bytes 3145728 | tf_op jit(solution)/shard_map/layer_norm/pallas_call | solution.py:97
  3.4 0.5 collective-permute-start.4
  3.9 2.6 %collective-permute-start = (bf16[256,1024]{1,0:T(8,128)(2,1)}, bf16[256,1024]{1,0:T(8,128)(2,1)S(1)}, u32[]{:S(2)}, u32[]{:S(2)}) collective-permute-start(bf16[256,1024]{1,0:T(8,128)(2,1)} %get-tuple-element.27.refs_2_.refs_15_), channel_id=1, source_target_pairs={{0,2},{1,3},{2,0},{3,1},{4,6},{5,7},{6,4},{7,5},{8,10},{9,11},{10,... | collective-permute-start | bytes 1572872 | tf_op jit(solution)/shard_map/ppermute | solution.py:492
  6.5 1.6 collective-permute-start.5
  8.1 0.0 collective-permute-done.4.refs_2_.refs_14_
  8.1 0.0 copy-start.4
  8.1 0.7 collective-permute-start.6
  8.8 2.2 collective-permute-start.2
  11.0 0.8 collective-permute-start.3
  12.5 11.9 %attend_own.1 = (bf16[512,1024]{1,0:T(8,128)(2,1)}, f32[512,1024]{1,0:T(8,128)}, f32[512,1024]{1,0:T(8,128)}) custom-call(s32[1]{0:T(128)S(6)} %copy.8.refs_0_, s32[4,5]{1,0:T(4,128)} %bitcast.9, bf16[256,1024]{1,0:T(8,128)(2,1)} %get-tuple-element.27.refs_2_.refs_15_, bf16[256,1024]{1,0:T(8,128)(2,1)} %get-tuple-element.28.refs_3_.refs_16_, ...), custom_call_target="tpu_custom_call" | custom-call | flops 469762048 | bytes 458752 | tf_op jit(solution)/shard_map/attend_own/pallas_call | solution.py:471
  24.4 0.0 copy-done.4
  24.4 0.0 collective-permute-done.refs_3_.refs_17_
  24.4 0.0 copy-start
  24.4 0.6 collective-permute-start.1
  25.0 0.0 collective-permute-done.5.refs_4_.refs_23_
  25.0 0.0 copy-start.7
  25.0 0.0 collective-permute-done.6.refs_5_.refs_24_
  25.0 0.2 copy-done
  25.2 0.5 copy-done.7
  25.7 0.0 copy-start.8
  25.7 0.7 copy-done.8
  26.4 20.2 %attend_partner_same.1 = (f32[512,1024]{1,0:T(8,128)}, f32[512,1024]{1,0:T(8,128)}) custom-call(s32[1]{0:T(128)S(6)} %copy.8.refs_0_, s32[4,5]{1,0:T(4,128)} %bitcast.10, bf16[512,1024]{1,0:T(8,128)(2,1)} %copy-done.4, bf16[256,1024]{1,0:T(8,128)(2,1)} %copy-done, bf16[128,1024]{1,0:T(8,128)(2,1)} %copy-done.7, bf16[128,1024]{1,0:T(8,128)(2,1)} %copy-done.8, ...), custom_call_target="tpu_custom_call" | custom-call | flops 12884901888 | bytes 851968 | tf_op jit(solution)/shard_map/attend_partner_same/pallas_call | solution.py:471
  46.6 0.0 collective-permute-done.2.refs_3_.refs_20_
  46.6 0.0 copy-start.1
  46.6 0.0 collective-permute-done.3.refs_4_.refs_18_
  46.7 0.0 copy-start.2
  46.7 0.0 collective-permute-done.1.refs_2_.refs_19_
  46.7 0.0 copy-start.3
  46.7 0.1 broadcast_select_fusion
  46.7 0.1 collective-permute-start.8
  46.8 1.5 broadcast_select_fusion.1
  48.3 0.1 collective-permute-start.7
  48.4 0.3 collective-permute-done.8.refs_6_.refs_22_
  48.7 0.0 copy-start.5
  48.7 1.6 collective-permute-done.7.refs_5_.refs_21_
  50.3 0.0 copy-done.1
  50.3 0.0 copy-done.2
  50.3 0.0 copy-done.3
  50.3 0.0 copy-done.5
  50.3 0.0 copy-start.6
  50.3 0.8 copy-done.6
  51.1 192.8 %attend_across_same_near.1 = f32[512,1024]{1,0:T(8,128)} custom-call(s32[1]{0:T(128)S(6)} %copy.8.refs_0_, s32[4,5]{1,0:T(4,128)} %bitcast.11, bf16[256,1024]{1,0:T(8,128)(2,1)} %copy-done.3, bf16[256,1024]{1,0:T(8,128)(2,1)} %copy-done.1, bf16[256,1024]{1,0:T(8,128)(2,1)} %copy-done.2, bf16[256,1024]{1,0:T(8,128)(2,1)} %copy-done.6, ...), custom_call_target="tpu_custom_call" | custom-call | flops 17179869184 | bytes 884736 | tf_op jit(solution)/shard_map/attend_across_same_near/pallas_call | solution.py:471
Async XLA Ops:
  3.4 4.7 %collective-permute-start.4 = (bf16[512,1024]{1,0:T(8,128)(2,1)}, bf16[512,1024]{1,0:T(8,128)(2,1)S(1)}, u32[]{:S(2)}, u32[]{:S(2)}) collective-permute-start(bf16[512,1024]{1,0:T(8,128)(2,1)} %get-tuple-element.34), channel_id=1, source_target_pairs={{0,1},{1,0},{2,3},{3,2},{4,5},{5,4},{6,7},{7,6},{8,9},{9,8},{10,11... | collective-permute-start | bytes 3145736 | tf_op jit(solution)/shard_map/ppermute | solution.py:492
  3.9 20.5 %collective-permute-start = (bf16[256,1024]{1,0:T(8,128)(2,1)}, bf16[256,1024]{1,0:T(8,128)(2,1)S(1)}, u32[]{:S(2)}, u32[]{:S(2)}) collective-permute-start(bf16[256,1024]{1,0:T(8,128)(2,1)} %get-tuple-element.27.refs_2_.refs_15_), channel_id=1, source_target_pairs={{0,2},{1,3},{2,0},{3,1},{4,6},{5,7},{6,4},{7,5},{8,10},{9,11},{10,... | collective-permute-start | bytes 1572872 | tf_op jit(solution)/shard_map/ppermute | solution.py:492
  6.5 18.5 %collective-permute-start.5 = (bf16[128,1024]{1,0:T(8,128)(2,1)}, bf16[128,1024]{1,0:T(8,128)(2,1)S(1)}, u32[]{:S(2)}, u32[]{:S(2)}) collective-permute-start(bf16[128,1024]{1,0:T(8,128)(2,1)} %get-tuple-element.36), channel_id=1, source_target_pairs={{0,8},{8,0},{16,24},{24,16},{1,9},{9,1},{17,25},{25,17},{2,10},{10... | collective-permute-start | bytes 786440 | tf_op jit(solution)/shard_map/ppermute | solution.py:492
  8.1 16.3 %copy-start.4 = (bf16[512,1024]{1,0:T(8,128)(2,1)}, bf16[512,1024]{1,0:T(8,128)(2,1)S(1)}, u32[]{:S(2)}) copy-start(bf16[512,1024]{1,0:T(8,128)(2,1)S(1)} %collective-permute-done.4.refs_2_.refs_14_) | copy-start | bytes 3145732
  8.1 16.9 %collective-permute-start.6 = (bf16[128,1024]{1,0:T(8,128)(2,1)}, bf16[128,1024]{1,0:T(8,128)(2,1)S(1)}, u32[]{:S(2)}, u32[]{:S(2)}) collective-permute-start(bf16[128,1024]{1,0:T(8,128)(2,1)} %get-tuple-element.37), channel_id=1, source_target_pairs={{8,16},{16,8},{9,17},{17,9},{10,18},{18,10},{11,19},{19,11},{12,20... | collective-permute-start | bytes 786440 | tf_op jit(solution)/shard_map/ppermute | solution.py:492
  8.8 37.9 %collective-permute-start.2 = (bf16[256,1024]{1,0:T(8,128)(2,1)}, bf16[256,1024]{1,0:T(8,128)(2,1)S(1)}, u32[]{:S(2)}, u32[]{:S(2)}) collective-permute-start(bf16[256,1024]{1,0:T(8,128)(2,1)} %get-tuple-element.28.refs_3_.refs_16_), channel_id=1, source_target_pairs={{0,6},{1,7},{2,4},{3,5},{4,2},{5,3},{6,0},{7,1},{8,14},{9,15},{10,... | collective-permute-start | bytes 1572872 | tf_op jit(solution)/shard_map/ppermute | solution.py:492
  11.0 35.7 %collective-permute-start.3 = (bf16[256,1024]{1,0:T(8,128)(2,1)}, bf16[256,1024]{1,0:T(8,128)(2,1)S(1)}, u32[]{:S(2)}, u32[]{:S(2)}) collective-permute-start(bf16[256,1024]{1,0:T(8,128)(2,1)} %get-tuple-element.28.refs_3_.refs_16_), channel_id=1, source_target_pairs={{0,2},{1,3},{2,0},{3,1},{4,6},{5,7},{6,4},{7,5},{8,10},{9,11},{10,... | collective-permute-start | bytes 1572872 | tf_op jit(solution)/shard_map/ppermute | solution.py:492
  24.4 0.8 copy-start
  24.4 22.2 %collective-permute-start.1 = (bf16[256,1024]{1,0:T(8,128)(2,1)S(1)}, bf16[256,1024]{1,0:T(8,128)(2,1)S(1)}, u32[]{:S(2)}, u32[]{:S(2)}) collective-permute-start(bf16[256,1024]{1,0:T(8,128)(2,1)S(1)} %collective-permute-done.refs_3_.refs_17_), channel_id=1, source_target_pairs={{0,4},{1,5},{2,6},{3,7},{4,0},{5,1},{6,2},{7,3},{8,12},{9,13},{10,... | collective-permute-start | bytes 1572872 | tf_op jit(solution)/shard_map/ppermute | solution.py:492
  25.0 0.7 copy-start.7
  25.7 0.7 copy-start.8
  46.6 3.6 %copy-start.1 = (bf16[256,1024]{1,0:T(8,128)(2,1)}, bf16[256,1024]{1,0:T(8,128)(2,1)S(1)}, u32[]{:S(2)}) copy-start(bf16[256,1024]{1,0:T(8,128)(2,1)S(1)} %collective-permute-done.2.refs_3_.refs_20_) | copy-start | bytes 1572868
  46.7 3.6 %copy-start.2 = (bf16[256,1024]{1,0:T(8,128)(2,1)}, bf16[256,1024]{1,0:T(8,128)(2,1)S(1)}, u32[]{:S(2)}) copy-start(bf16[256,1024]{1,0:T(8,128)(2,1)S(1)} %collective-permute-done.3.refs_4_.refs_18_) | copy-start | bytes 1572868
  46.7 3.6 %copy-start.3 = (bf16[256,1024]{1,0:T(8,128)(2,1)}, bf16[256,1024]{1,0:T(8,128)(2,1)S(1)}, u32[]{:S(2)}) copy-start(bf16[256,1024]{1,0:T(8,128)(2,1)S(1)} %collective-permute-done.1.refs_2_.refs_19_) | copy-start | bytes 1572868
  46.7 2.0 collective-permute-start.8
  48.3 2.0 collective-permute-start.7
  48.7 1.6 copy-start.5
  50.3 0.8 copy-start.6

commit v13 on v12

--- a/solution.py
+++ b/solution.py
@@ -209,7 +209,7 @@
     wq_ref = take(1)[0] if first else None
     wk_ref, wv_ref = take(2)
     if not first:
-        query_in, acc_hbm, sum_hbm = take(3)
+        query_in, acc_in, sum_in = take(3)
     if last:
         tokens_hbm, wo_hbm = take(2)
         all_refs = take(1 + 4 * PARTS + 2)
@@ -220,8 +220,6 @@
         acc_out, sum_out = take(2)
     key_ref, value_ref, ones_ref = take(3)
     score_refs, weight_refs = take(2), take(2)
-    if not first:
-        acc_in, sum_in, state_sem = take(3)
     if last:
         res_ref, att_ref, acc_out, sum_out, out_sem, wo_ref, final_sem = take(7)
 
@@ -234,22 +232,15 @@
     count = counts_ref[0]
 
     step = pl.program_id(0)
-    state_copies, final_copies = [], []
-    if not first:
-        state_copies = [
-            pltpu.make_async_copy(acc_hbm, acc_in, state_sem.at[0]),
-            pltpu.make_async_copy(sum_hbm, sum_in, state_sem.at[1]),
-        ]
     if last:
         final_copies = [
             pltpu.make_async_copy(tokens_hbm, res_ref, final_sem.at[0]),
             pltpu.make_async_copy(wo_hbm, wo_ref, final_sem.at[1]),
         ]
-    if state_copies:
 
         @pl.when(step == 0)
         def _():
-            for copy in state_copies + final_copies:
+            for copy in final_copies:
                 copy.start()
 
     wk, wv = wk_ref[...], wv_ref[...]
@@ -297,13 +288,6 @@
     def lanes_of(pair):
         return slice(pair * LANES, (pair + 1) * LANES)
 
-    if state_copies:
-
-        @pl.when(step == 0)
-        def _():
-            for copy in state_copies:
-                copy.wait()
-
 
     whole_query = query
 
@@ -328,9 +312,8 @@
         acc = jnp.where(low, result[:rows, :LANES], result[rows:, :LANES])
         total = jnp.where(low, result[:rows, LANES:], result[rows:, LANES:])
         if not first:
-            place = pl.ds(pl.multiple_of(step * width + pair * LANES, LANES), LANES)
-            acc = acc + acc_in[:, place]
-            total = total + sum_in[:, place]
+            acc = acc + acc_in[:, lanes]
+            total = total + sum_in[:, lanes]
         acc_out[:, lanes] = acc
         sum_out[:, lanes] = total
 
@@ -418,7 +401,7 @@
         specs.append(weight(third))
     if not first:
         args += [query, *state]
-        specs += [columns] + [pl.BlockSpec(memory_space=pl.ANY)] * 2
+        specs += [columns] * 3
     keys = sum(p.shape[0] for parts in sector_parts for p in parts) + sum(h.shape[0] for h in halos)
     scratch = [
         pltpu.VMEM((GROUP, keys), jnp.bfloat16),
@@ -429,8 +412,6 @@
         pltpu.VMEM((2 * rows, keys), jnp.bfloat16),
         pltpu.VMEM((2 * rows, keys), jnp.bfloat16),
     ]
-    if not first:
-        scratch += [pltpu.VMEM((rows, width), jnp.float32)] * 2 + [pltpu.SemaphoreType.DMA((2,))]
     wide = jax.ShapeDtypeStruct((rows, width), jnp.float32)
     moved = sum(a.size * a.dtype.itemsize for a in args[2:] if a is not qkv_weight) + 3 * model * width * 2
     if last:

time: 247 us -> 246 us (level)
  no operation moved by 1% of the time
where the time goes in v13:
time: 246 us; the launch traced here: 243 us
  Pallas kernels  227 us (92%)
  starting transfers between devices  9.09 us (4%)
    pallas_call x3, Pallas kernels, stage_call(): pl.pallas_call(functools.partial(stage_kernel, (first, last, sectors, sta...  224 us
    ppermute x9, starting transfers between devices, permuted(): return [lax.ppermute(v, axis, pairs) for v in values]  9.09 us
  transfers between devices with their start and end apart: 9, of which 2 were waited for; matrix products, arithmetic and copies ran while one was open for 1% of the time, Pallas kernels for 13%

profile of v13, /device:TPU:0, one launch (start us, length us, event | category | flops | bytes accessed | tf_op | source)
XLA Modules:
  0.0 242.9 jit_solution(3973204684193724015)
XLA Ops:
  0.0 3.4 %layer_norm.1 = (bf16[256,1024]{1,0:T(8,128)(2,1)}, bf16[256,1024]{1,0:T(8,128)(2,1)}, bf16[512,1024]{1,0:T(8,128)(2,1)}, bf16[128,1024]{1,0:T(8,128)(2,1)}, bf16[128,1024]{1,0:T(8,128)(2,1)}) custom-call(f32[512,1024]{1,0:T(8,128)} %bitcast.5, f32[1,1024]{1,0:T(1,128)} %bitcast.7, s32[8,128]{1,0:T(8,128)} %bitcast.8), custom_call_target="tpu_custom_call" | custom-call | flops 5242880 | bytes 3145728 | tf_op jit(solution)/shard_map/layer_norm/pallas_call | solution.py:97
  3.4 0.5 collective-permute-start.4
  3.9 2.6 %collective-permute-start = (bf16[256,1024]{1,0:T(8,128)(2,1)}, bf16[256,1024]{1,0:T(8,128)(2,1)S(1)}, u32[]{:S(2)}, u32[]{:S(2)}) collective-permute-start(bf16[256,1024]{1,0:T(8,128)(2,1)} %get-tuple-element.27.refs_2_.refs_15_), channel_id=1, source_target_pairs={{0,2},{1,3},{2,0},{3,1},{4,6},{5,7},{6,4},{7,5},{8,10},{9,11},{10,... | collective-permute-start | bytes 1572872 | tf_op jit(solution)/shard_map/ppermute | solution.py:473
  6.5 1.6 collective-permute-start.5
  8.1 0.0 collective-permute-done.4.refs_2_.refs_14_
  8.1 0.0 copy-start.4
  8.1 0.7 collective-permute-start.6
  8.8 2.2 collective-permute-start.2
  11.0 0.8 collective-permute-start.3
  12.5 11.9 %attend_own.1 = (bf16[512,1024]{1,0:T(8,128)(2,1)}, f32[512,1024]{1,0:T(8,128)}, f32[512,1024]{1,0:T(8,128)}) custom-call(s32[1]{0:T(128)S(6)} %copy.8.refs_0_, s32[4,5]{1,0:T(4,128)} %bitcast.9, bf16[256,1024]{1,0:T(8,128)(2,1)} %get-tuple-element.27.refs_2_.refs_15_, bf16[256,1024]{1,0:T(8,128)(2,1)} %get-tuple-element.28.refs_3_.refs_16_, ...), custom_call_target="tpu_custom_call" | custom-call | flops 469762048 | bytes 458752 | tf_op jit(solution)/shard_map/attend_own/pallas_call | solution.py:452
  24.4 0.0 copy-done.4
  24.4 0.0 collective-permute-done.refs_3_.refs_17_
  24.4 0.0 copy-start
  24.4 0.6 collective-permute-start.1
  25.0 0.0 collective-permute-done.5.refs_4_.refs_23_
  25.0 0.0 copy-start.7
  25.0 0.0 collective-permute-done.6.refs_5_.refs_24_
  25.0 0.2 copy-done
  25.2 0.5 copy-done.7
  25.7 0.0 copy-start.8
  25.7 0.7 copy-done.8
  26.4 18.5 %attend_partner_same.1 = (f32[512,1024]{1,0:T(8,128)}, f32[512,1024]{1,0:T(8,128)}) custom-call(s32[1]{0:T(128)S(6)} %copy.8.refs_0_, s32[4,5]{1,0:T(4,128)} %bitcast.10, bf16[512,1024]{1,0:T(8,128)(2,1)} %copy-done.4, bf16[256,1024]{1,0:T(8,128)(2,1)} %copy-done, bf16[128,1024]{1,0:T(8,128)(2,1)} %copy-done.7, bf16[128,1024]{1,0:T(8,128)(2,1)} %copy-done.8, ...), custom_call_target="tpu_custom_call" | custom-call | flops 12884901888 | bytes 851968 | tf_op jit(solution)/shard_map/attend_partner_same/pallas_call | solution.py:452
  44.9 0.0 collective-permute-done.2.refs_3_.refs_20_
  44.9 0.0 copy-start.1
  44.9 0.0 collective-permute-done.3.refs_4_.refs_18_
  44.9 0.0 copy-start.2
  45.0 0.0 collective-permute-done.1.refs_2_.refs_19_
  45.0 0.0 copy-start.3
  45.0 0.1 broadcast_select_fusion
  45.0 0.1 collective-permute-start.8
  45.1 1.5 broadcast_select_fusion.1
  46.6 0.1 collective-permute-start.7
  46.7 0.3 collective-permute-done.8.refs_6_.refs_22_
  47.0 0.0 copy-start.5
  47.0 1.6 collective-permute-done.7.refs_5_.refs_21_
  48.6 0.0 copy-done.1
  48.6 0.0 copy-done.2
  48.6 0.0 copy-done.3
  48.6 0.0 copy-done.5
  48.6 0.0 copy-start.6
  48.6 0.8 copy-done.6
  49.4 193.3 %attend_across_same_near.1 = f32[512,1024]{1,0:T(8,128)} custom-call(s32[1]{0:T(128)S(6)} %copy.8.refs_0_, s32[4,5]{1,0:T(4,128)} %bitcast.11, bf16[256,1024]{1,0:T(8,128)(2,1)} %copy-done.3, bf16[256,1024]{1,0:T(8,128)(2,1)} %copy-done.1, bf16[256,1024]{1,0:T(8,128)(2,1)} %copy-done.2, bf16[256,1024]{1,0:T(8,128)(2,1)} %copy-done.6, ...), custom_call_target="tpu_custom_call" | custom-call | flops 17179869184 | bytes 884736 | tf_op jit(solution)/shard_map/attend_across_same_near/pallas_call | solution.py:452
Async XLA Ops:
  3.4 4.7 %collective-permute-start.4 = (bf16[512,1024]{1,0:T(8,128)(2,1)}, bf16[512,1024]{1,0:T(8,128)(2,1)S(1)}, u32[]{:S(2)}, u32[]{:S(2)}) collective-permute-start(bf16[512,1024]{1,0:T(8,128)(2,1)} %get-tuple-element.34), channel_id=1, source_target_pairs={{0,1},{1,0},{2,3},{3,2},{4,5},{5,4},{6,7},{7,6},{8,9},{9,8},{10,11... | collective-permute-start | bytes 3145736 | tf_op jit(solution)/shard_map/ppermute | solution.py:473
  3.9 20.5 %collective-permute-start = (bf16[256,1024]{1,0:T(8,128)(2,1)}, bf16[256,1024]{1,0:T(8,128)(2,1)S(1)}, u32[]{:S(2)}, u32[]{:S(2)}) collective-permute-start(bf16[256,1024]{1,0:T(8,128)(2,1)} %get-tuple-element.27.refs_2_.refs_15_), channel_id=1, source_target_pairs={{0,2},{1,3},{2,0},{3,1},{4,6},{5,7},{6,4},{7,5},{8,10},{9,11},{10,... | collective-permute-start | bytes 1572872 | tf_op jit(solution)/shard_map/ppermute | solution.py:473
  6.5 18.5 %collective-permute-start.5 = (bf16[128,1024]{1,0:T(8,128)(2,1)}, bf16[128,1024]{1,0:T(8,128)(2,1)S(1)}, u32[]{:S(2)}, u32[]{:S(2)}) collective-permute-start(bf16[128,1024]{1,0:T(8,128)(2,1)} %get-tuple-element.36), channel_id=1, source_target_pairs={{0,8},{8,0},{16,24},{24,16},{1,9},{9,1},{17,25},{25,17},{2,10},{10... | collective-permute-start | bytes 786440 | tf_op jit(solution)/shard_map/ppermute | solution.py:473
  8.1 16.3 %copy-start.4 = (bf16[512,1024]{1,0:T(8,128)(2,1)}, bf16[512,1024]{1,0:T(8,128)(2,1)S(1)}, u32[]{:S(2)}) copy-start(bf16[512,1024]{1,0:T(8,128)(2,1)S(1)} %collective-permute-done.4.refs_2_.refs_14_) | copy-start | bytes 3145732
  8.1 16.9 %collective-permute-start.6 = (bf16[128,1024]{1,0:T(8,128)(2,1)}, bf16[128,1024]{1,0:T(8,128)(2,1)S(1)}, u32[]{:S(2)}, u32[]{:S(2)}) collective-permute-start(bf16[128,1024]{1,0:T(8,128)(2,1)} %get-tuple-element.37), channel_id=1, source_target_pairs={{8,16},{16,8},{9,17},{17,9},{10,18},{18,10},{11,19},{19,11},{12,20... | collective-permute-start | bytes 786440 | tf_op jit(solution)/shard_map/ppermute | solution.py:473
  8.8 36.2 %collective-permute-start.2 = (bf16[256,1024]{1,0:T(8,128)(2,1)}, bf16[256,1024]{1,0:T(8,128)(2,1)S(1)}, u32[]{:S(2)}, u32[]{:S(2)}) collective-permute-start(bf16[256,1024]{1,0:T(8,128)(2,1)} %get-tuple-element.28.refs_3_.refs_16_), channel_id=1, source_target_pairs={{0,6},{1,7},{2,4},{3,5},{4,2},{5,3},{6,0},{7,1},{8,14},{9,15},{10,... | collective-permute-start | bytes 1572872 | tf_op jit(solution)/shard_map/ppermute | solution.py:473
  11.0 33.9 %collective-permute-start.3 = (bf16[256,1024]{1,0:T(8,128)(2,1)}, bf16[256,1024]{1,0:T(8,128)(2,1)S(1)}, u32[]{:S(2)}, u32[]{:S(2)}) collective-permute-start(bf16[256,1024]{1,0:T(8,128)(2,1)} %get-tuple-element.28.refs_3_.refs_16_), channel_id=1, source_target_pairs={{0,2},{1,3},{2,0},{3,1},{4,6},{5,7},{6,4},{7,5},{8,10},{9,11},{10,... | collective-permute-start | bytes 1572872 | tf_op jit(solution)/shard_map/ppermute | solution.py:473
  24.4 0.8 copy-start
  24.4 20.5 %collective-permute-start.1 = (bf16[256,1024]{1,0:T(8,128)(2,1)S(1)}, bf16[256,1024]{1,0:T(8,128)(2,1)S(1)}, u32[]{:S(2)}, u32[]{:S(2)}) collective-permute-start(bf16[256,1024]{1,0:T(8,128)(2,1)S(1)} %collective-permute-done.refs_3_.refs_17_), channel_id=1, source_target_pairs={{0,4},{1,5},{2,6},{3,7},{4,0},{5,1},{6,2},{7,3},{8,12},{9,13},{10,... | collective-permute-start | bytes 1572872 | tf_op jit(solution)/shard_map/ppermute | solution.py:473
  25.0 0.7 copy-start.7
  25.7 0.7 copy-start.8
  44.9 3.6 %copy-start.1 = (bf16[256,1024]{1,0:T(8,128)(2,1)}, bf16[256,1024]{1,0:T(8,128)(2,1)S(1)}, u32[]{:S(2)}) copy-start(bf16[256,1024]{1,0:T(8,128)(2,1)S(1)} %collective-permute-done.2.refs_3_.refs_20_) | copy-start | bytes 1572868
  44.9 3.6 %copy-start.2 = (bf16[256,1024]{1,0:T(8,128)(2,1)}, bf16[256,1024]{1,0:T(8,128)(2,1)S(1)}, u32[]{:S(2)}) copy-start(bf16[256,1024]{1,0:T(8,128)(2,1)S(1)} %collective-permute-done.3.refs_4_.refs_18_) | copy-start | bytes 1572868
  45.0 3.6 %copy-start.3 = (bf16[256,1024]{1,0:T(8,128)(2,1)}, bf16[256,1024]{1,0:T(8,128)(2,1)S(1)}, u32[]{:S(2)}) copy-start(bf16[256,1024]{1,0:T(8,128)(2,1)S(1)} %collective-permute-done.1.refs_2_.refs_19_) | copy-start | bytes 1572868
  45.0 2.0 collective-permute-start.8
  46.6 2.0 collective-permute-start.7
  47.0 1.6 copy-start.5
  48.6 0.8 copy-start.6

commit v14 on v12

--- a/solution.py
+++ b/solution.py
@@ -209,7 +209,7 @@
     wq_ref = take(1)[0] if first else None
     wk_ref, wv_ref = take(2)
     if not first:
-        query_in, acc_hbm, sum_hbm = take(3)
+        query_in, acc_in, sum_in = take(3)
     if last:
         tokens_hbm, wo_hbm = take(2)
         all_refs = take(1 + 4 * PARTS + 2)
@@ -220,9 +220,9 @@
         acc_out, sum_out = take(2)
     key_ref, value_ref, ones_ref = take(3)
     score_refs, weight_refs = take(2), take(2)
-    if not first:
+    if last:
+        acc_hbm, sum_hbm = acc_in, sum_in
         acc_in, sum_in, state_sem = take(3)
-    if last:
         res_ref, att_ref, acc_out, sum_out, out_sem, wo_ref, final_sem = take(7)
 
     reach = mask_ref.shape[1] // 2
@@ -235,7 +235,7 @@
 
     step = pl.program_id(0)
     state_copies, final_copies = [], []
-    if not first:
+    if last:
         state_copies = [
             pltpu.make_async_copy(acc_hbm, acc_in, state_sem.at[0]),
             pltpu.make_async_copy(sum_hbm, sum_in, state_sem.at[1]),
@@ -328,7 +328,7 @@
         acc = jnp.where(low, result[:rows, :LANES], result[rows:, :LANES])
         total = jnp.where(low, result[:rows, LANES:], result[rows:, LANES:])
         if not first:
-            place = pl.ds(pl.multiple_of(step * width + pair * LANES, LANES), LANES)
+            place = pl.ds(pl.multiple_of(step * width + pair * LANES, LANES), LANES) if last else lanes
             acc = acc + acc_in[:, place]
             total = total + sum_in[:, place]
         acc_out[:, lanes] = acc
@@ -418,7 +418,7 @@
         specs.append(weight(third))
     if not first:
         args += [query, *state]
-        specs += [columns] + [pl.BlockSpec(memory_space=pl.ANY)] * 2
+        specs += [columns] + [pl.BlockSpec(memory_space=pl.ANY) if last else columns] * 2
     keys = sum(p.shape[0] for parts in sector_parts for p in parts) + sum(h.shape[0] for h in halos)
     scratch = [
         pltpu.VMEM((GROUP, keys), jnp.bfloat16),
@@ -429,7 +429,7 @@
         pltpu.VMEM((2 * rows, keys), jnp.bfloat16),
         pltpu.VMEM((2 * rows, keys), jnp.bfloat16),
     ]
-    if not first:
+    if last:
         scratch += [pltpu.VMEM((rows, width), jnp.float32)] * 2 + [pltpu.SemaphoreType.DMA((2,))]
     wide = jax.ShapeDtypeStruct((rows, width), jnp.float32)
     moved = sum(a.size * a.dtype.itemsize for a in args[2:] if a is not qkv_weight) + 3 * model * width * 2

time: 247 us -> 245 us (level)
  no operation moved by 1% of the time
where the time goes in v14:
time: 245 us; the launch traced here: 242 us
  Pallas kernels  227 us (93%)
  starting transfers between devices  9.09 us (4%)
    pallas_call x3, Pallas kernels, stage_call(): pl.pallas_call(functools.partial(stage_kernel, (first, last, sectors, sta...  223 us
    ppermute x9, starting transfers between devices, permuted(): return [lax.ppermute(v, axis, pairs) for v in values]  9.09 us
  transfers between devices with their start and end apart: 9, of which 2 were waited for; matrix products, arithmetic and copies ran while one was open for 1% of the time, Pallas kernels for 13%

profile of v14, /device:TPU:0, one launch (start us, length us, event | category | flops | bytes accessed | tf_op | source)
XLA Modules:
  0.0 242.3 jit_solution(9955514465946400387)
XLA Ops:
  0.0 3.4 %layer_norm.1 = (bf16[256,1024]{1,0:T(8,128)(2,1)}, bf16[256,1024]{1,0:T(8,128)(2,1)}, bf16[512,1024]{1,0:T(8,128)(2,1)}, bf16[128,1024]{1,0:T(8,128)(2,1)}, bf16[128,1024]{1,0:T(8,128)(2,1)}) custom-call(f32[512,1024]{1,0:T(8,128)} %bitcast.5, f32[1,1024]{1,0:T(1,128)} %bitcast.7, s32[8,128]{1,0:T(8,128)} %bitcast.8), custom_call_target="tpu_custom_call" | custom-call | flops 5242880 | bytes 3145728 | tf_op jit(solution)/shard_map/layer_norm/pallas_call | solution.py:97
  3.4 0.5 collective-permute-start.4
  3.9 2.6 %collective-permute-start = (bf16[256,1024]{1,0:T(8,128)(2,1)}, bf16[256,1024]{1,0:T(8,128)(2,1)S(1)}, u32[]{:S(2)}, u32[]{:S(2)}) collective-permute-start(bf16[256,1024]{1,0:T(8,128)(2,1)} %get-tuple-element.27.refs_2_.refs_15_), channel_id=1, source_target_pairs={{0,2},{1,3},{2,0},{3,1},{4,6},{5,7},{6,4},{7,5},{8,10},{9,11},{10,... | collective-permute-start | bytes 1572872 | tf_op jit(solution)/shard_map/ppermute | solution.py:492
  6.5 1.6 collective-permute-start.5
  8.1 0.0 collective-permute-done.4.refs_2_.refs_14_
  8.1 0.0 copy-start.4
  8.1 0.7 collective-permute-start.6
  8.8 2.2 collective-permute-start.2
  11.0 0.8 collective-permute-start.3
  12.5 11.9 %attend_own.1 = (bf16[512,1024]{1,0:T(8,128)(2,1)}, f32[512,1024]{1,0:T(8,128)}, f32[512,1024]{1,0:T(8,128)}) custom-call(s32[1]{0:T(128)S(6)} %copy.8.refs_0_, s32[4,5]{1,0:T(4,128)} %bitcast.9, bf16[256,1024]{1,0:T(8,128)(2,1)} %get-tuple-element.27.refs_2_.refs_15_, bf16[256,1024]{1,0:T(8,128)(2,1)} %get-tuple-element.28.refs_3_.refs_16_, ...), custom_call_target="tpu_custom_call" | custom-call | flops 469762048 | bytes 458752 | tf_op jit(solution)/shard_map/attend_own/pallas_call | solution.py:471
  24.4 0.0 copy-done.4
  24.4 0.0 collective-permute-done.refs_3_.refs_17_
  24.4 0.0 copy-start
  24.4 0.6 collective-permute-start.1
  25.0 0.0 collective-permute-done.5.refs_4_.refs_23_
  25.0 0.0 copy-start.7
  25.0 0.0 collective-permute-done.6.refs_5_.refs_24_
  25.0 0.2 copy-done
  25.2 0.5 copy-done.7
  25.7 0.0 copy-start.8
  25.7 0.7 copy-done.8
  26.4 18.5 %attend_partner_same.1 = (f32[512,1024]{1,0:T(8,128)}, f32[512,1024]{1,0:T(8,128)}) custom-call(s32[1]{0:T(128)S(6)} %copy.8.refs_0_, s32[4,5]{1,0:T(4,128)} %bitcast.10, bf16[512,1024]{1,0:T(8,128)(2,1)} %copy-done.4, bf16[256,1024]{1,0:T(8,128)(2,1)} %copy-done, bf16[128,1024]{1,0:T(8,128)(2,1)} %copy-done.7, bf16[128,1024]{1,0:T(8,128)(2,1)} %copy-done.8, ...), custom_call_target="tpu_custom_call" | custom-call | flops 12884901888 | bytes 851968 | tf_op jit(solution)/shard_map/attend_partner_same/pallas_call | solution.py:471
  44.9 0.0 collective-permute-done.2.refs_3_.refs_20_
  44.9 0.0 copy-start.1
  44.9 0.0 collective-permute-done.3.refs_4_.refs_18_
  44.9 0.0 copy-start.2
  45.0 0.0 collective-permute-done.1.refs_2_.refs_19_
  45.0 0.0 copy-start.3
  45.0 0.1 broadcast_select_fusion
  45.0 0.1 collective-permute-start.8
  45.1 1.5 broadcast_select_fusion.1
  46.6 0.1 collective-permute-start.7
  46.7 0.3 collective-permute-done.8.refs_6_.refs_22_
  47.0 0.0 copy-start.5
  47.0 1.6 collective-permute-done.7.refs_5_.refs_21_
  48.6 0.0 copy-done.1
  48.6 0.0 copy-done.2
  48.6 0.0 copy-done.3
  48.6 0.0 copy-done.5
  48.6 0.0 copy-start.6
  48.6 0.8 copy-done.6
  49.4 192.8 %attend_across_same_near.1 = f32[512,1024]{1,0:T(8,128)} custom-call(s32[1]{0:T(128)S(6)} %copy.8.refs_0_, s32[4,5]{1,0:T(4,128)} %bitcast.11, bf16[256,1024]{1,0:T(8,128)(2,1)} %copy-done.3, bf16[256,1024]{1,0:T(8,128)(2,1)} %copy-done.1, bf16[256,1024]{1,0:T(8,128)(2,1)} %copy-done.2, bf16[256,1024]{1,0:T(8,128)(2,1)} %copy-done.6, ...), custom_call_target="tpu_custom_call" | custom-call | flops 17179869184 | bytes 884736 | tf_op jit(solution)/shard_map/attend_across_same_near/pallas_call | solution.py:471
Async XLA Ops:
  3.4 4.7 %collective-permute-start.4 = (bf16[512,1024]{1,0:T(8,128)(2,1)}, bf16[512,1024]{1,0:T(8,128)(2,1)S(1)}, u32[]{:S(2)}, u32[]{:S(2)}) collective-permute-start(bf16[512,1024]{1,0:T(8,128)(2,1)} %get-tuple-element.34), channel_id=1, source_target_pairs={{0,1},{1,0},{2,3},{3,2},{4,5},{5,4},{6,7},{7,6},{8,9},{9,8},{10,11... | collective-permute-start | bytes 3145736 | tf_op jit(solution)/shard_map/ppermute | solution.py:492
  3.9 20.5 %collective-permute-start = (bf16[256,1024]{1,0:T(8,128)(2,1)}, bf16[256,1024]{1,0:T(8,128)(2,1)S(1)}, u32[]{:S(2)}, u32[]{:S(2)}) collective-permute-start(bf16[256,1024]{1,0:T(8,128)(2,1)} %get-tuple-element.27.refs_2_.refs_15_), channel_id=1, source_target_pairs={{0,2},{1,3},{2,0},{3,1},{4,6},{5,7},{6,4},{7,5},{8,10},{9,11},{10,... | collective-permute-start | bytes 1572872 | tf_op jit(solution)/shard_map/ppermute | solution.py:492
  6.5 18.5 %collective-permute-start.5 = (bf16[128,1024]{1,0:T(8,128)(2,1)}, bf16[128,1024]{1,0:T(8,128)(2,1)S(1)}, u32[]{:S(2)}, u32[]{:S(2)}) collective-permute-start(bf16[128,1024]{1,0:T(8,128)(2,1)} %get-tuple-element.36), channel_id=1, source_target_pairs={{0,8},{8,0},{16,24},{24,16},{1,9},{9,1},{17,25},{25,17},{2,10},{10... | collective-permute-start | bytes 786440 | tf_op jit(solution)/shard_map/ppermute | solution.py:492
  8.1 16.3 %copy-start.4 = (bf16[512,1024]{1,0:T(8,128)(2,1)}, bf16[512,1024]{1,0:T(8,128)(2,1)S(1)}, u32[]{:S(2)}) copy-start(bf16[512,1024]{1,0:T(8,128)(2,1)S(1)} %collective-permute-done.4.refs_2_.refs_14_) | copy-start | bytes 3145732
  8.1 16.9 %collective-permute-start.6 = (bf16[128,1024]{1,0:T(8,128)(2,1)}, bf16[128,1024]{1,0:T(8,128)(2,1)S(1)}, u32[]{:S(2)}, u32[]{:S(2)}) collective-permute-start(bf16[128,1024]{1,0:T(8,128)(2,1)} %get-tuple-element.37), channel_id=1, source_target_pairs={{8,16},{16,8},{9,17},{17,9},{10,18},{18,10},{11,19},{19,11},{12,20... | collective-permute-start | bytes 786440 | tf_op jit(solution)/shard_map/ppermute | solution.py:492
  8.8 36.2 %collective-permute-start.2 = (bf16[256,1024]{1,0:T(8,128)(2,1)}, bf16[256,1024]{1,0:T(8,128)(2,1)S(1)}, u32[]{:S(2)}, u32[]{:S(2)}) collective-permute-start(bf16[256,1024]{1,0:T(8,128)(2,1)} %get-tuple-element.28.refs_3_.refs_16_), channel_id=1, source_target_pairs={{0,6},{1,7},{2,4},{3,5},{4,2},{5,3},{6,0},{7,1},{8,14},{9,15},{10,... | collective-permute-start | bytes 1572872 | tf_op jit(solution)/shard_map/ppermute | solution.py:492
  11.0 33.9 %collective-permute-start.3 = (bf16[256,1024]{1,0:T(8,128)(2,1)}, bf16[256,1024]{1,0:T(8,128)(2,1)S(1)}, u32[]{:S(2)}, u32[]{:S(2)}) collective-permute-start(bf16[256,1024]{1,0:T(8,128)(2,1)} %get-tuple-element.28.refs_3_.refs_16_), channel_id=1, source_target_pairs={{0,2},{1,3},{2,0},{3,1},{4,6},{5,7},{6,4},{7,5},{8,10},{9,11},{10,... | collective-permute-start | bytes 1572872 | tf_op jit(solution)/shard_map/ppermute | solution.py:492
  24.4 0.8 copy-start
  24.4 20.5 %collective-permute-start.1 = (bf16[256,1024]{1,0:T(8,128)(2,1)S(1)}, bf16[256,1024]{1,0:T(8,128)(2,1)S(1)}, u32[]{:S(2)}, u32[]{:S(2)}) collective-permute-start(bf16[256,1024]{1,0:T(8,128)(2,1)S(1)} %collective-permute-done.refs_3_.refs_17_), channel_id=1, source_target_pairs={{0,4},{1,5},{2,6},{3,7},{4,0},{5,1},{6,2},{7,3},{8,12},{9,13},{10,... | collective-permute-start | bytes 1572872 | tf_op jit(solution)/shard_map/ppermute | solution.py:492
  25.0 0.7 copy-start.7
  25.7 0.7 copy-start.8
  44.9 3.6 %copy-start.1 = (bf16[256,1024]{1,0:T(8,128)(2,1)}, bf16[256,1024]{1,0:T(8,128)(2,1)S(1)}, u32[]{:S(2)}) copy-start(bf16[256,1024]{1,0:T(8,128)(2,1)S(1)} %collective-permute-done.2.refs_3_.refs_20_) | copy-start | bytes 1572868
  44.9 3.6 %copy-start.2 = (bf16[256,1024]{1,0:T(8,128)(2,1)}, bf16[256,1024]{1,0:T(8,128)(2,1)S(1)}, u32[]{:S(2)}) copy-start(bf16[256,1024]{1,0:T(8,128)(2,1)S(1)} %collective-permute-done.3.refs_4_.refs_18_) | copy-start | bytes 1572868
  45.0 3.6 %copy-start.3 = (bf16[256,1024]{1,0:T(8,128)(2,1)}, bf16[256,1024]{1,0:T(8,128)(2,1)S(1)}, u32[]{:S(2)}) copy-start(bf16[256,1024]{1,0:T(8,128)(2,1)S(1)} %collective-permute-done.1.refs_2_.refs_19_) | copy-start | bytes 1572868
  45.0 2.0 collective-permute-start.8
  46.6 2.0 collective-permute-start.7
  47.0 1.6 copy-start.5
  48.6 0.8 copy-start.6
